TPU v7x, 256 devices: a whole 4x4x8 slice. The times are simulated.
256 devices in a mesh: tiles: 32 (over z, x_hi, core), lat: 8 (over x_lo, y).
Axes of the slice: x: 4 (x_hi: 2, x_lo: 2; x = x_hi * 2 + x_lo), y: 4, z: 8, core: 2. Of those that a mesh axis runs over, the one named last changes fastest.
Arguments:
- ocean_state: bfloat16 [8, 64, 16, 3200], P('lat', 'tiles'), may hold values from -6 to 6
- land_mask: int32 [8, 64, 256], P('lat', 'tiles'), may hold values 0 or 1
- wet_count: int32 [8, 32], P('lat', 'tiles'), may hold values from 0 to 2, as said below
- neighbours: int32 [8, 64, 4], P('lat', 'tiles'), may hold values from -1 to 8, as said below
- kern_one: bfloat16 [7, 7, 200], replicated, may hold values from -0.875 to 0.875
- w_in_one: bfloat16 [200, 800], replicated, may hold values from -0.4375 to 0.4375
- w_out_one: bfloat16 [800, 200], replicated, may hold values from -0.21875 to 0.21875
- w_down: bfloat16 [800, 400], replicated, may hold values from -0.21875 to 0.21875
- kern_two: bfloat16 [7, 7, 400], replicated, may hold values from -0.875 to 0.875
- w_in_two: bfloat16 [400, 1600], replicated, may hold values from -0.3125 to 0.3125
- w_out_two: bfloat16 [1600, 400], replicated, may hold values from -0.15625 to 0.15625
- w_up: bfloat16 [400, 800], replicated, may hold values from -0.3125 to 0.3125
- cotangent: bfloat16 [8, 64, 16, 3200], P('lat', 'tiles'), may hold values from -0.0234375 to 0.0234375
Outputs:
- prediction: bfloat16 [8, 64, 16, 3200], P('lat', 'tiles')
- grads: float32 [2293760], P(('tiles', 'lat'))
Inputs may be any that keep to these rules, and one draw needn't show every extreme that they name: wet_count[b, g] counts the filled slots of group g in band b, slots 0 to wet_count - 1 of the group. Groups g and g + N/2 of a band (N groups) hold 2 tiles together, and one group, the same in every band, holds 2. `neighbours`: an entry of an empty slot, or one whose neighbour is land, off the grid's northern or southern edge, is -1. West and east entries use codes 0 to 2, north and south entries codes 0, 3 and 4. Bands hold 2 tile rows and every group 1 tile columns of its band, the same columns in every band, periodic from west to east; entries are mutual.
All inputs are finite; a program needn't handle non-finite values. No bound on the sum of `land_mask` on one device may be relied on, other than what follows from the above.
Results may differ from a plain program's by a relative error of at most 0.014.
Values may be sent and summed in bfloat16 or wider, within the bound.
No kernel may reach another device: no remote copies, remote signals or barrier semaphores. Data moves between devices by JAX's collectives and lax.ppermute only.
A program may use at most 128 MiB of HBM per device.

v0:
```python
import functools

import jax
import jax.numpy as jnp
from jax import lax
from jax.experimental import pallas as pl
from jax.experimental.pallas import tpu as pltpu
from jax.sharding import Mesh
from jax.sharding import PartitionSpec as P

TILES = ("z", "xh", "c")
LAT = ("xl", "y")
EPSILON = 1e-06
TANH_SCALE = 0.7978845608028654
CUBIC = 0.044715
LANES = 128
PIECE = 70
HELD = 72
UNIT = 3200
BLOCK = 560
C1, C2 = 200, 400
SIDE, HALF = 16, 8
F32, BF16 = jnp.float32, jnp.bfloat16
SPLIT_ROW = 5040
SPLIT = 4


def call(body, outs, scratch=(), smem=0, room=16, us=1):
    def run(*args):
        vmem = pl.BlockSpec(memory_space=pltpu.VMEM)
        specs = [pl.BlockSpec(memory_space=pltpu.SMEM)] * smem + [vmem] * (len(args) - smem)
        return pl.pallas_call(
            body,
            out_shape=[jax.ShapeDtypeStruct(shape, kind) for shape, kind in outs],
            in_specs=specs,
            out_specs=[vmem] * len(outs),
            scratch_shapes=[pltpu.VMEM(shape, kind) for shape, kind in scratch],
            compiler_params=pltpu.CompilerParams(vmem_limit_bytes=room * 2**20),
            cost_estimate=pl.CostEstimate(flops=us * 10**9, bytes_accessed=10**6, transcendentals=0),
        )(*args)

    return run


def product(left, right):
    return jnp.dot(left, right, preferred_element_type=F32)


def product_nt(left, right):
    return lax.dot_general(left, right, (((1,), (1,)), ((), ())), preferred_element_type=F32)


def product_tn(left, right):
    return lax.dot_general(left, right, (((0,), (0,)), ((), ())), preferred_element_type=F32)


def gelu_parts(values):
    square = values * values
    inner = jnp.tanh(TANH_SCALE * (values + CUBIC * square * values))
    half = 0.5 * (1.0 + inner)
    slope = half + 0.5 * values * (1.0 - inner * inner) * (TANH_SCALE * (1.0 + 3.0 * CUBIC * square))
    return values * half, slope


def lanes_of(shape):
    return lax.broadcasted_iota(jnp.int32, shape, len(shape) - 1)


def layer_norm(rows, channels):
    mean = jnp.sum(rows, axis=-1, keepdims=True) * (1.0 / channels)
    center = jnp.where(lanes_of(rows.shape) < channels, rows - mean, 0.0)
    scale = lax.rsqrt(jnp.sum(center * center, axis=-1, keepdims=True) * (1.0 / channels) + EPSILON)
    return center * scale, scale


def norm_back(grad_norm, normed, scale, channels):
    mean_grad = jnp.sum(grad_norm, axis=-1, keepdims=True) * (1.0 / channels)
    mean_cross = jnp.sum(grad_norm * normed, axis=-1, keepdims=True) * (1.0 / channels)
    return (grad_norm - mean_grad - normed * mean_cross) * scale


def choose(entries, slot, which, own, got):
    entry = entries[slot, which]
    held = jnp.maximum(entry, 0)
    place, source = held % 2, held // 2
    from_own = jnp.where((entry >= 0) & (source == 0), 1.0, 0.0)
    from_got = jnp.where((entry >= 0) & (source != 0), 1.0, 0.0)
    return own[place].astype(F32) * from_own + got[place].astype(F32) * from_got


def mask_lanes(mask, slot, filled):
    cells = SIDE * SIDE
    row = lax.broadcasted_iota(jnp.int32, (SIDE, cells), 0) * SIDE
    lane = lanes_of((SIDE, cells))
    live = jnp.broadcast_to(mask[slot : slot + 1, :].astype(F32), (SIDE, cells))
    live = jnp.where((lane >= row) & (lane < row + SIDE) & (filled > slot), live, 0.0).astype(BF16)
    cell = lax.broadcasted_iota(jnp.int32, (cells, SIDE), 0) % SIDE
    pick = jnp.where(cell == lanes_of((cells, SIDE)), 1.0, 0.0).astype(BF16)
    column = lax.broadcasted_iota(jnp.int32, (SIDE, SIDE * C1), 0) * C1
    lane = lanes_of((SIDE, SIDE * C1))
    spread = jnp.where((lane >= column) & (lane < column + C1), 1.0, 0.0).astype(BF16)
    return product(product(live, pick).astype(BF16), spread)


def rims_kernel(count, state, mask, west, east):
    for slot in range(2):
        masked = state[slot].astype(F32) * mask_lanes(mask, slot, count[0, 0])
        for k in range(3):
            west[slot, k] = masked[:, C1 * k : C1 * (k + 1)].astype(BF16)
            column = SIDE - 3 + k
            east[slot, k] = masked[:, C1 * column : C1 * (column + 1)].astype(BF16)


def to_blocks(values, wide, striped, lined, cat, slot):
    for t in range(25):
        striped[t] = values[:, LANES * t : LANES * (t + 1)]
    for a in range(2):
        for t in range(25):
            lined[:, LANES * t : LANES * (t + 1)] = striped[t, pl.ds(a, HALF, stride=2), :]
        for column in range(HALF):
            row = slot * 64 + column * HALF
            cat[row : row + HALF, C2 * a : C2 * (a + 1)] = lined[:, C2 * column : C2 * (column + 1)]


def before_kernel(count, state, mask, cotangent, w_up, field, mask_cat, cot_cat, change, mask_two, wide, striped, lined, held):
    field[...] = jnp.zeros(field.shape, F32)
    lane = lanes_of((SIDE, LANES))
    wide[...] = jnp.zeros(wide.shape, F32)
    for slot in range(2):
        spread = mask_lanes(mask, slot, count[0, 0])
        to_blocks(spread, wide, striped, lined, mask_cat, slot)
        to_blocks(cotangent[slot].astype(F32) * spread, wide, striped, lined, held, slot)
        wide[:, : SIDE * C1] = state[slot].astype(F32) * spread
        for column in range(SIDE):
            part = wide[:, C1 * column : C1 * column + 256]
            field[slot, 0, 3 + column, 3:19, :] = part[:, :LANES]
            field[slot, 1, 3 + column, 3:19, :] = jnp.where(lane < C1 - LANES, part[:, LANES:], 0.0)
    cot_cat[...] = held[...].astype(BF16)
    wet = mask_cat[:, 0:1]
    for k in range(1, 4):
        wet = jnp.maximum(wet, mask_cat[:, C1 * k : C1 * k + 1])
    mask_two[...] = jnp.broadcast_to(wet, (LANES, LANES))
    change[...] = (wet * product_nt(cot_cat[...], w_up[...])).astype(BF16)


def add_columns(entries, out, slot, side, channels, west, west_got, east, east_got):
    tiles = -(-channels // LANES)
    for which, start, own, got in ((0, 0, east, west_got), (1, side + 3, west, east_got)):
        value = choose(entries, slot, which, own, got)
        for t in range(tiles):
            width = min(LANES, channels - LANES * t)
            out[slot, t, start : start + 3, 3 : 3 + side, :width] = value[:, :, LANES * t : LANES * t + width]


def across(entries, slot, which, code):
    entry = entries[slot, which]
    return jnp.where((entry >= 0) & (entry // 2 == code), 1.0, 0.0)


def strips_of(entries, out, side, channels, top, bottom):
    north = [across(entries, slot, 2, 3) for slot in range(2)]
    south = [across(entries, slot, 3, 4) for slot in range(2)]
    for t in range(-(-channels // LANES)):
        width = min(LANES, channels - LANES * t)
        span = slice(LANES * t, LANES * t + width)
        parts = [out[slot, t, :, 3:6, :width] * north[slot] for slot in range(2)]
        top[:, :, span] = (parts[0] + parts[1]).astype(BF16)
        parts = [out[slot, t, :, side : side + 3, :width] * south[slot] for slot in range(2)]
        bottom[:, :, span] = (parts[0] + parts[1]).astype(BF16)


def add_rows(entries, out, slot, side, channels, top_got, bottom_got):
    for which, code, start, inner, got in ((2, 3, 0, side, top_got), (3, 4, side + 3, 3, bottom_got)):
        entry = entries[slot, which]
        place = jnp.maximum(entry, 0) % 2
        from_own = jnp.where((entry >= 0) & (entry // 2 == 0), 1.0, 0.0)
        from_got = across(entries, slot, which, code)
        for t in range(-(-channels // LANES)):
            width = min(LANES, channels - LANES * t)
            own = out[place, t, :, inner : inner + 3, :width]
            value = got[:, :, LANES * t : LANES * t + width].astype(F32)
            out[slot, t, :, start : start + 3, :width] = own * from_own + value * from_got


def strips_one_kernel(entries, field, west, west_got, east, east_got, out, top, bottom):
    out[...] = field[...]
    for slot in range(2):
        add_columns(entries, out, slot, SIDE, C1, west, west_got, east, east_got)
    strips_of(entries, out, SIDE, C1, top, bottom)


def strips_two_kernel(entries, rows, west, west_got, east, east_got, out, top, bottom):
    out[...] = jnp.zeros(out.shape, F32)
    for slot in range(2):
        for t in range(4):
            width = min(LANES, C2 - LANES * t)
            for column in range(HALF):
                start = slot * 64 + column * HALF
                out[slot, t, 3 + column, 3 : 3 + HALF, :width] = rows[start : start + HALF, LANES * t : LANES * t + width].astype(F32)
        add_columns(entries, out, slot, HALF, C2, west, west_got, east, east_got)
    strips_of(entries, out, HALF, C2, top, bottom)


def load_taps(kernel, taps, channels):
    tiles = -(-channels // LANES)
    taps[...] = jnp.zeros(taps.shape, F32)
    for t in range(tiles):
        width = min(LANES, channels - LANES * t)
        for p in range(7):
            taps[t, 7 * p : 7 * p + 7, :width] = kernel[p, :, LANES * t : LANES * t + width].astype(F32)


def conv_one(field, taps, out):
    def body(index, carry):
        slot, t = index // 2, index % 2
        for a in range(2):
            total = jnp.zeros((SIDE, HALF, LANES), F32)
            for p in range(7):
                for q in range(7):
                    window = field[slot, t, q : q + SIDE, pl.ds(a + p, HALF, stride=2), :]
                    total = total + window * taps[t, pl.ds(7 * p + q, 1), :][None]
            out[t, a, slot] = total
        return carry

    lax.fori_loop(0, 4, body, 0)


def conv_two(field, taps, out, flipped):
    def body(index, carry):
        slot, t = index // 4, index % 4
        total = jnp.zeros((HALF, HALF, LANES), F32)
        for p in range(7):
            for q in range(7):
                tap = 48 - (7 * p + q) if flipped else 7 * p + q
                total = total + field[slot, t, q : q + HALF, p : p + HALF, :] * taps[t, pl.ds(tap, 1), :][None]
        out[t, slot] = total
        return carry

    lax.fori_loop(0, 8, body, 0)


def first_kernel(entries, field, top_got, bottom_got, kern, w_in, w_out, w_down, mask_cat, mask_two,
                 out, normed, scales, blocks, coarse, west, east, taps, conv, held):
    out[...] = field[...]
    for slot in range(2):
        add_rows(entries, out, slot, SIDE, C1, top_got, bottom_got)
    load_taps(kern, taps, C1)
    conv_one(out, taps, conv)
    for a in range(2):
        for co in range(2):
            k = 2 * a + co
            rows, base = [], []
            for slot in range(2):
                for column in range(HALF):
                    place = 2 * column + co
                    rows.append(jnp.concatenate([conv[t, a, slot, place] for t in range(2)], axis=1))
                    base.append(jnp.concatenate([out[slot, t, 3 + place, pl.ds(3 + a, HALF, stride=2), :] for t in range(2)], axis=1))
            values, scale = layer_norm(jnp.concatenate(rows, axis=0), C1)
            normed[LANES * k : LANES * (k + 1), :] = values
            scales[LANES * k : LANES * (k + 1), :] = jnp.broadcast_to(scale, (LANES, LANES))
            hidden, _ = gelu_parts(product(values[:, :C1].astype(BF16), w_in[...]))
            branch = product_nt(hidden.astype(BF16), w_out[...])
            held[:, C1 * k : C1 * (k + 1)] = jnp.concatenate(base, axis=0)[:, :C1] + branch
    blocks[...] = (mask_cat[...] * held[...]).astype(BF16)
    wet = jnp.concatenate([mask_two[...]] * 4, axis=1)[:, :C2]
    rough = wet * product_nt(blocks[...], w_down[...])
    coarse[...] = rough.astype(BF16)
    send_rims(rough, west, east)


def send_rims(values, west, east):
    for slot in range(2):
        for k in range(3):
            start = slot * 64 + k * HALF
            west[slot, k] = values[start : start + HALF].astype(BF16)
            start = slot * 64 + (HALF - 3 + k) * HALF
            east[slot, k] = values[start : start + HALF].astype(BF16)


def rows_two(conv):
    return jnp.concatenate([conv[t].reshape(LANES, LANES) for t in range(4)], axis=1)


def second_kernel(entries, field, top_got, bottom_got, kern, w_in, w_out, coarse, change, mask_two,
                  out, normed_b, hidden, grad_pre, level, back, west, east, taps, conv):
    out[...] = field[...]
    for slot in range(2):
        add_rows(entries, out, slot, HALF, C2, top_got, bottom_got)
    load_taps(kern, taps, C2)
    conv_two(out, taps, conv, False)
    values, scale = layer_norm(rows_two(conv), C2)
    values = values[:, :C2]
    normed_b[...] = values.astype(BF16)
    act, slope = gelu_parts(product(normed_b[...], w_in[...]))
    hidden[...] = act.astype(BF16)
    grad_pre[...] = (product(change[...], w_out[...]) * slope).astype(BF16)
    wet = jnp.concatenate([mask_two[...]] * 4, axis=1)[:, :C2]
    level[...] = (wet * (coarse[...].astype(F32) + product_nt(hidden[...], w_out[...]))).astype(BF16)
    reverse = norm_back(product_nt(grad_pre[...], w_in[...]), values, scale, C2)
    back[...] = reverse.astype(BF16)
    send_rims(reverse, west, east)


def predict_kernel(blocks, level, w_up, mask_cat, prediction, held, lined, striped):
    held[...] = mask_cat[...] * (blocks[...].astype(F32) + product(level[...], w_up[...]))
    for slot in range(2):
        for a in range(2):
            for column in range(HALF):
                row = slot * 64 + column * HALF
                lined[:, C2 * column : C2 * (column + 1)] = held[row : row + HALF, C2 * a : C2 * (a + 1)]
            for t in range(25):
                striped[t, pl.ds(a, HALF, stride=2), :] = lined[:, LANES * t : LANES * (t + 1)]
        for t in range(25):
            prediction[slot, :, LANES * t : LANES * (t + 1)] = striped[t].astype(BF16)


def hold(held, value):
    rows, width = value.shape
    for t in range(-(-width // LANES)):
        part = value[:, LANES * t : min(width, LANES * (t + 1))]
        if part.shape[1] < LANES:
            held[t, :rows, :] = jnp.zeros((rows, LANES), F32)
        held[t, :rows, : part.shape[1]] = part


def lay_flat(flat, source, first_entry, rows, width, first_row):
    unit = UNIT // width
    count = rows // unit
    base = first_entry // LANES - first_row
    tiles = -(-width // LANES)
    lane = lax.broadcasted_iota(jnp.int32, (count, LANES), 1)
    parts = {}
    for a in range(unit):
        for t in range(tiles):
            value = source[t, pl.ds(a, count, stride=unit), :]
            place = first_entry % LANES + width * a + LANES * t
            shift = place % LANES
            if shift:
                value = pltpu.roll(value, shift, 1)
                low = jnp.where(lane >= shift, value, 0.0)
                high = jnp.where(lane < shift, value, 0.0)
                parts.setdefault(place // LANES, []).append(low)
                if not (t == tiles - 1 and shift + width - LANES * t <= LANES):
                    parts.setdefault(place // LANES + 1, []).append(high)
            else:
                parts.setdefault(place // LANES, []).append(value)
    merged = {j: functools.reduce(jnp.add, values) for j, values in parts.items()}
    for j in range(1, 25):
        flat[pl.ds(base + j, count, stride=25), :] = merged[j]
    head = merged[0]
    if 25 in merged:
        tail = merged[25]
        row = lax.broadcasted_iota(jnp.int32, (count, LANES), 0)
        before = pltpu.roll(tail, 1, 0) if count % 8 == 0 else jnp.concatenate([tail[-1:], tail[:-1]], axis=0)
        head = head + jnp.where(row > 0, before, 0.0)
    opening = flat[base : base + 1, :]
    flat[pl.ds(base, count, stride=25), :] = head
    flat[base : base + 1, :] = flat[base : base + 1, :] + opening
    if 25 in merged:
        flat[base + 25 * count : base + 25 * count + 1, :] = tail[count - 1 : count, :]
    else:
        flat[base + 25 * count : base + 25 * count + 1, :] = jnp.zeros((1, LANES), jnp.float32)


def clear_taps(held, tiles, rows):
    for t in range(tiles):
        held[t, 48:rows, :] = jnp.zeros((rows - 48, LANES), F32)


def grads_two_kernel(field, back, normed_b, hidden, grad_pre, level, change, cot_cat, keep, send, flat, held, tall, sums):
    flat[0:64, :] = jnp.zeros((64, LANES), F32)
    clear_taps(held, 4, 56)
    for t in range(4):
        width = min(LANES, C2 - LANES * t)
        deltas = []
        for slot in range(2):
            delta = back[64 * slot : 64 * (slot + 1), LANES * t : LANES * t + width].astype(F32)
            if width < LANES:
                delta = jnp.concatenate([delta, jnp.zeros((64, LANES - width), F32)], axis=1)
            deltas.append(delta.reshape(HALF, HALF, LANES))
        for p in range(7):
            for q in range(7):
                total = jnp.zeros((HALF, LANES), F32)
                for slot in range(2):
                    total = total + jnp.sum(field[slot, t, q : q + HALF, p : p + HALF, :] * deltas[slot], axis=0)
                sums[7 * p + q] = total
        held[t, :49, :] = jnp.sum(sums[...], axis=1)
    lay_flat(flat, held, 649800, 56, C2, SPLIT_ROW)
    hold(held, product_tn(normed_b[...], grad_pre[...]))
    lay_flat(flat, held, 669400, C2, 4 * C2, SPLIT_ROW)
    hold(tall, product_tn(hidden[...], change[...]))
    lay_flat(flat, tall, 1309400, 4 * C2, C2, SPLIT_ROW)
    hold(held, product_tn(level[...], cot_cat[...]))
    lay_flat(flat, held, 1949400, C2, 4 * C1, SPLIT_ROW)
    last = 17730 - SPLIT_ROW
    flat[last:, :] = jnp.zeros((17920 + 8 - SPLIT_ROW - last, LANES), F32)
    keep[:8, 0] = jnp.zeros((8, HELD, LANES), BF16)
    send[:8, 0] = jnp.zeros((8, HELD, LANES), BF16)
    split_out(lax.axis_index("c"), flat, keep, send, 9, 32, store_two)


def split_out(core, flat, keep, send, first, stop, store):
    def write(even, odd):
        for block in range(first, stop):
            target = odd if block % 2 else even
            for xl in range(2):
                for y in range(4):
                    start = (block - first) * BLOCK + (xl * 4 + y) * PIECE
                    store(target, block // 4, block // 2 % 2, xl, y, flat[start : start + HELD, :].astype(BF16))

    @pl.when(core == 0)
    def _():
        write(keep, send)

    @pl.when(core != 0)
    def _():
        write(send, keep)


def store_two(target, z, xh, xl, y, value):
    target[8 * xh + 4 * xl + y, z - 2] = value


def store_one(target, z, xh, xl, y, value):
    target[8 * xh + 4 * xl + y, z] = value


def last_kernel(entries, delta, top_got, bottom_got, kern, change, mask_two, mask_cat, cot_cat, blocks,
                w_down, w_in, w_out, normed, scales, field, keep, send,
                out, taps, conv, held_cat, rough, hidden, grad_pre, fine, back, sums, flat, held):
    out[...] = delta[...]
    for slot in range(2):
        add_rows(entries, out, slot, HALF, C2, top_got, bottom_got)
    load_taps(kern, taps, C2)
    conv_two(out, taps, conv, True)
    wet = jnp.concatenate([mask_two[...]] * 4, axis=1)[:, :C2]
    rough[...] = (wet * (change[...].astype(F32) + rows_two(conv)[:, :C2])).astype(BF16)
    held_cat[...] = mask_cat[...] * (cot_cat[...].astype(F32) + product(rough[...], w_down[...]))
    flat[0:8, :] = jnp.zeros((8, LANES), F32)
    for k in range(4):
        a, co = k // 2, k % 2
        rows = slice(LANES * k, LANES * (k + 1))
        fine[rows, :] = held_cat[:, C1 * k : C1 * (k + 1)].astype(BF16)
        values = normed[rows, :]
        act, slope = gelu_parts(product(values[:, :C1].astype(BF16), w_in[...]))
        hidden[rows, :] = act.astype(BF16)
        grad_pre[rows, :] = (product(fine[rows, :], w_out[...]) * slope).astype(BF16)
        grad = product_nt(grad_pre[rows, :], w_in[...])
        reverse = norm_back(grad, values[:, :C1], scales[rows, 0:1], C1)
        for slot in range(2):
            for column in range(HALF):
                start = slot * 64 + column * HALF
                part = reverse[start : start + HALF]
                back[0, a, slot, 2 * column + co] = part[:, :LANES]
                back[1, a, slot, 2 * column + co] = jnp.concatenate([part[:, LANES:], jnp.zeros((HALF, 2 * LANES - C1), F32)], axis=1)
    clear_taps(held, 2, 64)
    for t in range(2):
        sums[...] = jnp.zeros(sums.shape, F32)

        def body(index, carry):
            slot, a = index // 2, index % 2
            part = back[t, a, slot]
            for p in range(7):
                for q in range(7):
                    window = field[slot, t, q : q + SIDE, pl.ds(a + p, HALF, stride=2), :]
                    sums[7 * p + q] = sums[7 * p + q] + jnp.sum(window * part, axis=0)
            return carry

        lax.fori_loop(0, 4, body, 0)
        held[t, :49, :] = jnp.sum(sums[...], axis=1)
    lay_flat(flat, held, 0, 64, C1, 0)
    hold(held, product_tn(normed[:, :C1].astype(BF16), grad_pre[...]))
    lay_flat(flat, held, 9800, C1, 4 * C1, 0)
    hold(held, product_tn(hidden[...], fine[...]))
    lay_flat(flat, held, 169800, 4 * C1, C1, 0)
    hold(held, product_tn(blocks[...], rough[...]))
    lay_flat(flat, held, 329800, 4 * C1, C2, 0)
    flat[5077:, :] = jnp.zeros((5608 - 5077, LANES), F32)
    keep[8:, 2] = jnp.zeros((8, HELD, LANES), BF16)
    send[8:, 2] = jnp.zeros((8, HELD, LANES), BF16)
    split_out(lax.axis_index("c"), flat, keep, send, 0, 10, store_one)


def around(array, axes, step):
    size = 1
    for axis in axes:
        size *= lax.axis_size(axis)
    return lax.ppermute(array, axes, [(i, (i + step) % size) for i in range(size)])


def wide_sum(*parts):
    total = parts[0].astype(F32)
    for part in parts[1:]:
        total = total + part.astype(F32)
    return total.astype(BF16)


def other_core(send):
    return lax.ppermute(send, "c", [(0, 1), (1, 0)])


def added(terms):
    result = terms[0].astype(F32)
    for term in terms[1:]:
        result = result + term.astype(F32)
    return result.astype(BF16)


def x_parts_kernel(*refs):
    parts, outs = refs[:-4], refs[-4:]
    x = 2 * lax.axis_index("xh") + lax.axis_index("xl")
    for k in range(4):
        for z in range(outs[k].shape[0]):
            outs[k][z] = added([part[x ^ k, z] for part in parts])


def y_parts_kernel(keep, got, *outs):
    y = lax.axis_index("y")
    for k in range(4):
        for x in range(4):
            place = 4 * x + (y + k) % 4
            for z in range(outs[k].shape[1]):
                outs[k][x, z] = added([keep[place, z], got[place, z]])


def x_first_kernel(keep, got, *outs):
    x = 2 * lax.axis_index("xh") + lax.axis_index("xl")
    for k in range(4):
        for y in range(4):
            place = 4 * (x ^ k) + y
            for z in range(3):
                outs[k][y, z] = added([keep[place, z], got[place, z]])


def y_second_kernel(*refs):
    parts, outs = refs[:4], refs[4:]
    y = lax.axis_index("y")
    for k in range(4):
        for z in range(3):
            outs[k][z] = added([part[(y + k) % 4, z] for part in parts])


def over_y(parts):
    return [parts[0]] + [around(parts[k], ("y",), k) for k in range(1, 4)]


def over_x(parts):
    return [parts[0]] + [lax.ppermute(parts[k], ("xh", "xl"), [(i, i ^ k) for i in range(4)]) for k in range(1, 4)]


def merge_kernel(*refs):
    one, two, out = refs[:4], refs[4:8], refs[8]
    for z in range(8):
        terms = []
        if z < 3:
            terms += [ref[z] for ref in one]
        if z >= 2:
            terms += [ref[z - 2] for ref in two]
        out[z] = added(terms)


def final_kernel(parts, out):
    total = parts[0].astype(F32)
    for k in range(1, parts.shape[0]):
        total = total + parts[k].astype(F32)
    out[...] = total


def local(ocean_state, land_mask, wet_count, neighbours, kern_one, w_in_one, w_out_one, w_down, kern_two, w_in_two, w_out_two, w_up, cotangent):
    state, cot = ocean_state[0], cotangent[0]
    w_out_one, w_down, w_out_two = w_out_one.T, w_down.T, w_out_two.T
    mask = land_mask[0]
    entries = neighbours[0]
    rims_one, rims_two = (2, 3, SIDE, C1), (2, 3, HALF, C2)
    strip_one, strip_two = (22, 3, C1), (14, 3, C2)
    field_one, field_two = (2, 2, 22, 24, LANES), (2, 4, 14, 16, LANES)
    cat = (LANES, 4 * C1)
    west, east = call(rims_kernel, [(rims_one, BF16)] * 2, smem=1)(wet_count, state, mask)
    west_got, east_got = around(east, TILES, 1), around(west, TILES, -1)
    field, mask_cat, cot_cat, change, mask_two = call(
        before_kernel,
        [(field_one, F32), (cat, F32), (cat, BF16), ((LANES, C2), BF16), ((LANES, LANES), F32)],
        [((SIDE, 3328), F32), ((25, SIDE, LANES), F32), ((HALF, SIDE * C1), F32), (cat, F32)],
        room=16, us=2, smem=1,
    )(wet_count, state, mask, cot, w_up)
    field, top, bottom = call(strips_one_kernel, [(field_one, F32), (strip_one, BF16), (strip_one, BF16)], smem=1)(
        entries, field, west, west_got, east, east_got
    )
    top_got, bottom_got = around(bottom, LAT, 1), around(top, LAT, -1)
    field_one_own, normed_one, scales_one, blocks, coarse, west, east = call(
        first_kernel,
        [(field_one, F32), ((512, 256), F32), ((512, LANES), F32), (cat, BF16), ((LANES, C2), BF16), (rims_two, BF16), (rims_two, BF16)],
        [((2, 49, LANES), F32), ((2, 2, 2, SIDE, HALF, LANES), F32), (cat, F32)],
        room=16, us=6, smem=1,
    )(entries, field, top_got, bottom_got, kern_one, w_in_one, w_out_one, w_down, mask_cat, mask_two)

    def strips_two(rows, west, west_got, east, east_got):
        return call(strips_two_kernel, [(field_two, F32), (strip_two, BF16), (strip_two, BF16)], smem=1)(
            entries, rows, west, west_got, east, east_got
        )

    two = ((LANES, 4 * C2), BF16)
    slim = ((LANES, C2), BF16)
    west_got, east_got = around(east, TILES, 1), around(west, TILES, -1)
    field_two_own, top, bottom = strips_two(coarse, west, west_got, east, east_got)
    sides = field_two_own, around(bottom, LAT, 1), around(top, LAT, -1)
    field_in_two, normed_two, hidden_two, grad_pre_two, level, back, west, east = call(
        second_kernel,
        [(field_two, F32), slim, two, two, slim, slim, (rims_two, BF16), (rims_two, BF16)],
        [((4, 49, LANES), F32), ((4, 2, HALF, HALF, LANES), F32)],
        room=16, us=6, smem=1,
    )(entries, *sides, kern_two, w_in_two, w_out_two, coarse, change, mask_two)
    west_got, east_got = around(east, TILES, 1), around(west, TILES, -1)
    keep_two, send_two = call(
        grads_two_kernel,
        [((16, 6, HELD, LANES), BF16)] * 2,
        [((17920 + 8 - SPLIT_ROW, LANES), F32), ((13, C2, LANES), F32), ((4, 4 * C2, LANES), F32), ((49, HALF, LANES), F32)],
        room=16, us=7,
    )(field_in_two, back, normed_two, hidden_two, grad_pre_two, level, change, cot_cat)
    west_got, east_got, send_two = lax.optimization_barrier((west_got, east_got, send_two))
    got_two = other_core(send_two)
    (prediction,) = call(
        predict_kernel,
        [((2, SIDE, SIDE * C1), BF16)],
        [(cat, F32), ((HALF, SIDE * C1), F32), ((25, SIDE, LANES), F32)],
    )(blocks, level, w_up, mask_cat)
    field, top, bottom = strips_two(back, west, west_got, east, east_got)
    top_got, bottom_got = around(bottom, LAT, 1), around(top, LAT, -1)
    parts = list(call(y_parts_kernel, [((4, 6, HELD, LANES), BF16)] * 4)(keep_two, got_two))
    top_got, bottom_got, *parts[1:] = lax.optimization_barrier((top_got, bottom_got, *parts[1:]))
    parts_two = over_y(parts)
    sides = field, top_got, bottom_got
    keep_one, send_one = call(
        last_kernel,
        [((16, 3, HELD, LANES), BF16)] * 2,
        [
            (field_two, F32),
            ((4, 49, LANES), F32),
            ((4, 2, HALF, HALF, LANES), F32),
            (cat, F32),
            slim,
            ((512, 4 * C1), BF16),
            ((512, 4 * C1), BF16),
            ((512, C1), BF16),
            ((2, 2, 2, SIDE, HALF, LANES), F32),
            ((49, HALF, LANES), F32),
            ((5608, LANES), F32),
            ((7, 800, LANES), F32),
        ],
        room=16, us=10, smem=1,
    )(entries, *sides, kern_two, change, mask_two, mask_cat, cot_cat, blocks, w_down, w_in_one, w_out_one, normed_one, scales_one, field_one_own)
    send_one, parts_two[1], parts_two[3] = lax.optimization_barrier((send_one, parts_two[1], parts_two[3]))
    return prediction[None], finish(keep_one, send_one, parts_two)


def finish(keep_one, send_one, parts_two):
    piece = ((3, HELD, LANES), BF16)
    parts = call(x_first_kernel, [((4, 3, HELD, LANES), BF16)] * 4)(keep_one, other_core(send_one))
    parts_one = over_x(parts)
    parts_two = call(x_parts_kernel, [((6, HELD, LANES), BF16)] * 4)(*parts_two)
    parts_one[1], _ = lax.optimization_barrier((parts_one[1], parts_two[1]))
    parts_two = over_x(parts_two)
    parts_one = over_y(call(y_second_kernel, [piece] * 4)(*parts_one))
    (total,) = call(merge_kernel, [((8, HELD, LANES), BF16)])(*parts_one, *parts_two)
    total = lax.all_to_all(total, "z", 0, 0)
    (total,) = call(final_kernel, [((HELD, LANES), F32)])(total)
    return total[:PIECE].reshape(-1)


def solution(mesh):
    mesh = Mesh(mesh.devices.reshape(8, 2, 2, 2, 4), TILES + LAT)
    return jax.shard_map(
        local,
        mesh=mesh,
        in_specs=(
            P(LAT, TILES, None, None),
            P(LAT, TILES, None),
            P(LAT, TILES),
            P(LAT, TILES, None),
            P(),
            P(),
            P(),
            P(),
            P(),
            P(),
            P(),
            P(),
            P(LAT, TILES, None, None),
        ),
        out_specs=(P(LAT, TILES, None, None), P(TILES + LAT)),
        check_vma=False,
    )
```

profile of v0, /device:TPU:24, one launch (start us, length us, event | category | flops | bytes accessed | tf_op | source)
XLA Modules:
  0.0 117.9 jit_solution(16788803121818710715)
XLA Ops:
  1.3 0.9 copy-done.6
  2.2 0.7 copy-done.10
  2.9 0.5 shard_map.141
  3.5 7.8 %collective-permute-start.1 = (bf16[2,3,16,200]{3,2,1,0:T(8,128)(2,1)S(1)}, bf16[2,3,16,200]{3,2,1,0:T(8,128)(2,1)S(1)}, u32[]{:S(2)}, u32[]{:S(2)}) collective-permute-start(bf16[2,3,16,200]{3,2,1,0:T(8,128)(2,1)S(1)} %get-tuple-element.66.west), channel_id=1, source_target_pairs={{0,248},{8,0},{16,8},{24,16},{32,24},{40,32},{48,40},{56,48},{64,5... | collective-permute-start | bytes 115208 | tf_op jit(solution)/shard_map/ppermute | solution.py:488
  11.3 1.0 shard_map.140
  12.3 0.7 collective-permute-done.west_got
  13.1 0.7 shard_map.142
  13.8 0.3 collective-permute-start.2
  14.2 1.8 %collective-permute-start.3 = (bf16[22,3,200]{2,1,0:T(4,128)(2,1)S(1)}, bf16[22,3,200]{2,1,0:T(4,128)(2,1)S(1)}, u32[]{:S(2)}, u32[]{:S(2)}) collective-permute-start(bf16[22,3,200]{2,1,0:T(4,128)(2,1)S(1)} %get-tuple-element.70), channel_id=1, source_target_pairs={{0,7},{1,0},{2,1},{3,2},{4,3},{5,4},{6,5},{7,6},{8,15},{9,8},{10,9... | collective-permute-start | bytes 79208 | tf_op jit(solution)/shard_map/ppermute | solution.py:488
  15.9 2.0 %collective-permute-done.2.top_got = bf16[22,3,200]{2,1,0:T(4,128)(2,1)S(1)} collective-permute-done((bf16[22,3,200]{2,1,0:T(4,128)(2,1)S(1)}, bf16[22,3,200]{2,1,0:T(4,128)(2,1)S(1)}, u32[]{:S(2)}, u32[]{:S(2)}) %collective-permute-start.2) | collective-permute-done | bytes 26432 | tf_op jit(solution)/shard_map/ppermute | solution.py:488
  18.0 2.4 %collective-permute-done.3.bottom_got = bf16[22,3,200]{2,1,0:T(4,128)(2,1)S(1)} collective-permute-done((bf16[22,3,200]{2,1,0:T(4,128)(2,1)S(1)}, bf16[22,3,200]{2,1,0:T(4,128)(2,1)S(1)}, u32[]{:S(2)}, u32[]{:S(2)}) %collective-permute-start.3) | collective-permute-done | bytes 26432 | tf_op jit(solution)/shard_map/ppermute | solution.py:488
  20.3 4.5 %shard_map.143 = (f32[2,2,22,24,128]{4,3,2,1,0:T(8,128)S(1)}, f32[512,256]{1,0:T(8,128)S(1)}, f32[512,128]{1,0:T(8,128)S(1)}, bf16[128,800]{1,0:T(8,128)(2,1)S(1...) custom-call(s32[2,4]{1,0:T(2,128)S(1)} %bitcast.21, ...), custom_call_target="tpu_custom_call" | custom-call | flops 6000000000 | bytes 1000000 | tf_op jit(solution)/shard_map/pallas_call | solution.py:32
  25.0 5.3 %collective-permute-start.5 = (bf16[2,3,8,400]{3,2,1,0:T(8,128)(2,1)S(1)}, bf16[2,3,8,400]{3,2,1,0:T(8,128)(2,1)S(1)}, u32[]{:S(2)}, u32[]{:S(2)}) collective-permute-start(bf16[2,3,8,400]{3,2,1,0:T(8,128)(2,1)S(1)} %get-tuple-element.75.west), channel_id=1, source_target_pairs={{0,248},{8,0},{16,8},{24,16},{32,24},{40,32},{48,40},{56,48},{64,5... | collective-permute-start | bytes 115208 | tf_op jit(solution)/shard_map/ppermute | solution.py:488
  30.3 1.9 %collective-permute-done.4.west_got = bf16[2,3,8,400]{3,2,1,0:T(8,128)(2,1)S(1)} collective-permute-done((bf16[2,3,8,400]{3,2,1,0:T(8,128)(2,1)S(1)}, bf16[2,3,8,400]{3,2,1,0:T(8,128)(2,1)S(1)}, u32[]{:S(2)}, u32[]{:S(2)}) %collective-permute-start.4) | collective-permute-done | bytes 38432 | tf_op jit(solution)/shard_map/ppermute | solution.py:488
  32.2 0.7 shard_map.144
  33.0 2.0 %collective-permute-start.7 = (bf16[14,3,400]{2,1,0:T(4,128)(2,1)S(1)}, bf16[14,3,400]{2,1,0:T(4,128)(2,1)S(1)}, u32[]{:S(2)}, u32[]{:S(2)}) collective-permute-start(bf16[14,3,400]{2,1,0:T(4,128)(2,1)S(1)} %get-tuple-element.79), channel_id=1, source_target_pairs={{0,7},{1,0},{2,1},{3,2},{4,3},{5,4},{6,5},{7,6},{8,15},{9,8},{10,9... | collective-permute-start | bytes 100808 | tf_op jit(solution)/shard_map/ppermute | solution.py:488
  35.1 2.2 %collective-permute-done.6.top_got = bf16[14,3,400]{2,1,0:T(4,128)(2,1)S(1)} collective-permute-done((bf16[14,3,400]{2,1,0:T(4,128)(2,1)S(1)}, bf16[14,3,400]{2,1,0:T(4,128)(2,1)S(1)}, u32[]{:S(2)}, u32[]{:S(2)}) %collective-permute-start.6) | collective-permute-done | bytes 33632 | tf_op jit(solution)/shard_map/ppermute | solution.py:488
  37.2 2.2 %collective-permute-done.7.bottom_got = bf16[14,3,400]{2,1,0:T(4,128)(2,1)S(1)} collective-permute-done((bf16[14,3,400]{2,1,0:T(4,128)(2,1)S(1)}, bf16[14,3,400]{2,1,0:T(4,128)(2,1)S(1)}, u32[]{:S(2)}, u32[]{:S(2)}) %collective-permute-start.7) | collective-permute-done | bytes 33632 | tf_op jit(solution)/shard_map/ppermute | solution.py:488
  39.4 3.9 %shard_map.145 = (f32[2,4,14,16,128]{4,3,2,1,0:T(8,128)S(1)}, bf16[128,400]{1,0:T(8,128)(2,1)S(1)}, bf16[128,1600]{1,0:T(8,128)(2,1)S(1)}, bf16[128,1600]{1,0:T(...) custom-call(s32[2,4]{1,0:T(2,128)S(1)} %bitcast.23, ...), custom_call_target="tpu_custom_call" | custom-call | flops 6000000000 | bytes 1000000 | tf_op jit(solution)/shard_map/pallas_call | solution.py:32
  43.6 5.3 %collective-permute-start.9 = (bf16[2,3,8,400]{3,2,1,0:T(8,128)(2,1)S(1)}, bf16[2,3,8,400]{3,2,1,0:T(8,128)(2,1)S(1)}, u32[]{:S(2)}, u32[]{:S(2)}) collective-permute-start(bf16[2,3,8,400]{3,2,1,0:T(8,128)(2,1)S(1)} %get-tuple-element.83.west), channel_id=1, source_target_pairs={{0,248},{8,0},{16,8},{24,16},{32,24},{40,32},{48,40},{56,48},{64,5... | collective-permute-start | bytes 115208 | tf_op jit(solution)/shard_map/ppermute | solution.py:488
  49.0 3.6 %shard_map.147 = (bf16[16,6,72,128]{3,2,1,0:T(8,128)(2,1)S(1)}, bf16[16,6,72,128]{3,2,1,0:T(8,128)(2,1)S(1)}) custom-call(f32[2,4,14,16,128]{4,3,2,1,0:T(8,128)S(1)} %get-tuple-element.85.field, bf16[128,400]{1,0:T(8,128)(2,1)S(1)} %get-tuple-element.82.back.rows, bf16[128,400]{1,0:T(8,128)(2,1)S(1)} %get-tuple-element.86.normed_b, ...), custom_call_target="tpu_custom_call" | custom-call | flops 7000000000 | bytes 1000000 | tf_op jit(solution)/shard_map/pallas_call | solution.py:32
  52.7 0.7 shard_map.148
  53.6 2.0 %collective-permute-start.11 = (bf16[14,3,400]{2,1,0:T(4,128)(2,1)S(1)}, bf16[14,3,400]{2,1,0:T(4,128)(2,1)S(1)}, u32[]{:S(2)}, u32[]{:S(2)}) collective-permute-start(bf16[14,3,400]{2,1,0:T(4,128)(2,1)S(1)} %get-tuple-element.95), channel_id=1, source_target_pairs={{0,7},{1,0},{2,1},{3,2},{4,3},{5,4},{6,5},{7,6},{8,15},{9,8},{10,9... | collective-permute-start | bytes 100808 | tf_op jit(solution)/shard_map/ppermute | solution.py:488
  55.6 0.8 collective-permute-done.12.got
  56.4 0.4 shard_map.149
  56.8 1.1 collective-permute-done.10.top_got
  57.9 2.2 %collective-permute-done.11.bottom_got = bf16[14,3,400]{2,1,0:T(4,128)(2,1)S(1)} collective-permute-done((bf16[14,3,400]{2,1,0:T(4,128)(2,1)S(1)}, bf16[14,3,400]{2,1,0:T(4,128)(2,1)S(1)}, u32[]{:S(2)}, u32[]{:S(2)}) %collective-permute-start.11) | collective-permute-done | bytes 33632 | tf_op jit(solution)/shard_map/ppermute | solution.py:488
  60.1 2.0 %collective-permute-start.14 = (bf16[4,6,72,128]{3,2,1,0:T(8,128)(2,1)S(1)}, bf16[4,6,72,128]{3,2,1,0:T(8,128)(2,1)S(1)}, u32[]{:S(2)}, u32[]{:S(2)}) collective-permute-start(bf16[4,6,72,128]{3,2,1,0:T(8,128)(2,1)S(1)} %get-tuple-element.109), channel_id=1, source_target_pairs={{0,3},{1,0},{2,1},{3,2},{4,7},{5,4},{6,5},{7,6},{8,11},{9,8},{10,9... | collective-permute-start | bytes 1327112 | tf_op jit(solution)/shard_map/ppermute | solution.py:488
  62.1 8.0 %shard_map.150 = (bf16[16,3,72,128]{3,2,1,0:T(8,128)(2,1)S(1)}, bf16[16,3,72,128]{3,2,1,0:T(8,128)(2,1)S(1)}) custom-call(s32[2,4]{1,0:T(2,128)S(1)} %bitcast.25, f32[2,4,14,16,128]{4,3,2,1,0:T(8,128)S(1)} %get-tuple-element.93.delta, bf16[14,3,400]{2,1,0:T(4,128)(2,1)S(1)} %collective-permute-done.10.top_got, ...), custom_call_target="tpu_custom_call" | custom-call | flops 10000000000 | bytes 1000000 | tf_op jit(solution)/shard_map/pallas_call | solution.py:32
  70.1 1.8 %collective-permute-done.13.refs_1_ = bf16[4,6,72,128]{3,2,1,0:T(8,128)(2,1)S(1)} collective-permute-done((bf16[4,6,72,128]{3,2,1,0:T(8,128)(2,1)S(1)}, bf16[4,6,72,128]{3,2,1,0:T(8,128)(2,1)S(1)}, u32[]{:S(2)}, u32[]{:S(2)}) %collective-permute-start.13) | collective-permute-done | bytes 442400 | tf_op jit(solution)/shard_map/ppermute | solution.py:488
  71.9 1.2 %collective-permute-done.14.refs_3_ = bf16[4,6,72,128]{3,2,1,0:T(8,128)(2,1)S(1)} collective-permute-done((bf16[4,6,72,128]{3,2,1,0:T(8,128)(2,1)S(1)}, bf16[4,6,72,128]{3,2,1,0:T(8,128)(2,1)S(1)}, u32[]{:S(2)}, u32[]{:S(2)}) %collective-permute-start.14) | collective-permute-done | bytes 442400 | tf_op jit(solution)/shard_map/ppermute | solution.py:488
  73.1 0.9 collective-permute-start.17
  73.9 1.6 %collective-permute-done.15.got = bf16[16,3,72,128]{3,2,1,0:T(8,128)(2,1)S(1)} collective-permute-done((bf16[16,3,72,128]{3,2,1,0:T(8,128)(2,1)S(1)}, bf16[16,3,72,128]{3,2,1,0:T(8,128)(2,1)S(1)}, u32[]{:S(2)}, u32[]{:S(2)}) %collective-permute-start.15) | collective-permute-done | bytes 884768 | tf_op jit(solution)/shard_map/ppermute | solution.py:499
  75.7 1.4 %collective-permute-start.16 = (bf16[4,3,72,128]{3,2,1,0:T(8,128)(2,1)S(1)}, bf16[4,3,72,128]{3,2,1,0:T(8,128)(2,1)S(1)}, u32[]{:S(2)}, u32[]{:S(2)}) collective-permute-start(bf16[4,3,72,128]{3,2,1,0:T(8,128)(2,1)S(1)} %get-tuple-element.112), channel_id=1, source_target_pairs={{0,4},{4,0},{16,20},{20,16},{1,5},{5,1},{17,21},{21,17},{2,6},{6,2... | collective-permute-start | bytes 663560 | tf_op jit(solution)/shard_map/ppermute | solution.py:548
  77.1 3.4 %collective-permute-start.19 = (bf16[4,3,72,128]{3,2,1,0:T(8,128)(2,1)S(1)}, bf16[4,3,72,128]{3,2,1,0:T(8,128)(2,1)S(1)}, u32[]{:S(2)}, u32[]{:S(2)}) collective-permute-start(bf16[4,3,72,128]{3,2,1,0:T(8,128)(2,1)S(1)} %get-tuple-element.120), channel_id=1, source_target_pairs={{0,20},{4,16},{16,4},{20,0},{1,21},{5,17},{17,5},{21,1},{2,22},{6,... | collective-permute-start | bytes 663560 | tf_op jit(solution)/shard_map/ppermute | solution.py:548
  80.5 6.7 %collective-permute-done.17.refs_2_ = bf16[4,6,72,128]{3,2,1,0:T(8,128)(2,1)S(1)} collective-permute-done((bf16[4,6,72,128]{3,2,1,0:T(8,128)(2,1)S(1)}, bf16[4,6,72,128]{3,2,1,0:T(8,128)(2,1)S(1)}, u32[]{:S(2)}, u32[]{:S(2)}) %collective-permute-start.17) | collective-permute-done | bytes 442400 | tf_op jit(solution)/shard_map/ppermute | solution.py:488
  87.4 1.4 %collective-permute-start.23 = (bf16[6,72,128]{2,1,0:T(8,128)(2,1)S(1)}, bf16[6,72,128]{2,1,0:T(8,128)(2,1)S(1)}, u32[]{:S(2)}, u32[]{:S(2)}) collective-permute-start(bf16[6,72,128]{2,1,0:T(8,128)(2,1)S(1)} %get-tuple-element.117), channel_id=1, source_target_pairs={{0,4},{4,0},{16,20},{20,16},{1,5},{5,1},{17,21},{21,17},{2,6},{6,2... | collective-permute-start | bytes 331784 | tf_op jit(solution)/shard_map/ppermute | solution.py:548
  88.8 3.4 %collective-permute-start.25 = (bf16[6,72,128]{2,1,0:T(8,128)(2,1)S(1)}, bf16[6,72,128]{2,1,0:T(8,128)(2,1)S(1)}, u32[]{:S(2)}, u32[]{:S(2)}) collective-permute-start(bf16[6,72,128]{2,1,0:T(8,128)(2,1)S(1)} %get-tuple-element.127), channel_id=1, source_target_pairs={{0,20},{4,16},{16,4},{20,0},{1,21},{5,17},{17,5},{21,1},{2,22},{6,... | collective-permute-start | bytes 331784 | tf_op jit(solution)/shard_map/ppermute | solution.py:548
  92.3 0.4 collective-permute-start.20
  92.7 2.3 %collective-permute-start.21 = (bf16[3,72,128]{2,1,0:T(8,128)(2,1)S(1)}, bf16[3,72,128]{2,1,0:T(8,128)(2,1)S(1)}, u32[]{:S(2)}, u32[]{:S(2)}) collective-permute-start(bf16[3,72,128]{2,1,0:T(8,128)(2,1)S(1)} %get-tuple-element.123), channel_id=1, source_target_pairs={{0,2},{1,3},{2,0},{3,1},{4,6},{5,7},{6,4},{7,5},{8,10},{9,11},{10,... | collective-permute-start | bytes 165896 | tf_op jit(solution)/shard_map/ppermute | solution.py:488
  95.1 1.8 %collective-permute-done.25.refs_7_ = bf16[6,72,128]{2,1,0:T(8,128)(2,1)S(1)} collective-permute-done((bf16[6,72,128]{2,1,0:T(8,128)(2,1)S(1)}, bf16[6,72,128]{2,1,0:T(8,128)(2,1)S(1)}, u32[]{:S(2)}, u32[]{:S(2)}) %collective-permute-start.25) | collective-permute-done | bytes 110624 | tf_op jit(solution)/shard_map/ppermute | solution.py:548
  97.0 1.7 %collective-permute-done.21.refs_2_ = bf16[3,72,128]{2,1,0:T(8,128)(2,1)S(1)} collective-permute-done((bf16[3,72,128]{2,1,0:T(8,128)(2,1)S(1)}, bf16[3,72,128]{2,1,0:T(8,128)(2,1)S(1)}, u32[]{:S(2)}, u32[]{:S(2)}) %collective-permute-start.21) | collective-permute-done | bytes 55328 | tf_op jit(solution)/shard_map/ppermute | solution.py:488
  98.6 1.7 %collective-permute-done.22.refs_3_ = bf16[3,72,128]{2,1,0:T(8,128)(2,1)S(1)} collective-permute-done((bf16[3,72,128]{2,1,0:T(8,128)(2,1)S(1)}, bf16[3,72,128]{2,1,0:T(8,128)(2,1)S(1)}, u32[]{:S(2)}, u32[]{:S(2)}) %collective-permute-start.22) | collective-permute-done | bytes 55328 | tf_op jit(solution)/shard_map/ppermute | solution.py:488
  100.4 0.7 shard_map.154
  101.1 6.8 %all-to-all-start = ((bf16[8,72,128]{2,1,0:T(8,128)(2,1)}), bf16[8,72,128]{2,1,0:T(8,128)(2,1)S(1)}, u32[]{:S(2)}, u32[]{:S(2)}) async-start(bf16[8,72,128]{2,1,0:T(8,128)(2,1)} %shard_map.154), calls=%async_computation | async-start | bytes 294912 | tf_op jit(solution)/shard_map/all_to_all | solution.py:665
  108.0 1.2 shard_map.146
  109.1 8.1 %all-to-all-done.parts = bf16[8,72,128]{2,1,0:T(8,128)(2,1)S(1)} async-done(((bf16[8,72,128]{2,1,0:T(8,128)(2,1)}), bf16[8,72,128]{2,1,0:T(8,128)(2,1)S(1)}, u32[]{:S(2)}, u32[]{:S(2)}) %all-to-all-start) | async-done | bytes 147488 | tf_op jit(solution)/shard_map/all_to_all | solution.py:665
  117.2 0.6 slice_bitcast_fusion
  (47 shorter events, 1.6 us)
Async XLA Ops:
  1.3 0.9 copy-start.6
  2.2 0.7 copy-start.10
  2.9 8.4 %copy-start.3 = (bf16[400,800]{1,0:T(8,128)(2,1)S(1)}, bf16[400,800]{1,0:T(8,128)(2,1)}, u32[]{:S(2)}) copy-start(bf16[400,800]{1,0:T(8,128)(2,1)} %w_up.3) | copy-start | bytes 1920004
  2.9 8.4 %copy-start.7 = (bf16[1,2,16,3200]{3,2,1,0:T(8,128)(2,1)S(1)}, bf16[1,2,16,3200]{3,2,1,0:T(8,128)(2,1)}, u32[]{:S(2)}) copy-start(bf16[1,2,16,3200]{3,2,1,0:T(8,128)(2,1)} %param.25) | copy-start | bytes 614404
  3.4 9.6 %collective-permute-start = (bf16[2,3,16,200]{3,2,1,0:T(8,128)(2,1)S(1)}, bf16[2,3,16,200]{3,2,1,0:T(8,128)(2,1)S(1)}, u32[]{:S(2)}, u32[]{:S(2)}) collective-permute-start(bf16[2,3,16,200]{3,2,1,0:T(8,128)(2,1)S(1)} %get-tuple-element.67.east), channel_id=1, source_target_pairs={{0,8},{8,16},{16,24},{24,32},{32,40},{40,48},{48,56},{56,64},{64,7... | collective-permute-start | bytes 115208 | tf_op jit(solution)/shard_map/ppermute | solution.py:488
  3.5 9.6 %collective-permute-start.1 = (bf16[2,3,16,200]{3,2,1,0:T(8,128)(2,1)S(1)}, bf16[2,3,16,200]{3,2,1,0:T(8,128)(2,1)S(1)}, u32[]{:S(2)}, u32[]{:S(2)}) collective-permute-start(bf16[2,3,16,200]{3,2,1,0:T(8,128)(2,1)S(1)} %get-tuple-element.66.west), channel_id=1, source_target_pairs={{0,248},{8,0},{16,8},{24,16},{32,24},{40,32},{48,40},{56,48},{64,5... | collective-permute-start | bytes 115208 | tf_op jit(solution)/shard_map/ppermute | solution.py:488
  11.3 1.7 %copy-start.11 = (s32[1,2,4]{2,1,0:T(2,128)S(1)}, s32[1,2,4]{2,1,0:T(2,128)}, u32[]{:S(2)}) copy-start(s32[1,2,4]{2,1,0:T(2,128)} %param.16) | copy-start | bytes 100
  13.1 7.2 %copy-start.2 = (bf16[800,400]{0,1:T(8,128)(2,1)S(1)}, bf16[800,400]{0,1:T(8,128)(2,1)}, u32[]{:S(2)}) copy-start(bf16[800,400]{0,1:T(8,128)(2,1)} %param.20) | copy-start | bytes 1920004
  13.1 7.2 %copy-start.4 = (bf16[200,800]{1,0:T(8,128)(2,1)S(1)}, bf16[200,800]{1,0:T(8,128)(2,1)}, u32[]{:S(2)}) copy-start(bf16[200,800]{1,0:T(8,128)(2,1)} %w_in.5) | copy-start | bytes 960004
  13.1 7.2 %copy-start.5 = (bf16[800,200]{0,1:T(8,128)(2,1)S(1)}, bf16[800,200]{0,1:T(8,128)(2,1)}, u32[]{:S(2)}) copy-start(bf16[800,200]{0,1:T(8,128)(2,1)} %param.19) | copy-start | bytes 960004
  13.1 7.2 %copy-start.9 = (bf16[7,7,200]{2,1,0:T(8,128)(2,1)S(1)}, bf16[7,7,200]{2,1,0:T(8,128)(2,1)}, u32[]{:S(2)}) copy-start(bf16[7,7,200]{2,1,0:T(8,128)(2,1)} %kern.3) | copy-start | bytes 58804
  13.8 4.1 %collective-permute-start.2 = (bf16[22,3,200]{2,1,0:T(4,128)(2,1)S(1)}, bf16[22,3,200]{2,1,0:T(4,128)(2,1)S(1)}, u32[]{:S(2)}, u32[]{:S(2)}) collective-permute-start(bf16[22,3,200]{2,1,0:T(4,128)(2,1)S(1)} %get-tuple-element.69), channel_id=1, source_target_pairs={{0,1},{1,2},{2,3},{3,4},{4,5},{5,6},{6,7},{7,0},{8,9},{9,10},{10,1... | collective-permute-start | bytes 79208 | tf_op jit(solution)/shard_map/ppermute | solution.py:488
  14.2 6.2 %collective-permute-start.3 = (bf16[22,3,200]{2,1,0:T(4,128)(2,1)S(1)}, bf16[22,3,200]{2,1,0:T(4,128)(2,1)S(1)}, u32[]{:S(2)}, u32[]{:S(2)}) collective-permute-start(bf16[22,3,200]{2,1,0:T(4,128)(2,1)S(1)} %get-tuple-element.70), channel_id=1, source_target_pairs={{0,7},{1,0},{2,1},{3,2},{4,3},{5,4},{6,5},{7,6},{8,15},{9,8},{10,9... | collective-permute-start | bytes 79208 | tf_op jit(solution)/shard_map/ppermute | solution.py:488
  24.9 7.3 %collective-permute-start.4 = (bf16[2,3,8,400]{3,2,1,0:T(8,128)(2,1)S(1)}, bf16[2,3,8,400]{3,2,1,0:T(8,128)(2,1)S(1)}, u32[]{:S(2)}, u32[]{:S(2)}) collective-permute-start(bf16[2,3,8,400]{3,2,1,0:T(8,128)(2,1)S(1)} %get-tuple-element.76.east), channel_id=1, source_target_pairs={{0,8},{8,16},{16,24},{24,32},{32,40},{40,48},{48,56},{56,64},{64,7... | collective-permute-start | bytes 115208 | tf_op jit(solution)/shard_map/ppermute | solution.py:488
  25.0 7.2 %collective-permute-start.5 = (bf16[2,3,8,400]{3,2,1,0:T(8,128)(2,1)S(1)}, bf16[2,3,8,400]{3,2,1,0:T(8,128)(2,1)S(1)}, u32[]{:S(2)}, u32[]{:S(2)}) collective-permute-start(bf16[2,3,8,400]{3,2,1,0:T(8,128)(2,1)S(1)} %get-tuple-element.75.west), channel_id=1, source_target_pairs={{0,248},{8,0},{16,8},{24,16},{32,24},{40,32},{48,40},{56,48},{64,5... | collective-permute-start | bytes 115208 | tf_op jit(solution)/shard_map/ppermute | solution.py:488
  32.2 7.2 %copy-start = (bf16[400,1600]{1,0:T(8,128)(2,1)S(1)}, bf16[400,1600]{1,0:T(8,128)(2,1)}, u32[]{:S(2)}) copy-start(bf16[400,1600]{1,0:T(8,128)(2,1)} %w_in.4) | copy-start | bytes 3840004
  32.2 7.2 %copy-start.1 = (bf16[1600,400]{0,1:T(8,128)(2,1)S(1)}, bf16[1600,400]{0,1:T(8,128)(2,1)}, u32[]{:S(2)}) copy-start(bf16[1600,400]{0,1:T(8,128)(2,1)} %param.23) | copy-start | bytes 3840004
  32.2 7.2 %copy-start.8 = (bf16[7,7,400]{2,1,0:T(8,128)(2,1)S(1)}, bf16[7,7,400]{2,1,0:T(8,128)(2,1)}, u32[]{:S(2)}) copy-start(bf16[7,7,400]{2,1,0:T(8,128)(2,1)} %kern.5) | copy-start | bytes 117604
  33.0 4.3 %collective-permute-start.6 = (bf16[14,3,400]{2,1,0:T(4,128)(2,1)S(1)}, bf16[14,3,400]{2,1,0:T(4,128)(2,1)S(1)}, u32[]{:S(2)}, u32[]{:S(2)}) collective-permute-start(bf16[14,3,400]{2,1,0:T(4,128)(2,1)S(1)} %get-tuple-element.78), channel_id=1, source_target_pairs={{0,1},{1,2},{2,3},{3,4},{4,5},{5,6},{6,7},{7,0},{8,9},{9,10},{10,1... | collective-permute-start | bytes 100808 | tf_op jit(solution)/shard_map/ppermute | solution.py:488
  33.0 6.4 %collective-permute-start.7 = (bf16[14,3,400]{2,1,0:T(4,128)(2,1)S(1)}, bf16[14,3,400]{2,1,0:T(4,128)(2,1)S(1)}, u32[]{:S(2)}, u32[]{:S(2)}) collective-permute-start(bf16[14,3,400]{2,1,0:T(4,128)(2,1)S(1)} %get-tuple-element.79), channel_id=1, source_target_pairs={{0,7},{1,0},{2,1},{3,2},{4,3},{5,4},{6,5},{7,6},{8,15},{9,8},{10,9... | collective-permute-start | bytes 100808 | tf_op jit(solution)/shard_map/ppermute | solution.py:488
  43.4 9.2 %collective-permute-start.8 = (bf16[2,3,8,400]{3,2,1,0:T(8,128)(2,1)S(1)}, bf16[2,3,8,400]{3,2,1,0:T(8,128)(2,1)S(1)}, u32[]{:S(2)}, u32[]{:S(2)}) collective-permute-start(bf16[2,3,8,400]{3,2,1,0:T(8,128)(2,1)S(1)} %get-tuple-element.84.east), channel_id=1, source_target_pairs={{0,8},{8,16},{16,24},{24,32},{32,40},{40,48},{48,56},{56,64},{64,7... | collective-permute-start | bytes 115208 | tf_op jit(solution)/shard_map/ppermute | solution.py:488
  43.6 9.0 %collective-permute-start.9 = (bf16[2,3,8,400]{3,2,1,0:T(8,128)(2,1)S(1)}, bf16[2,3,8,400]{3,2,1,0:T(8,128)(2,1)S(1)}, u32[]{:S(2)}, u32[]{:S(2)}) collective-permute-start(bf16[2,3,8,400]{3,2,1,0:T(8,128)(2,1)S(1)} %get-tuple-element.83.west), channel_id=1, source_target_pairs={{0,248},{8,0},{16,8},{24,16},{32,24},{40,32},{48,40},{56,48},{64,5... | collective-permute-start | bytes 115208 | tf_op jit(solution)/shard_map/ppermute | solution.py:488
  52.6 3.8 %collective-permute-start.12 = (bf16[16,6,72,128]{3,2,1,0:T(8,128)(2,1)S(1)}, bf16[16,6,72,128]{3,2,1,0:T(8,128)(2,1)S(1)}, u32[]{:S(2)}, u32[]{:S(2)}) collective-permute-start(bf16[16,6,72,128]{3,2,1,0:T(8,128)(2,1)S(1)} %get-tuple-element.97), channel_id=1, source_target_pairs={{0,8},{8,0},{1,9},{9,1},{2,10},{10,2},{3,11},{11,3},{4,12},{12,4},... | collective-permute-start | bytes 5308424 | tf_op jit(solution)/shard_map/ppermute | solution.py:499
  53.5 4.4 %collective-permute-start.10 = (bf16[14,3,400]{2,1,0:T(4,128)(2,1)S(1)}, bf16[14,3,400]{2,1,0:T(4,128)(2,1)S(1)}, u32[]{:S(2)}, u32[]{:S(2)}) collective-permute-start(bf16[14,3,400]{2,1,0:T(4,128)(2,1)S(1)} %get-tuple-element.94), channel_id=1, source_target_pairs={{0,1},{1,2},{2,3},{3,4},{4,5},{5,6},{6,7},{7,0},{8,9},{9,10},{10,1... | collective-permute-start | bytes 100808 | tf_op jit(solution)/shard_map/ppermute | solution.py:488
  53.6 6.5 %collective-permute-start.11 = (bf16[14,3,400]{2,1,0:T(4,128)(2,1)S(1)}, bf16[14,3,400]{2,1,0:T(4,128)(2,1)S(1)}, u32[]{:S(2)}, u32[]{:S(2)}) collective-permute-start(bf16[14,3,400]{2,1,0:T(4,128)(2,1)S(1)} %get-tuple-element.95), channel_id=1, source_target_pairs={{0,7},{1,0},{2,1},{3,2},{4,3},{5,4},{6,5},{7,6},{8,15},{9,8},{10,9... | collective-permute-start | bytes 100808 | tf_op jit(solution)/shard_map/ppermute | solution.py:488
  60.1 11.8 %collective-permute-start.13 = (bf16[4,6,72,128]{3,2,1,0:T(8,128)(2,1)S(1)}, bf16[4,6,72,128]{3,2,1,0:T(8,128)(2,1)S(1)}, u32[]{:S(2)}, u32[]{:S(2)}) collective-permute-start(bf16[4,6,72,128]{3,2,1,0:T(8,128)(2,1)S(1)} %get-tuple-element.108), channel_id=1, source_target_pairs={{0,1},{1,2},{2,3},{3,0},{4,5},{5,6},{6,7},{7,4},{8,9},{9,10},{10,1... | collective-permute-start | bytes 1327112 | tf_op jit(solution)/shard_map/ppermute | solution.py:488
  60.1 12.9 %collective-permute-start.14 = (bf16[4,6,72,128]{3,2,1,0:T(8,128)(2,1)S(1)}, bf16[4,6,72,128]{3,2,1,0:T(8,128)(2,1)S(1)}, u32[]{:S(2)}, u32[]{:S(2)}) collective-permute-start(bf16[4,6,72,128]{3,2,1,0:T(8,128)(2,1)S(1)} %get-tuple-element.109), channel_id=1, source_target_pairs={{0,3},{1,0},{2,1},{3,2},{4,7},{5,4},{6,5},{7,6},{8,11},{9,8},{10,9... | collective-permute-start | bytes 1327112 | tf_op jit(solution)/shard_map/ppermute | solution.py:488
  73.1 2.4 %collective-permute-start.15 = (bf16[16,3,72,128]{3,2,1,0:T(8,128)(2,1)S(1)}, bf16[16,3,72,128]{3,2,1,0:T(8,128)(2,1)S(1)}, u32[]{:S(2)}, u32[]{:S(2)}) collective-permute-start(bf16[16,3,72,128]{3,2,1,0:T(8,128)(2,1)S(1)} %get-tuple-element.110), channel_id=1, source_target_pairs={{0,8},{8,0},{1,9},{9,1},{2,10},{10,2},{3,11},{11,3},{4,12},{12,4},... | collective-permute-start | bytes 2654216 | tf_op jit(solution)/shard_map/ppermute | solution.py:499
  73.1 14.1 %collective-permute-start.17 = (bf16[4,6,72,128]{3,2,1,0:T(8,128)(2,1)S(1)}, bf16[4,6,72,128]{3,2,1,0:T(8,128)(2,1)S(1)}, u32[]{:S(2)}, u32[]{:S(2)}) collective-permute-start(bf16[4,6,72,128]{3,2,1,0:T(8,128)(2,1)S(1)} %get-tuple-element.115), channel_id=1, source_target_pairs={{0,2},{1,3},{2,0},{3,1},{4,6},{5,7},{6,4},{7,5},{8,10},{9,11},{10,... | collective-permute-start | bytes 1327112 | tf_op jit(solution)/shard_map/ppermute | solution.py:488
  75.7 13.1 %collective-permute-start.16 = (bf16[4,3,72,128]{3,2,1,0:T(8,128)(2,1)S(1)}, bf16[4,3,72,128]{3,2,1,0:T(8,128)(2,1)S(1)}, u32[]{:S(2)}, u32[]{:S(2)}) collective-permute-start(bf16[4,3,72,128]{3,2,1,0:T(8,128)(2,1)S(1)} %get-tuple-element.112), channel_id=1, source_target_pairs={{0,4},{4,0},{16,20},{20,16},{1,5},{5,1},{17,21},{21,17},{2,6},{6,2... | collective-permute-start | bytes 663560 | tf_op jit(solution)/shard_map/ppermute | solution.py:548
  77.1 15.1 %collective-permute-start.18 = (bf16[4,3,72,128]{3,2,1,0:T(8,128)(2,1)S(1)}, bf16[4,3,72,128]{3,2,1,0:T(8,128)(2,1)S(1)}, u32[]{:S(2)}, u32[]{:S(2)}) collective-permute-start(bf16[4,3,72,128]{3,2,1,0:T(8,128)(2,1)S(1)} %get-tuple-element.119), channel_id=1, source_target_pairs={{0,16},{4,20},{16,0},{20,4},{1,17},{5,21},{17,1},{21,5},{2,18},{6,... | collective-permute-start | bytes 663560 | tf_op jit(solution)/shard_map/ppermute | solution.py:548
  77.1 15.1 %collective-permute-start.19 = (bf16[4,3,72,128]{3,2,1,0:T(8,128)(2,1)S(1)}, bf16[4,3,72,128]{3,2,1,0:T(8,128)(2,1)S(1)}, u32[]{:S(2)}, u32[]{:S(2)}) collective-permute-start(bf16[4,3,72,128]{3,2,1,0:T(8,128)(2,1)S(1)} %get-tuple-element.120), channel_id=1, source_target_pairs={{0,20},{4,16},{16,4},{20,0},{1,21},{5,17},{17,5},{21,1},{2,22},{6,... | collective-permute-start | bytes 663560 | tf_op jit(solution)/shard_map/ppermute | solution.py:548
  87.4 7.6 %collective-permute-start.23 = (bf16[6,72,128]{2,1,0:T(8,128)(2,1)S(1)}, bf16[6,72,128]{2,1,0:T(8,128)(2,1)S(1)}, u32[]{:S(2)}, u32[]{:S(2)}) collective-permute-start(bf16[6,72,128]{2,1,0:T(8,128)(2,1)S(1)} %get-tuple-element.117), channel_id=1, source_target_pairs={{0,4},{4,0},{16,20},{20,16},{1,5},{5,1},{17,21},{21,17},{2,6},{6,2... | collective-permute-start | bytes 331784 | tf_op jit(solution)/shard_map/ppermute | solution.py:548
  88.8 6.3 %collective-permute-start.24 = (bf16[6,72,128]{2,1,0:T(8,128)(2,1)S(1)}, bf16[6,72,128]{2,1,0:T(8,128)(2,1)S(1)}, u32[]{:S(2)}, u32[]{:S(2)}) collective-permute-start(bf16[6,72,128]{2,1,0:T(8,128)(2,1)S(1)} %get-tuple-element.126), channel_id=1, source_target_pairs={{0,16},{4,20},{16,0},{20,4},{1,17},{5,21},{17,1},{21,5},{2,18},{6,... | collective-permute-start | bytes 331784 | tf_op jit(solution)/shard_map/ppermute | solution.py:548
  88.8 8.1 %collective-permute-start.25 = (bf16[6,72,128]{2,1,0:T(8,128)(2,1)S(1)}, bf16[6,72,128]{2,1,0:T(8,128)(2,1)S(1)}, u32[]{:S(2)}, u32[]{:S(2)}) collective-permute-start(bf16[6,72,128]{2,1,0:T(8,128)(2,1)S(1)} %get-tuple-element.127), channel_id=1, source_target_pairs={{0,20},{4,16},{16,4},{20,0},{1,21},{5,17},{17,5},{21,1},{2,22},{6,... | collective-permute-start | bytes 331784 | tf_op jit(solution)/shard_map/ppermute | solution.py:548
  92.3 4.6 %collective-permute-start.20 = (bf16[3,72,128]{2,1,0:T(8,128)(2,1)S(1)}, bf16[3,72,128]{2,1,0:T(8,128)(2,1)S(1)}, u32[]{:S(2)}, u32[]{:S(2)}) collective-permute-start(bf16[3,72,128]{2,1,0:T(8,128)(2,1)S(1)} %get-tuple-element.122), channel_id=1, source_target_pairs={{0,1},{1,2},{2,3},{3,0},{4,5},{5,6},{6,7},{7,4},{8,9},{9,10},{10,1... | collective-permute-start | bytes 165896 | tf_op jit(solution)/shard_map/ppermute | solution.py:488
  92.7 6.0 %collective-permute-start.21 = (bf16[3,72,128]{2,1,0:T(8,128)(2,1)S(1)}, bf16[3,72,128]{2,1,0:T(8,128)(2,1)S(1)}, u32[]{:S(2)}, u32[]{:S(2)}) collective-permute-start(bf16[3,72,128]{2,1,0:T(8,128)(2,1)S(1)} %get-tuple-element.123), channel_id=1, source_target_pairs={{0,2},{1,3},{2,0},{3,1},{4,6},{5,7},{6,4},{7,5},{8,10},{9,11},{10,... | collective-permute-start | bytes 165896 | tf_op jit(solution)/shard_map/ppermute | solution.py:488
  95.0 5.4 %collective-permute-start.22 = (bf16[3,72,128]{2,1,0:T(8,128)(2,1)S(1)}, bf16[3,72,128]{2,1,0:T(8,128)(2,1)S(1)}, u32[]{:S(2)}, u32[]{:S(2)}) collective-permute-start(bf16[3,72,128]{2,1,0:T(8,128)(2,1)S(1)} %get-tuple-element.124), channel_id=1, source_target_pairs={{0,3},{1,0},{2,1},{3,2},{4,7},{5,4},{6,5},{7,6},{8,11},{9,8},{10,9... | collective-permute-start | bytes 165896 | tf_op jit(solution)/shard_map/ppermute | solution.py:488
  101.1 16.1 %all-to-all-start = ((bf16[8,72,128]{2,1,0:T(8,128)(2,1)}), bf16[8,72,128]{2,1,0:T(8,128)(2,1)S(1)}, u32[]{:S(2)}, u32[]{:S(2)}) async-start(bf16[8,72,128]{2,1,0:T(8,128)(2,1)} %shard_map.154), calls=%async_computation | async-start | bytes 294912 | tf_op jit(solution)/shard_map/all_to_all | solution.py:665
where the time goes:
time: 118 us
  starting transfers between devices  47.3 us (40%)
  waiting for transfers between devices  40.1 us (34%)
  Pallas kernels  26.7 us (23%)
  local copies, waits for them, and re-layouts  2.26 us (2%)
  between operations  1.5 us (1%)
    ppermute x18, starting transfers between devices, around(): lax.ppermute(array, axes, [(i, (i + step) % size) for i in range(size)])  30.8 us
    ppermute x18, waiting for transfers between devices, around(): lax.ppermute(array, axes, [(i, (i + step) % size) for i in range(size)])  27.7 us
    pallas_call x16, Pallas kernels, run(): pl.pallas_call(body, out_shape=[jax.ShapeDtypeStruct(shape, kind) for sha...  26.7 us
    ppermute x6, starting transfers between devices, over_x(): lax.ppermute(parts[k], ('xh', 'xl'), [(i, i ^ k) for i in range(4)])  9.57 us
    all_to_all x1, waiting for transfers between devices, finish(): total = lax.all_to_all(total, 'z', 0, 0)  8.1 us
    all_to_all x1, starting transfers between devices, finish(): total = lax.all_to_all(total, 'z', 0, 0)  6.85 us
    ppermute x2, waiting for transfers between devices, other_core(): return lax.ppermute(send, 'c', [(0, 1), (1, 0)])  2.39 us
  transfers between devices with their start and end apart: 27, of which 19 were waited for; matrix products, arithmetic and copies ran while one was open for 0% of the time, Pallas kernels for 13%

commit v1 on v0

--- a/solution.py
+++ b/solution.py
@@ -627,7 +627,6 @@
     field, top, bottom = strips_two(back, west, west_got, east, east_got)
     top_got, bottom_got = around(bottom, LAT, 1), around(top, LAT, -1)
     parts = list(call(y_parts_kernel, [((4, 6, HELD, LANES), BF16)] * 4)(keep_two, got_two))
-    top_got, bottom_got, *parts[1:] = lax.optimization_barrier((top_got, bottom_got, *parts[1:]))
     parts_two = over_y(parts)
     sides = field, top_got, bottom_got
     keep_one, send_one = call(

time: 118 us -> 115 us (0.975)
  waiting for transfers between devices: 40.1 us -> 38.7 us
  starting transfers between devices: 47.3 us -> 46 us
    ppermute x18, waiting for transfers between devices: 27.7 us -> 25.3 us  [around(): lax.ppermute(array, axes, [(i, (i + step) % size) for i in range(size)])]
    ppermute x18, starting transfers between devices: 30.8 us -> 29.5 us  [around(): lax.ppermute(array, axes, [(i, (i + step) % size) for i in range(size)])]
where the time goes in v1:
time: 115 us
  starting transfers between devices  46 us (40%)
  waiting for transfers between devices  38.7 us (34%)
  Pallas kernels  26.7 us (23%)
  local copies, waits for them, and re-layouts  2.26 us (2%)
  between operations  1.5 us (1%)
    ppermute x18, starting transfers between devices, around(): lax.ppermute(array, axes, [(i, (i + step) % size) for i in range(size)])  29.5 us
    pallas_call x16, Pallas kernels, run(): pl.pallas_call(body, out_shape=[jax.ShapeDtypeStruct(shape, kind) for sha...  26.7 us
    ppermute x18, waiting for transfers between devices, around(): lax.ppermute(array, axes, [(i, (i + step) % size) for i in range(size)])  25.3 us
    ppermute x6, starting transfers between devices, over_x(): lax.ppermute(parts[k], ('xh', 'xl'), [(i, i ^ k) for i in range(4)])  9.57 us
    all_to_all x1, waiting for transfers between devices, finish(): total = lax.all_to_all(total, 'z', 0, 0)  8.1 us
    all_to_all x1, starting transfers between devices, finish(): total = lax.all_to_all(total, 'z', 0, 0)  6.85 us
    ppermute x2, waiting for transfers between devices, other_core(): return lax.ppermute(send, 'c', [(0, 1), (1, 0)])  3.25 us
  transfers between devices with their start and end apart: 27, of which 19 were waited for; matrix products, arithmetic and copies ran while one was open for 0% of the time, Pallas kernels for 13%

profile of v1, /device:TPU:24, one launch (start us, length us, event | category | flops | bytes accessed | tf_op | source)
XLA Modules:
  0.0 115.1 jit_solution(6201939040736692068)
XLA Ops:
  1.3 0.9 copy-done.6
  2.2 0.7 copy-done.10
  2.9 0.5 shard_map.141
  3.5 7.8 %collective-permute-start.1 = (bf16[2,3,16,200]{3,2,1,0:T(8,128)(2,1)S(1)}, bf16[2,3,16,200]{3,2,1,0:T(8,128)(2,1)S(1)}, u32[]{:S(2)}, u32[]{:S(2)}) collective-permute-start(bf16[2,3,16,200]{3,2,1,0:T(8,128)(2,1)S(1)} %get-tuple-element.61.west), channel_id=1, source_target_pairs={{0,248},{8,0},{16,8},{24,16},{32,24},{40,32},{48,40},{56,48},{64,5... | collective-permute-start | bytes 115208 | tf_op jit(solution)/shard_map/ppermute | solution.py:488
  11.3 1.0 shard_map.140
  12.3 0.7 collective-permute-done.west_got
  13.1 0.7 shard_map.142
  13.8 0.3 collective-permute-start.2
  14.2 1.8 %collective-permute-start.3 = (bf16[22,3,200]{2,1,0:T(4,128)(2,1)S(1)}, bf16[22,3,200]{2,1,0:T(4,128)(2,1)S(1)}, u32[]{:S(2)}, u32[]{:S(2)}) collective-permute-start(bf16[22,3,200]{2,1,0:T(4,128)(2,1)S(1)} %get-tuple-element.65), channel_id=1, source_target_pairs={{0,7},{1,0},{2,1},{3,2},{4,3},{5,4},{6,5},{7,6},{8,15},{9,8},{10,9... | collective-permute-start | bytes 79208 | tf_op jit(solution)/shard_map/ppermute | solution.py:488
  15.9 2.0 %collective-permute-done.2.top_got = bf16[22,3,200]{2,1,0:T(4,128)(2,1)S(1)} collective-permute-done((bf16[22,3,200]{2,1,0:T(4,128)(2,1)S(1)}, bf16[22,3,200]{2,1,0:T(4,128)(2,1)S(1)}, u32[]{:S(2)}, u32[]{:S(2)}) %collective-permute-start.2) | collective-permute-done | bytes 26432 | tf_op jit(solution)/shard_map/ppermute | solution.py:488
  18.0 2.4 %collective-permute-done.3.bottom_got = bf16[22,3,200]{2,1,0:T(4,128)(2,1)S(1)} collective-permute-done((bf16[22,3,200]{2,1,0:T(4,128)(2,1)S(1)}, bf16[22,3,200]{2,1,0:T(4,128)(2,1)S(1)}, u32[]{:S(2)}, u32[]{:S(2)}) %collective-permute-start.3) | collective-permute-done | bytes 26432 | tf_op jit(solution)/shard_map/ppermute | solution.py:488
  20.3 4.5 %shard_map.143 = (f32[2,2,22,24,128]{4,3,2,1,0:T(8,128)S(1)}, f32[512,256]{1,0:T(8,128)S(1)}, f32[512,128]{1,0:T(8,128)S(1)}, bf16[128,800]{1,0:T(8,128)(2,1)S(1...) custom-call(s32[2,4]{1,0:T(2,128)S(1)} %bitcast.21, ...), custom_call_target="tpu_custom_call" | custom-call | flops 6000000000 | bytes 1000000 | tf_op jit(solution)/shard_map/pallas_call | solution.py:32
  25.0 5.3 %collective-permute-start.5 = (bf16[2,3,8,400]{3,2,1,0:T(8,128)(2,1)S(1)}, bf16[2,3,8,400]{3,2,1,0:T(8,128)(2,1)S(1)}, u32[]{:S(2)}, u32[]{:S(2)}) collective-permute-start(bf16[2,3,8,400]{3,2,1,0:T(8,128)(2,1)S(1)} %get-tuple-element.70.west), channel_id=1, source_target_pairs={{0,248},{8,0},{16,8},{24,16},{32,24},{40,32},{48,40},{56,48},{64,5... | collective-permute-start | bytes 115208 | tf_op jit(solution)/shard_map/ppermute | solution.py:488
  30.3 1.9 %collective-permute-done.4.west_got = bf16[2,3,8,400]{3,2,1,0:T(8,128)(2,1)S(1)} collective-permute-done((bf16[2,3,8,400]{3,2,1,0:T(8,128)(2,1)S(1)}, bf16[2,3,8,400]{3,2,1,0:T(8,128)(2,1)S(1)}, u32[]{:S(2)}, u32[]{:S(2)}) %collective-permute-start.4) | collective-permute-done | bytes 38432 | tf_op jit(solution)/shard_map/ppermute | solution.py:488
  32.2 0.7 shard_map.144
  33.0 2.0 %collective-permute-start.7 = (bf16[14,3,400]{2,1,0:T(4,128)(2,1)S(1)}, bf16[14,3,400]{2,1,0:T(4,128)(2,1)S(1)}, u32[]{:S(2)}, u32[]{:S(2)}) collective-permute-start(bf16[14,3,400]{2,1,0:T(4,128)(2,1)S(1)} %get-tuple-element.74), channel_id=1, source_target_pairs={{0,7},{1,0},{2,1},{3,2},{4,3},{5,4},{6,5},{7,6},{8,15},{9,8},{10,9... | collective-permute-start | bytes 100808 | tf_op jit(solution)/shard_map/ppermute | solution.py:488
  35.1 2.2 %collective-permute-done.6.top_got = bf16[14,3,400]{2,1,0:T(4,128)(2,1)S(1)} collective-permute-done((bf16[14,3,400]{2,1,0:T(4,128)(2,1)S(1)}, bf16[14,3,400]{2,1,0:T(4,128)(2,1)S(1)}, u32[]{:S(2)}, u32[]{:S(2)}) %collective-permute-start.6) | collective-permute-done | bytes 33632 | tf_op jit(solution)/shard_map/ppermute | solution.py:488
  37.2 2.2 %collective-permute-done.7.bottom_got = bf16[14,3,400]{2,1,0:T(4,128)(2,1)S(1)} collective-permute-done((bf16[14,3,400]{2,1,0:T(4,128)(2,1)S(1)}, bf16[14,3,400]{2,1,0:T(4,128)(2,1)S(1)}, u32[]{:S(2)}, u32[]{:S(2)}) %collective-permute-start.7) | collective-permute-done | bytes 33632 | tf_op jit(solution)/shard_map/ppermute | solution.py:488
  39.4 3.9 %shard_map.145 = (f32[2,4,14,16,128]{4,3,2,1,0:T(8,128)S(1)}, bf16[128,400]{1,0:T(8,128)(2,1)S(1)}, bf16[128,1600]{1,0:T(8,128)(2,1)S(1)}, bf16[128,1600]{1,0:T(...) custom-call(s32[2,4]{1,0:T(2,128)S(1)} %bitcast.23, ...), custom_call_target="tpu_custom_call" | custom-call | flops 6000000000 | bytes 1000000 | tf_op jit(solution)/shard_map/pallas_call | solution.py:32
  43.6 5.3 %collective-permute-start.9 = (bf16[2,3,8,400]{3,2,1,0:T(8,128)(2,1)S(1)}, bf16[2,3,8,400]{3,2,1,0:T(8,128)(2,1)S(1)}, u32[]{:S(2)}, u32[]{:S(2)}) collective-permute-start(bf16[2,3,8,400]{3,2,1,0:T(8,128)(2,1)S(1)} %get-tuple-element.78.west), channel_id=1, source_target_pairs={{0,248},{8,0},{16,8},{24,16},{32,24},{40,32},{48,40},{56,48},{64,5... | collective-permute-start | bytes 115208 | tf_op jit(solution)/shard_map/ppermute | solution.py:488
  49.0 3.6 %shard_map.147 = (bf16[16,6,72,128]{3,2,1,0:T(8,128)(2,1)S(1)}, bf16[16,6,72,128]{3,2,1,0:T(8,128)(2,1)S(1)}) custom-call(f32[2,4,14,16,128]{4,3,2,1,0:T(8,128)S(1)} %get-tuple-element.80.field, bf16[128,400]{1,0:T(8,128)(2,1)S(1)} %get-tuple-element.77.back.rows, bf16[128,400]{1,0:T(8,128)(2,1)S(1)} %get-tuple-element.81.normed_b, ...), custom_call_target="tpu_custom_call" | custom-call | flops 7000000000 | bytes 1000000 | tf_op jit(solution)/shard_map/pallas_call | solution.py:32
  52.7 0.7 shard_map.148
  53.6 2.0 %collective-permute-start.11 = (bf16[14,3,400]{2,1,0:T(4,128)(2,1)S(1)}, bf16[14,3,400]{2,1,0:T(4,128)(2,1)S(1)}, u32[]{:S(2)}, u32[]{:S(2)}) collective-permute-start(bf16[14,3,400]{2,1,0:T(4,128)(2,1)S(1)} %get-tuple-element.90), channel_id=1, source_target_pairs={{0,7},{1,0},{2,1},{3,2},{4,3},{5,4},{6,5},{7,6},{8,15},{9,8},{10,9... | collective-permute-start | bytes 100808 | tf_op jit(solution)/shard_map/ppermute | solution.py:488
  55.6 0.8 collective-permute-done.12.got
  56.4 0.4 shard_map.150
  56.8 1.3 %collective-permute-start.13 = (bf16[4,6,72,128]{3,2,1,0:T(8,128)(2,1)S(1)}, bf16[4,6,72,128]{3,2,1,0:T(8,128)(2,1)S(1)}, u32[]{:S(2)}, u32[]{:S(2)}) collective-permute-start(bf16[4,6,72,128]{3,2,1,0:T(8,128)(2,1)S(1)} %get-tuple-element.98), channel_id=1, source_target_pairs={{0,1},{1,2},{2,3},{3,0},{4,5},{5,6},{6,7},{7,4},{8,9},{9,10},{10,1... | collective-permute-start | bytes 1327112 | tf_op jit(solution)/shard_map/ppermute | solution.py:488
  58.1 0.8 collective-permute-start.14
  58.9 1.1 collective-permute-done.11.bottom_got
  60.1 8.0 %shard_map.149 = (bf16[16,3,72,128]{3,2,1,0:T(8,128)(2,1)S(1)}, bf16[16,3,72,128]{3,2,1,0:T(8,128)(2,1)S(1)}) custom-call(s32[2,4]{1,0:T(2,128)S(1)} %bitcast.25, f32[2,4,14,16,128]{4,3,2,1,0:T(8,128)S(1)} %get-tuple-element.88.delta, bf16[14,3,400]{2,1,0:T(4,128)(2,1)S(1)} %collective-permute-done.10.top_got, ...), custom_call_target="tpu_custom_call" | custom-call | flops 10000000000 | bytes 1000000 | tf_op jit(solution)/shard_map/pallas_call | solution.py:32
  68.1 1.0 collective-permute-done.13.refs_1_
  69.1 2.3 %collective-permute-done.14.refs_3_ = bf16[4,6,72,128]{3,2,1,0:T(8,128)(2,1)S(1)} collective-permute-done((bf16[4,6,72,128]{3,2,1,0:T(8,128)(2,1)S(1)}, bf16[4,6,72,128]{3,2,1,0:T(8,128)(2,1)S(1)}, u32[]{:S(2)}, u32[]{:S(2)}) %collective-permute-start.14) | collective-permute-done | bytes 442400 | tf_op jit(solution)/shard_map/ppermute | solution.py:488
  71.4 2.4 %collective-permute-done.15.got = bf16[16,3,72,128]{3,2,1,0:T(8,128)(2,1)S(1)} collective-permute-done((bf16[16,3,72,128]{3,2,1,0:T(8,128)(2,1)S(1)}, bf16[16,3,72,128]{3,2,1,0:T(8,128)(2,1)S(1)}, u32[]{:S(2)}, u32[]{:S(2)}) %collective-permute-start.15) | collective-permute-done | bytes 884768 | tf_op jit(solution)/shard_map/ppermute | solution.py:499
  74.0 0.8 collective-permute-start.16
  74.8 4.0 %collective-permute-start.19 = (bf16[4,3,72,128]{3,2,1,0:T(8,128)(2,1)S(1)}, bf16[4,3,72,128]{3,2,1,0:T(8,128)(2,1)S(1)}, u32[]{:S(2)}, u32[]{:S(2)}) collective-permute-start(bf16[4,3,72,128]{3,2,1,0:T(8,128)(2,1)S(1)} %get-tuple-element.110), channel_id=1, source_target_pairs={{0,20},{4,16},{16,4},{20,0},{1,21},{5,17},{17,5},{21,1},{2,22},{6,... | collective-permute-start | bytes 663560 | tf_op jit(solution)/shard_map/ppermute | solution.py:548
  78.8 6.7 %collective-permute-done.17.refs_2_ = bf16[4,6,72,128]{3,2,1,0:T(8,128)(2,1)S(1)} collective-permute-done((bf16[4,6,72,128]{3,2,1,0:T(8,128)(2,1)S(1)}, bf16[4,6,72,128]{3,2,1,0:T(8,128)(2,1)S(1)}, u32[]{:S(2)}, u32[]{:S(2)}) %collective-permute-start.17) | collective-permute-done | bytes 442400 | tf_op jit(solution)/shard_map/ppermute | solution.py:488
  85.7 0.8 collective-permute-start.23
  86.5 4.0 %collective-permute-start.25 = (bf16[6,72,128]{2,1,0:T(8,128)(2,1)S(1)}, bf16[6,72,128]{2,1,0:T(8,128)(2,1)S(1)}, u32[]{:S(2)}, u32[]{:S(2)}) collective-permute-start(bf16[6,72,128]{2,1,0:T(8,128)(2,1)S(1)} %get-tuple-element.117), channel_id=1, source_target_pairs={{0,20},{4,16},{16,4},{20,0},{1,21},{5,17},{17,5},{21,1},{2,22},{6,... | collective-permute-start | bytes 331784 | tf_op jit(solution)/shard_map/ppermute | solution.py:548
  90.6 0.4 collective-permute-start.20
  91.0 1.3 %collective-permute-start.21 = (bf16[3,72,128]{2,1,0:T(8,128)(2,1)S(1)}, bf16[3,72,128]{2,1,0:T(8,128)(2,1)S(1)}, u32[]{:S(2)}, u32[]{:S(2)}) collective-permute-start(bf16[3,72,128]{2,1,0:T(8,128)(2,1)S(1)} %get-tuple-element.113), channel_id=1, source_target_pairs={{0,2},{1,3},{2,0},{3,1},{4,6},{5,7},{6,4},{7,5},{8,10},{9,11},{10,... | collective-permute-start | bytes 165896 | tf_op jit(solution)/shard_map/ppermute | solution.py:488
  92.2 0.5 collective-permute-start.22
  92.8 2.0 %collective-permute-done.25.refs_7_ = bf16[6,72,128]{2,1,0:T(8,128)(2,1)S(1)} collective-permute-done((bf16[6,72,128]{2,1,0:T(8,128)(2,1)S(1)}, bf16[6,72,128]{2,1,0:T(8,128)(2,1)S(1)}, u32[]{:S(2)}, u32[]{:S(2)}) %collective-permute-start.25) | collective-permute-done | bytes 110624 | tf_op jit(solution)/shard_map/ppermute | solution.py:548
  94.8 2.1 %collective-permute-done.21.refs_2_ = bf16[3,72,128]{2,1,0:T(8,128)(2,1)S(1)} collective-permute-done((bf16[3,72,128]{2,1,0:T(8,128)(2,1)S(1)}, bf16[3,72,128]{2,1,0:T(8,128)(2,1)S(1)}, u32[]{:S(2)}, u32[]{:S(2)}) %collective-permute-start.21) | collective-permute-done | bytes 55328 | tf_op jit(solution)/shard_map/ppermute | solution.py:488
  96.9 0.7 collective-permute-done.22.refs_3_
  97.6 0.7 shard_map.154
  98.4 6.8 %all-to-all-start = ((bf16[8,72,128]{2,1,0:T(8,128)(2,1)}), bf16[8,72,128]{2,1,0:T(8,128)(2,1)S(1)}, u32[]{:S(2)}, u32[]{:S(2)}) async-start(bf16[8,72,128]{2,1,0:T(8,128)(2,1)} %shard_map.154), calls=%async_computation | async-start | bytes 294912 | tf_op jit(solution)/shard_map/all_to_all | solution.py:664
  105.2 1.2 %shard_map.146 = bf16[2,16,3200]{2,1,0:T(8,128)(2,1)} custom-call(bf16[128,800]{1,0:T(8,128)(2,1)S(1)} %get-tuple-element.68.blocks, bf16[128,400]{1,0:T(8,128)(2,1)S(1)} %get-tuple-element.76.level, bf16[400,800]{1,0:T(8,128)(2,1)S(1)} %copy-done.3, f32[128,800]{1,0:T(8,128)S(1)} %get-tuple-element.66.mask_cat), custom_call_target="tpu_custom_call" | custom-call | flops 1000000000 | bytes 1000000 | tf_op jit(solution)/shard_map/pallas_call | solution.py:32
  106.4 8.1 %all-to-all-done.parts = bf16[8,72,128]{2,1,0:T(8,128)(2,1)S(1)} async-done(((bf16[8,72,128]{2,1,0:T(8,128)(2,1)}), bf16[8,72,128]{2,1,0:T(8,128)(2,1)S(1)}, u32[]{:S(2)}, u32[]{:S(2)}) %all-to-all-start) | async-done | bytes 147488 | tf_op jit(solution)/shard_map/all_to_all | solution.py:664
  114.5 0.6 slice_bitcast_fusion
  (47 shorter events, 1.6 us)
Async XLA Ops:
  1.3 0.9 copy-start.6
  2.2 0.7 copy-start.10
  2.9 8.4 %copy-start.3 = (bf16[400,800]{1,0:T(8,128)(2,1)S(1)}, bf16[400,800]{1,0:T(8,128)(2,1)}, u32[]{:S(2)}) copy-start(bf16[400,800]{1,0:T(8,128)(2,1)} %w_up.3) | copy-start | bytes 1920004
  2.9 8.4 %copy-start.7 = (bf16[1,2,16,3200]{3,2,1,0:T(8,128)(2,1)S(1)}, bf16[1,2,16,3200]{3,2,1,0:T(8,128)(2,1)}, u32[]{:S(2)}) copy-start(bf16[1,2,16,3200]{3,2,1,0:T(8,128)(2,1)} %param.25) | copy-start | bytes 614404
  3.4 9.6 %collective-permute-start = (bf16[2,3,16,200]{3,2,1,0:T(8,128)(2,1)S(1)}, bf16[2,3,16,200]{3,2,1,0:T(8,128)(2,1)S(1)}, u32[]{:S(2)}, u32[]{:S(2)}) collective-permute-start(bf16[2,3,16,200]{3,2,1,0:T(8,128)(2,1)S(1)} %get-tuple-element.62.east), channel_id=1, source_target_pairs={{0,8},{8,16},{16,24},{24,32},{32,40},{40,48},{48,56},{56,64},{64,7... | collective-permute-start | bytes 115208 | tf_op jit(solution)/shard_map/ppermute | solution.py:488
  3.5 9.6 %collective-permute-start.1 = (bf16[2,3,16,200]{3,2,1,0:T(8,128)(2,1)S(1)}, bf16[2,3,16,200]{3,2,1,0:T(8,128)(2,1)S(1)}, u32[]{:S(2)}, u32[]{:S(2)}) collective-permute-start(bf16[2,3,16,200]{3,2,1,0:T(8,128)(2,1)S(1)} %get-tuple-element.61.west), channel_id=1, source_target_pairs={{0,248},{8,0},{16,8},{24,16},{32,24},{40,32},{48,40},{56,48},{64,5... | collective-permute-start | bytes 115208 | tf_op jit(solution)/shard_map/ppermute | solution.py:488
  11.3 1.7 %copy-start.11 = (s32[1,2,4]{2,1,0:T(2,128)S(1)}, s32[1,2,4]{2,1,0:T(2,128)}, u32[]{:S(2)}) copy-start(s32[1,2,4]{2,1,0:T(2,128)} %param.16) | copy-start | bytes 100
  13.1 7.2 %copy-start.2 = (bf16[800,400]{0,1:T(8,128)(2,1)S(1)}, bf16[800,400]{0,1:T(8,128)(2,1)}, u32[]{:S(2)}) copy-start(bf16[800,400]{0,1:T(8,128)(2,1)} %param.20) | copy-start | bytes 1920004
  13.1 7.2 %copy-start.4 = (bf16[200,800]{1,0:T(8,128)(2,1)S(1)}, bf16[200,800]{1,0:T(8,128)(2,1)}, u32[]{:S(2)}) copy-start(bf16[200,800]{1,0:T(8,128)(2,1)} %w_in.5) | copy-start | bytes 960004
  13.1 7.2 %copy-start.5 = (bf16[800,200]{0,1:T(8,128)(2,1)S(1)}, bf16[800,200]{0,1:T(8,128)(2,1)}, u32[]{:S(2)}) copy-start(bf16[800,200]{0,1:T(8,128)(2,1)} %param.19) | copy-start | bytes 960004
  13.1 7.2 %copy-start.9 = (bf16[7,7,200]{2,1,0:T(8,128)(2,1)S(1)}, bf16[7,7,200]{2,1,0:T(8,128)(2,1)}, u32[]{:S(2)}) copy-start(bf16[7,7,200]{2,1,0:T(8,128)(2,1)} %kern.3) | copy-start | bytes 58804
  13.8 4.1 %collective-permute-start.2 = (bf16[22,3,200]{2,1,0:T(4,128)(2,1)S(1)}, bf16[22,3,200]{2,1,0:T(4,128)(2,1)S(1)}, u32[]{:S(2)}, u32[]{:S(2)}) collective-permute-start(bf16[22,3,200]{2,1,0:T(4,128)(2,1)S(1)} %get-tuple-element.64), channel_id=1, source_target_pairs={{0,1},{1,2},{2,3},{3,4},{4,5},{5,6},{6,7},{7,0},{8,9},{9,10},{10,1... | collective-permute-start | bytes 79208 | tf_op jit(solution)/shard_map/ppermute | solution.py:488
  14.2 6.2 %collective-permute-start.3 = (bf16[22,3,200]{2,1,0:T(4,128)(2,1)S(1)}, bf16[22,3,200]{2,1,0:T(4,128)(2,1)S(1)}, u32[]{:S(2)}, u32[]{:S(2)}) collective-permute-start(bf16[22,3,200]{2,1,0:T(4,128)(2,1)S(1)} %get-tuple-element.65), channel_id=1, source_target_pairs={{0,7},{1,0},{2,1},{3,2},{4,3},{5,4},{6,5},{7,6},{8,15},{9,8},{10,9... | collective-permute-start | bytes 79208 | tf_op jit(solution)/shard_map/ppermute | solution.py:488
  24.9 7.3 %collective-permute-start.4 = (bf16[2,3,8,400]{3,2,1,0:T(8,128)(2,1)S(1)}, bf16[2,3,8,400]{3,2,1,0:T(8,128)(2,1)S(1)}, u32[]{:S(2)}, u32[]{:S(2)}) collective-permute-start(bf16[2,3,8,400]{3,2,1,0:T(8,128)(2,1)S(1)} %get-tuple-element.71.east), channel_id=1, source_target_pairs={{0,8},{8,16},{16,24},{24,32},{32,40},{40,48},{48,56},{56,64},{64,7... | collective-permute-start | bytes 115208 | tf_op jit(solution)/shard_map/ppermute | solution.py:488
  25.0 7.2 %collective-permute-start.5 = (bf16[2,3,8,400]{3,2,1,0:T(8,128)(2,1)S(1)}, bf16[2,3,8,400]{3,2,1,0:T(8,128)(2,1)S(1)}, u32[]{:S(2)}, u32[]{:S(2)}) collective-permute-start(bf16[2,3,8,400]{3,2,1,0:T(8,128)(2,1)S(1)} %get-tuple-element.70.west), channel_id=1, source_target_pairs={{0,248},{8,0},{16,8},{24,16},{32,24},{40,32},{48,40},{56,48},{64,5... | collective-permute-start | bytes 115208 | tf_op jit(solution)/shard_map/ppermute | solution.py:488
  32.2 7.2 %copy-start = (bf16[400,1600]{1,0:T(8,128)(2,1)S(1)}, bf16[400,1600]{1,0:T(8,128)(2,1)}, u32[]{:S(2)}) copy-start(bf16[400,1600]{1,0:T(8,128)(2,1)} %w_in.4) | copy-start | bytes 3840004
  32.2 7.2 %copy-start.1 = (bf16[1600,400]{0,1:T(8,128)(2,1)S(1)}, bf16[1600,400]{0,1:T(8,128)(2,1)}, u32[]{:S(2)}) copy-start(bf16[1600,400]{0,1:T(8,128)(2,1)} %param.23) | copy-start | bytes 3840004
  32.2 7.2 %copy-start.8 = (bf16[7,7,400]{2,1,0:T(8,128)(2,1)S(1)}, bf16[7,7,400]{2,1,0:T(8,128)(2,1)}, u32[]{:S(2)}) copy-start(bf16[7,7,400]{2,1,0:T(8,128)(2,1)} %kern.5) | copy-start | bytes 117604
  33.0 4.3 %collective-permute-start.6 = (bf16[14,3,400]{2,1,0:T(4,128)(2,1)S(1)}, bf16[14,3,400]{2,1,0:T(4,128)(2,1)S(1)}, u32[]{:S(2)}, u32[]{:S(2)}) collective-permute-start(bf16[14,3,400]{2,1,0:T(4,128)(2,1)S(1)} %get-tuple-element.73), channel_id=1, source_target_pairs={{0,1},{1,2},{2,3},{3,4},{4,5},{5,6},{6,7},{7,0},{8,9},{9,10},{10,1... | collective-permute-start | bytes 100808 | tf_op jit(solution)/shard_map/ppermute | solution.py:488
  33.0 6.4 %collective-permute-start.7 = (bf16[14,3,400]{2,1,0:T(4,128)(2,1)S(1)}, bf16[14,3,400]{2,1,0:T(4,128)(2,1)S(1)}, u32[]{:S(2)}, u32[]{:S(2)}) collective-permute-start(bf16[14,3,400]{2,1,0:T(4,128)(2,1)S(1)} %get-tuple-element.74), channel_id=1, source_target_pairs={{0,7},{1,0},{2,1},{3,2},{4,3},{5,4},{6,5},{7,6},{8,15},{9,8},{10,9... | collective-permute-start | bytes 100808 | tf_op jit(solution)/shard_map/ppermute | solution.py:488
  43.4 9.2 %collective-permute-start.8 = (bf16[2,3,8,400]{3,2,1,0:T(8,128)(2,1)S(1)}, bf16[2,3,8,400]{3,2,1,0:T(8,128)(2,1)S(1)}, u32[]{:S(2)}, u32[]{:S(2)}) collective-permute-start(bf16[2,3,8,400]{3,2,1,0:T(8,128)(2,1)S(1)} %get-tuple-element.79.east), channel_id=1, source_target_pairs={{0,8},{8,16},{16,24},{24,32},{32,40},{40,48},{48,56},{56,64},{64,7... | collective-permute-start | bytes 115208 | tf_op jit(solution)/shard_map/ppermute | solution.py:488
  43.6 9.0 %collective-permute-start.9 = (bf16[2,3,8,400]{3,2,1,0:T(8,128)(2,1)S(1)}, bf16[2,3,8,400]{3,2,1,0:T(8,128)(2,1)S(1)}, u32[]{:S(2)}, u32[]{:S(2)}) collective-permute-start(bf16[2,3,8,400]{3,2,1,0:T(8,128)(2,1)S(1)} %get-tuple-element.78.west), channel_id=1, source_target_pairs={{0,248},{8,0},{16,8},{24,16},{32,24},{40,32},{48,40},{56,48},{64,5... | collective-permute-start | bytes 115208 | tf_op jit(solution)/shard_map/ppermute | solution.py:488
  52.6 3.8 %collective-permute-start.12 = (bf16[16,6,72,128]{3,2,1,0:T(8,128)(2,1)S(1)}, bf16[16,6,72,128]{3,2,1,0:T(8,128)(2,1)S(1)}, u32[]{:S(2)}, u32[]{:S(2)}) collective-permute-start(bf16[16,6,72,128]{3,2,1,0:T(8,128)(2,1)S(1)} %get-tuple-element.97), channel_id=1, source_target_pairs={{0,8},{8,0},{1,9},{9,1},{2,10},{10,2},{3,11},{11,3},{4,12},{12,4},... | collective-permute-start | bytes 5308424 | tf_op jit(solution)/shard_map/ppermute | solution.py:499
  53.5 5.4 %collective-permute-start.10 = (bf16[14,3,400]{2,1,0:T(4,128)(2,1)S(1)}, bf16[14,3,400]{2,1,0:T(4,128)(2,1)S(1)}, u32[]{:S(2)}, u32[]{:S(2)}) collective-permute-start(bf16[14,3,400]{2,1,0:T(4,128)(2,1)S(1)} %get-tuple-element.89), channel_id=1, source_target_pairs={{0,1},{1,2},{2,3},{3,4},{4,5},{5,6},{6,7},{7,0},{8,9},{9,10},{10,1... | collective-permute-start | bytes 100808 | tf_op jit(solution)/shard_map/ppermute | solution.py:488
  53.6 6.5 %collective-permute-start.11 = (bf16[14,3,400]{2,1,0:T(4,128)(2,1)S(1)}, bf16[14,3,400]{2,1,0:T(4,128)(2,1)S(1)}, u32[]{:S(2)}, u32[]{:S(2)}) collective-permute-start(bf16[14,3,400]{2,1,0:T(4,128)(2,1)S(1)} %get-tuple-element.90), channel_id=1, source_target_pairs={{0,7},{1,0},{2,1},{3,2},{4,3},{5,4},{6,5},{7,6},{8,15},{9,8},{10,9... | collective-permute-start | bytes 100808 | tf_op jit(solution)/shard_map/ppermute | solution.py:488
  56.8 12.3 %collective-permute-start.13 = (bf16[4,6,72,128]{3,2,1,0:T(8,128)(2,1)S(1)}, bf16[4,6,72,128]{3,2,1,0:T(8,128)(2,1)S(1)}, u32[]{:S(2)}, u32[]{:S(2)}) collective-permute-start(bf16[4,6,72,128]{3,2,1,0:T(8,128)(2,1)S(1)} %get-tuple-element.98), channel_id=1, source_target_pairs={{0,1},{1,2},{2,3},{3,0},{4,5},{5,6},{6,7},{7,4},{8,9},{9,10},{10,1... | collective-permute-start | bytes 1327112 | tf_op jit(solution)/shard_map/ppermute | solution.py:488
  58.1 13.2 %collective-permute-start.14 = (bf16[4,6,72,128]{3,2,1,0:T(8,128)(2,1)S(1)}, bf16[4,6,72,128]{3,2,1,0:T(8,128)(2,1)S(1)}, u32[]{:S(2)}, u32[]{:S(2)}) collective-permute-start(bf16[4,6,72,128]{3,2,1,0:T(8,128)(2,1)S(1)} %get-tuple-element.99), channel_id=1, source_target_pairs={{0,3},{1,0},{2,1},{3,2},{4,7},{5,4},{6,5},{7,6},{8,11},{9,8},{10,9... | collective-permute-start | bytes 1327112 | tf_op jit(solution)/shard_map/ppermute | solution.py:488
  71.4 2.4 %collective-permute-start.15 = (bf16[16,3,72,128]{3,2,1,0:T(8,128)(2,1)S(1)}, bf16[16,3,72,128]{3,2,1,0:T(8,128)(2,1)S(1)}, u32[]{:S(2)}, u32[]{:S(2)}) collective-permute-start(bf16[16,3,72,128]{3,2,1,0:T(8,128)(2,1)S(1)} %get-tuple-element.100), channel_id=1, source_target_pairs={{0,8},{8,0},{1,9},{9,1},{2,10},{10,2},{3,11},{11,3},{4,12},{12,4},... | collective-permute-start | bytes 2654216 | tf_op jit(solution)/shard_map/ppermute | solution.py:499
  71.4 14.1 %collective-permute-start.17 = (bf16[4,6,72,128]{3,2,1,0:T(8,128)(2,1)S(1)}, bf16[4,6,72,128]{3,2,1,0:T(8,128)(2,1)S(1)}, u32[]{:S(2)}, u32[]{:S(2)}) collective-permute-start(bf16[4,6,72,128]{3,2,1,0:T(8,128)(2,1)S(1)} %get-tuple-element.105), channel_id=1, source_target_pairs={{0,2},{1,3},{2,0},{3,1},{4,6},{5,7},{6,4},{7,5},{8,10},{9,11},{10,... | collective-permute-start | bytes 1327112 | tf_op jit(solution)/shard_map/ppermute | solution.py:488
  74.0 12.5 %collective-permute-start.16 = (bf16[4,3,72,128]{3,2,1,0:T(8,128)(2,1)S(1)}, bf16[4,3,72,128]{3,2,1,0:T(8,128)(2,1)S(1)}, u32[]{:S(2)}, u32[]{:S(2)}) collective-permute-start(bf16[4,3,72,128]{3,2,1,0:T(8,128)(2,1)S(1)} %get-tuple-element.102), channel_id=1, source_target_pairs={{0,4},{4,0},{16,20},{20,16},{1,5},{5,1},{17,21},{21,17},{2,6},{6,2... | collective-permute-start | bytes 663560 | tf_op jit(solution)/shard_map/ppermute | solution.py:548
  74.8 15.7 %collective-permute-start.18 = (bf16[4,3,72,128]{3,2,1,0:T(8,128)(2,1)S(1)}, bf16[4,3,72,128]{3,2,1,0:T(8,128)(2,1)S(1)}, u32[]{:S(2)}, u32[]{:S(2)}) collective-permute-start(bf16[4,3,72,128]{3,2,1,0:T(8,128)(2,1)S(1)} %get-tuple-element.109), channel_id=1, source_target_pairs={{0,16},{4,20},{16,0},{20,4},{1,17},{5,21},{17,1},{21,5},{2,18},{6,... | collective-permute-start | bytes 663560 | tf_op jit(solution)/shard_map/ppermute | solution.py:548
  74.8 15.7 %collective-permute-start.19 = (bf16[4,3,72,128]{3,2,1,0:T(8,128)(2,1)S(1)}, bf16[4,3,72,128]{3,2,1,0:T(8,128)(2,1)S(1)}, u32[]{:S(2)}, u32[]{:S(2)}) collective-permute-start(bf16[4,3,72,128]{3,2,1,0:T(8,128)(2,1)S(1)} %get-tuple-element.110), channel_id=1, source_target_pairs={{0,20},{4,16},{16,4},{20,0},{1,21},{5,17},{17,5},{21,1},{2,22},{6,... | collective-permute-start | bytes 663560 | tf_op jit(solution)/shard_map/ppermute | solution.py:548
  85.7 6.5 %collective-permute-start.23 = (bf16[6,72,128]{2,1,0:T(8,128)(2,1)S(1)}, bf16[6,72,128]{2,1,0:T(8,128)(2,1)S(1)}, u32[]{:S(2)}, u32[]{:S(2)}) collective-permute-start(bf16[6,72,128]{2,1,0:T(8,128)(2,1)S(1)} %get-tuple-element.107), channel_id=1, source_target_pairs={{0,4},{4,0},{16,20},{20,16},{1,5},{5,1},{17,21},{21,17},{2,6},{6,2... | collective-permute-start | bytes 331784 | tf_op jit(solution)/shard_map/ppermute | solution.py:548
  86.5 6.3 %collective-permute-start.24 = (bf16[6,72,128]{2,1,0:T(8,128)(2,1)S(1)}, bf16[6,72,128]{2,1,0:T(8,128)(2,1)S(1)}, u32[]{:S(2)}, u32[]{:S(2)}) collective-permute-start(bf16[6,72,128]{2,1,0:T(8,128)(2,1)S(1)} %get-tuple-element.116), channel_id=1, source_target_pairs={{0,16},{4,20},{16,0},{20,4},{1,17},{5,21},{17,1},{21,5},{2,18},{6,... | collective-permute-start | bytes 331784 | tf_op jit(solution)/shard_map/ppermute | solution.py:548
  86.5 8.3 %collective-permute-start.25 = (bf16[6,72,128]{2,1,0:T(8,128)(2,1)S(1)}, bf16[6,72,128]{2,1,0:T(8,128)(2,1)S(1)}, u32[]{:S(2)}, u32[]{:S(2)}) collective-permute-start(bf16[6,72,128]{2,1,0:T(8,128)(2,1)S(1)} %get-tuple-element.117), channel_id=1, source_target_pairs={{0,20},{4,16},{16,4},{20,0},{1,21},{5,17},{17,5},{21,1},{2,22},{6,... | collective-permute-start | bytes 331784 | tf_op jit(solution)/shard_map/ppermute | solution.py:548
  90.6 4.2 %collective-permute-start.20 = (bf16[3,72,128]{2,1,0:T(8,128)(2,1)S(1)}, bf16[3,72,128]{2,1,0:T(8,128)(2,1)S(1)}, u32[]{:S(2)}, u32[]{:S(2)}) collective-permute-start(bf16[3,72,128]{2,1,0:T(8,128)(2,1)S(1)} %get-tuple-element.112), channel_id=1, source_target_pairs={{0,1},{1,2},{2,3},{3,0},{4,5},{5,6},{6,7},{7,4},{8,9},{9,10},{10,1... | collective-permute-start | bytes 165896 | tf_op jit(solution)/shard_map/ppermute | solution.py:488
  91.0 6.0 %collective-permute-start.21 = (bf16[3,72,128]{2,1,0:T(8,128)(2,1)S(1)}, bf16[3,72,128]{2,1,0:T(8,128)(2,1)S(1)}, u32[]{:S(2)}, u32[]{:S(2)}) collective-permute-start(bf16[3,72,128]{2,1,0:T(8,128)(2,1)S(1)} %get-tuple-element.113), channel_id=1, source_target_pairs={{0,2},{1,3},{2,0},{3,1},{4,6},{5,7},{6,4},{7,5},{8,10},{9,11},{10,... | collective-permute-start | bytes 165896 | tf_op jit(solution)/shard_map/ppermute | solution.py:488
  92.2 5.4 %collective-permute-start.22 = (bf16[3,72,128]{2,1,0:T(8,128)(2,1)S(1)}, bf16[3,72,128]{2,1,0:T(8,128)(2,1)S(1)}, u32[]{:S(2)}, u32[]{:S(2)}) collective-permute-start(bf16[3,72,128]{2,1,0:T(8,128)(2,1)S(1)} %get-tuple-element.114), channel_id=1, source_target_pairs={{0,3},{1,0},{2,1},{3,2},{4,7},{5,4},{6,5},{7,6},{8,11},{9,8},{10,9... | collective-permute-start | bytes 165896 | tf_op jit(solution)/shard_map/ppermute | solution.py:488
  98.4 16.1 %all-to-all-start = ((bf16[8,72,128]{2,1,0:T(8,128)(2,1)}), bf16[8,72,128]{2,1,0:T(8,128)(2,1)S(1)}, u32[]{:S(2)}, u32[]{:S(2)}) async-start(bf16[8,72,128]{2,1,0:T(8,128)(2,1)} %shard_map.154), calls=%async_computation | async-start | bytes 294912 | tf_op jit(solution)/shard_map/all_to_all | solution.py:664

commit v2 on v1

--- a/solution.py
+++ b/solution.py
@@ -367,7 +367,7 @@
         held[t, 48:rows, :] = jnp.zeros((rows - 48, LANES), F32)
 
 
-def grads_two_kernel(field, back, normed_b, hidden, grad_pre, level, change, cot_cat, keep, send, flat, held, tall, sums):
+def grads_two_kernel(field, back, normed_b, hidden, grad_pre, level, change, cot_cat, keep, send, carry, flat, held, tall, sums):
     flat[0:64, :] = jnp.zeros((64, LANES), F32)
     clear_taps(held, 4, 56)
     for t in range(4):
@@ -394,6 +394,7 @@
     lay_flat(flat, held, 1949400, C2, 4 * C1, SPLIT_ROW)
     last = 17730 - SPLIT_ROW
     flat[last:, :] = jnp.zeros((17920 + 8 - SPLIT_ROW - last, LANES), F32)
+    carry[...] = flat[0:BLOCK, :]
     keep[:8, 0] = jnp.zeros((8, HELD, LANES), BF16)
     send[:8, 0] = jnp.zeros((8, HELD, LANES), BF16)
     split_out(lax.axis_index("c"), flat, keep, send, 9, 32, store_two)
@@ -426,7 +427,7 @@
 
 
 def last_kernel(entries, delta, top_got, bottom_got, kern, change, mask_two, mask_cat, cot_cat, blocks,
-                w_down, w_in, w_out, normed, scales, field, keep, send,
+                w_down, w_in, w_out, normed, scales, field, carry, keep, send,
                 out, taps, conv, held_cat, rough, hidden, grad_pre, fine, back, sums, flat, held):
     out[...] = delta[...]
     for slot in range(2):
@@ -476,6 +477,7 @@
     hold(held, product_tn(blocks[...], rough[...]))
     lay_flat(flat, held, 329800, 4 * C1, C2, 0)
     flat[5077:, :] = jnp.zeros((5608 - 5077, LANES), F32)
+    flat[SPLIT_ROW : SPLIT_ROW + BLOCK, :] = flat[SPLIT_ROW : SPLIT_ROW + BLOCK, :] + carry[...]
     keep[8:, 2] = jnp.zeros((8, HELD, LANES), BF16)
     send[8:, 2] = jnp.zeros((8, HELD, LANES), BF16)
     split_out(lax.axis_index("c"), flat, keep, send, 0, 10, store_one)
@@ -510,8 +512,12 @@
     parts, outs = refs[:-4], refs[-4:]
     x = 2 * lax.axis_index("xh") + lax.axis_index("xl")
     for k in range(4):
-        for z in range(outs[k].shape[0]):
-            outs[k][z] = added([part[x ^ k, z] for part in parts])
+        place = x ^ k
+        first = added([part[jnp.maximum(6 * place - 2, 10)] for part in parts])
+        outs[k][0] = jnp.where(place >= 2, first.astype(F32), 0.0).astype(BF16)
+        for z in range(1, 6):
+            index = jnp.where(place < 2, 5 * place + z - 1, 6 * place - 2 + z)
+            outs[k][z] = added([part[index] for part in parts])
 
 
 def y_parts_kernel(keep, got, *outs):
@@ -519,8 +525,9 @@
     for k in range(4):
         for x in range(4):
             place = 4 * x + (y + k) % 4
-            for z in range(outs[k].shape[1]):
-                outs[k][x, z] = added([keep[place, z], got[place, z]])
+            for z in range(1 if x < 2 else 0, 6):
+                index = 5 * x + z - 1 if x < 2 else 6 * x - 2 + z
+                outs[k][index] = added([keep[place, z], got[place, z]])
 
 
 def x_first_kernel(keep, got, *outs):
@@ -611,9 +618,9 @@
         room=16, us=6, smem=1,
     )(entries, *sides, kern_two, w_in_two, w_out_two, coarse, change, mask_two)
     west_got, east_got = around(east, TILES, 1), around(west, TILES, -1)
-    keep_two, send_two = call(
+    keep_two, send_two, carry = call(
         grads_two_kernel,
-        [((16, 6, HELD, LANES), BF16)] * 2,
+        [((16, 6, HELD, LANES), BF16)] * 2 + [((BLOCK, LANES), F32)],
         [((17920 + 8 - SPLIT_ROW, LANES), F32), ((13, C2, LANES), F32), ((4, 4 * C2, LANES), F32), ((49, HALF, LANES), F32)],
         room=16, us=7,
     )(field_in_two, back, normed_two, hidden_two, grad_pre_two, level, change, cot_cat)
@@ -626,7 +633,7 @@
     )(blocks, level, w_up, mask_cat)
     field, top, bottom = strips_two(back, west, west_got, east, east_got)
     top_got, bottom_got = around(bottom, LAT, 1), around(top, LAT, -1)
-    parts = list(call(y_parts_kernel, [((4, 6, HELD, LANES), BF16)] * 4)(keep_two, got_two))
+    parts = list(call(y_parts_kernel, [((22, HELD, LANES), BF16)] * 4)(keep_two, got_two))
     parts_two = over_y(parts)
     sides = field, top_got, bottom_got
     keep_one, send_one = call(
@@ -647,7 +654,7 @@
             ((7, 800, LANES), F32),
         ],
         room=16, us=10, smem=1,
-    )(entries, *sides, kern_two, change, mask_two, mask_cat, cot_cat, blocks, w_down, w_in_one, w_out_one, normed_one, scales_one, field_one_own)
+    )(entries, *sides, kern_two, change, mask_two, mask_cat, cot_cat, blocks, w_down, w_in_one, w_out_one, normed_one, scales_one, field_one_own, carry)
     send_one, parts_two[1], parts_two[3] = lax.optimization_barrier((send_one, parts_two[1], parts_two[3]))
     return prediction[None], finish(keep_one, send_one, parts_two)
 

time: 115 us -> 116 us (level)
  starting transfers between devices: 46 us -> 48.2 us
  waiting for transfers between devices: 38.7 us -> 37.1 us
    all_to_all x1, starting transfers between devices: 6.85 us -> 9.02 us  [finish(): total = lax.all_to_all(total, 'z', 0, 0)]
    ppermute x18, waiting for transfers between devices: 25.3 us -> 23.7 us  [around(): lax.ppermute(array, axes, [(i, (i + step) % size) for i in range(size)])]
  transfers between devices with their start and end apart: 27 -> 27, of which waited for: 19 -> 18; matrix products, arithmetic and copies ran while one was open for 0% -> 0% of each run, Pallas kernels for 13% -> 13%
where the time goes in v2:
time: 116 us
  starting transfers between devices  48.2 us (42%)
  waiting for transfers between devices  37.1 us (32%)
  Pallas kernels  26.9 us (23%)
  local copies, waits for them, and re-layouts  2.26 us (2%)
  between operations  1.5 us (1%)
    ppermute x18, starting transfers between devices, around(): lax.ppermute(array, axes, [(i, (i + step) % size) for i in range(size)])  29.5 us
    pallas_call x16, Pallas kernels, run(): pl.pallas_call(body, out_shape=[jax.ShapeDtypeStruct(shape, kind) for sha...  26.9 us
    ppermute x18, waiting for transfers between devices, around(): lax.ppermute(array, axes, [(i, (i + step) % size) for i in range(size)])  23.7 us
    ppermute x6, starting transfers between devices, over_x(): lax.ppermute(parts[k], ('xh', 'xl'), [(i, i ^ k) for i in range(4)])  9.57 us
    all_to_all x1, starting transfers between devices, finish(): total = lax.all_to_all(total, 'z', 0, 0)  9.02 us
    all_to_all x1, waiting for transfers between devices, finish(): total = lax.all_to_all(total, 'z', 0, 0)  8.1 us
    ppermute x2, waiting for transfers between devices, other_core(): return lax.ppermute(send, 'c', [(0, 1), (1, 0)])  3.25 us
  transfers between devices with their start and end apart: 27, of which 18 were waited for; matrix products, arithmetic and copies ran while one was open for 0% of the time, Pallas kernels for 13%

profile of v2, /device:TPU:24, one launch (start us, length us, event | category | flops | bytes accessed | tf_op | source)
XLA Modules:
  0.0 115.9 jit_solution(10590726556889245004)
XLA Ops:
  1.3 0.9 copy-done.6
  2.2 0.7 copy-done.10
  2.9 0.5 shard_map.141
  3.5 7.8 %collective-permute-start.1 = (bf16[2,3,16,200]{3,2,1,0:T(8,128)(2,1)S(1)}, bf16[2,3,16,200]{3,2,1,0:T(8,128)(2,1)S(1)}, u32[]{:S(2)}, u32[]{:S(2)}) collective-permute-start(bf16[2,3,16,200]{3,2,1,0:T(8,128)(2,1)S(1)} %get-tuple-element.62.west), channel_id=1, source_target_pairs={{0,248},{8,0},{16,8},{24,16},{32,24},{40,32},{48,40},{56,48},{64,5... | collective-permute-start | bytes 115208 | tf_op jit(solution)/shard_map/ppermute | solution.py:490
  11.3 1.0 shard_map.140
  12.3 0.7 collective-permute-done.west_got
  13.1 0.7 shard_map.142
  13.8 0.3 collective-permute-start.2
  14.2 1.8 %collective-permute-start.3 = (bf16[22,3,200]{2,1,0:T(4,128)(2,1)S(1)}, bf16[22,3,200]{2,1,0:T(4,128)(2,1)S(1)}, u32[]{:S(2)}, u32[]{:S(2)}) collective-permute-start(bf16[22,3,200]{2,1,0:T(4,128)(2,1)S(1)} %get-tuple-element.66), channel_id=1, source_target_pairs={{0,7},{1,0},{2,1},{3,2},{4,3},{5,4},{6,5},{7,6},{8,15},{9,8},{10,9... | collective-permute-start | bytes 79208 | tf_op jit(solution)/shard_map/ppermute | solution.py:490
  15.9 2.0 %collective-permute-done.2.top_got = bf16[22,3,200]{2,1,0:T(4,128)(2,1)S(1)} collective-permute-done((bf16[22,3,200]{2,1,0:T(4,128)(2,1)S(1)}, bf16[22,3,200]{2,1,0:T(4,128)(2,1)S(1)}, u32[]{:S(2)}, u32[]{:S(2)}) %collective-permute-start.2) | collective-permute-done | bytes 26432 | tf_op jit(solution)/shard_map/ppermute | solution.py:490
  18.0 2.4 %collective-permute-done.3.bottom_got = bf16[22,3,200]{2,1,0:T(4,128)(2,1)S(1)} collective-permute-done((bf16[22,3,200]{2,1,0:T(4,128)(2,1)S(1)}, bf16[22,3,200]{2,1,0:T(4,128)(2,1)S(1)}, u32[]{:S(2)}, u32[]{:S(2)}) %collective-permute-start.3) | collective-permute-done | bytes 26432 | tf_op jit(solution)/shard_map/ppermute | solution.py:490
  20.3 4.6 %shard_map.143 = (f32[2,2,22,24,128]{4,3,2,1,0:T(8,128)S(1)}, f32[512,256]{1,0:T(8,128)S(1)}, f32[512,128]{1,0:T(8,128)S(1)}, bf16[128,800]{1,0:T(8,128)(2,1)S(1...) custom-call(s32[2,4]{1,0:T(2,128)S(1)} %bitcast.21, ...), custom_call_target="tpu_custom_call" | custom-call | flops 6000000000 | bytes 1000000 | tf_op jit(solution)/shard_map/pallas_call | solution.py:32
  25.1 5.3 %collective-permute-start.5 = (bf16[2,3,8,400]{3,2,1,0:T(8,128)(2,1)S(1)}, bf16[2,3,8,400]{3,2,1,0:T(8,128)(2,1)S(1)}, u32[]{:S(2)}, u32[]{:S(2)}) collective-permute-start(bf16[2,3,8,400]{3,2,1,0:T(8,128)(2,1)S(1)} %get-tuple-element.71.west), channel_id=1, source_target_pairs={{0,248},{8,0},{16,8},{24,16},{32,24},{40,32},{48,40},{56,48},{64,5... | collective-permute-start | bytes 115208 | tf_op jit(solution)/shard_map/ppermute | solution.py:490
  30.4 1.9 %collective-permute-done.4.west_got = bf16[2,3,8,400]{3,2,1,0:T(8,128)(2,1)S(1)} collective-permute-done((bf16[2,3,8,400]{3,2,1,0:T(8,128)(2,1)S(1)}, bf16[2,3,8,400]{3,2,1,0:T(8,128)(2,1)S(1)}, u32[]{:S(2)}, u32[]{:S(2)}) %collective-permute-start.4) | collective-permute-done | bytes 38432 | tf_op jit(solution)/shard_map/ppermute | solution.py:490
  32.3 0.7 shard_map.144
  33.1 2.0 %collective-permute-start.7 = (bf16[14,3,400]{2,1,0:T(4,128)(2,1)S(1)}, bf16[14,3,400]{2,1,0:T(4,128)(2,1)S(1)}, u32[]{:S(2)}, u32[]{:S(2)}) collective-permute-start(bf16[14,3,400]{2,1,0:T(4,128)(2,1)S(1)} %get-tuple-element.75), channel_id=1, source_target_pairs={{0,7},{1,0},{2,1},{3,2},{4,3},{5,4},{6,5},{7,6},{8,15},{9,8},{10,9... | collective-permute-start | bytes 100808 | tf_op jit(solution)/shard_map/ppermute | solution.py:490
  35.2 2.2 %collective-permute-done.6.top_got = bf16[14,3,400]{2,1,0:T(4,128)(2,1)S(1)} collective-permute-done((bf16[14,3,400]{2,1,0:T(4,128)(2,1)S(1)}, bf16[14,3,400]{2,1,0:T(4,128)(2,1)S(1)}, u32[]{:S(2)}, u32[]{:S(2)}) %collective-permute-start.6) | collective-permute-done | bytes 33632 | tf_op jit(solution)/shard_map/ppermute | solution.py:490
  37.3 2.2 %collective-permute-done.7.bottom_got = bf16[14,3,400]{2,1,0:T(4,128)(2,1)S(1)} collective-permute-done((bf16[14,3,400]{2,1,0:T(4,128)(2,1)S(1)}, bf16[14,3,400]{2,1,0:T(4,128)(2,1)S(1)}, u32[]{:S(2)}, u32[]{:S(2)}) %collective-permute-start.7) | collective-permute-done | bytes 33632 | tf_op jit(solution)/shard_map/ppermute | solution.py:490
  39.5 4.0 %shard_map.145 = (f32[2,4,14,16,128]{4,3,2,1,0:T(8,128)S(1)}, bf16[128,400]{1,0:T(8,128)(2,1)S(1)}, bf16[128,1600]{1,0:T(8,128)(2,1)S(1)}, bf16[128,1600]{1,0:T(...) custom-call(s32[2,4]{1,0:T(2,128)S(1)} %bitcast.23, ...), custom_call_target="tpu_custom_call" | custom-call | flops 6000000000 | bytes 1000000 | tf_op jit(solution)/shard_map/pallas_call | solution.py:32
  43.5 0.3 collective-permute-start.8
  43.8 5.3 %collective-permute-start.9 = (bf16[2,3,8,400]{3,2,1,0:T(8,128)(2,1)S(1)}, bf16[2,3,8,400]{3,2,1,0:T(8,128)(2,1)S(1)}, u32[]{:S(2)}, u32[]{:S(2)}) collective-permute-start(bf16[2,3,8,400]{3,2,1,0:T(8,128)(2,1)S(1)} %get-tuple-element.79.west), channel_id=1, source_target_pairs={{0,248},{8,0},{16,8},{24,16},{32,24},{40,32},{48,40},{56,48},{64,5... | collective-permute-start | bytes 115208 | tf_op jit(solution)/shard_map/ppermute | solution.py:490
  49.2 3.7 %shard_map.147 = (bf16[16,6,72,128]{3,2,1,0:T(8,128)(2,1)S(1)}, bf16[16,6,72,128]{3,2,1,0:T(8,128)(2,1)S(1)}, f32[560,128]{1,0:T(8,128)S(1)}) custom-call(f32[2,4,14,16,128]{4,3,2,1,0:T(8,128)S(1)} %get-tuple-element.81.field, bf16[128,400]{1,0:T(8,128)(2,1)S(1)} %get-tuple-element.78.back.rows, bf16[128,400]{1,0:T(8,128)(2,1)S(1)} %get-tuple-element.82.normed_b, ...), custom_call_target="tpu_custom_call" | custom-call | flops 7000000000 | bytes 1000000 | tf_op jit(solution)/shard_map/pallas_call | solution.py:32
  52.9 0.7 shard_map.148
  53.8 2.0 %collective-permute-start.11 = (bf16[14,3,400]{2,1,0:T(4,128)(2,1)S(1)}, bf16[14,3,400]{2,1,0:T(4,128)(2,1)S(1)}, u32[]{:S(2)}, u32[]{:S(2)}) collective-permute-start(bf16[14,3,400]{2,1,0:T(4,128)(2,1)S(1)} %get-tuple-element.91), channel_id=1, source_target_pairs={{0,7},{1,0},{2,1},{3,2},{4,3},{5,4},{6,5},{7,6},{8,15},{9,8},{10,9... | collective-permute-start | bytes 100808 | tf_op jit(solution)/shard_map/ppermute | solution.py:490
  55.8 0.8 collective-permute-done.12.got
  56.6 0.4 shard_map.150
  57.0 1.3 %collective-permute-start.13 = (bf16[22,72,128]{2,1,0:T(8,128)(2,1)S(1)}, bf16[22,72,128]{2,1,0:T(8,128)(2,1)S(1)}, u32[]{:S(2)}, u32[]{:S(2)}) collective-permute-start(bf16[22,72,128]{2,1,0:T(8,128)(2,1)S(1)} %get-tuple-element.100), channel_id=1, source_target_pairs={{0,1},{1,2},{2,3},{3,0},{4,5},{5,6},{6,7},{7,4},{8,9},{9,10},{10,1... | collective-permute-start | bytes 1216520 | tf_op jit(solution)/shard_map/ppermute | solution.py:490
  58.3 0.8 collective-permute-start.14
  59.1 1.2 %collective-permute-done.11.bottom_got = bf16[14,3,400]{2,1,0:T(4,128)(2,1)S(1)} collective-permute-done((bf16[14,3,400]{2,1,0:T(4,128)(2,1)S(1)}, bf16[14,3,400]{2,1,0:T(4,128)(2,1)S(1)}, u32[]{:S(2)}, u32[]{:S(2)}) %collective-permute-start.11) | collective-permute-done | bytes 33632 | tf_op jit(solution)/shard_map/ppermute | solution.py:490
  60.3 8.0 %shard_map.149 = (bf16[16,3,72,128]{3,2,1,0:T(8,128)(2,1)S(1)}, bf16[16,3,72,128]{3,2,1,0:T(8,128)(2,1)S(1)}) custom-call(s32[2,4]{1,0:T(2,128)S(1)} %bitcast.25, f32[2,4,14,16,128]{4,3,2,1,0:T(8,128)S(1)} %get-tuple-element.89.delta, bf16[14,3,400]{2,1,0:T(4,128)(2,1)S(1)} %collective-permute-done.10.top_got, ...), custom_call_target="tpu_custom_call" | custom-call | flops 10000000000 | bytes 1000000 | tf_op jit(solution)/shard_map/pallas_call | solution.py:32
  68.5 2.3 %collective-permute-done.14.refs_3_ = bf16[22,72,128]{2,1,0:T(8,128)(2,1)S(1)} collective-permute-done((bf16[22,72,128]{2,1,0:T(8,128)(2,1)S(1)}, bf16[22,72,128]{2,1,0:T(8,128)(2,1)S(1)}, u32[]{:S(2)}, u32[]{:S(2)}) %collective-permute-start.14) | collective-permute-done | bytes 405536 | tf_op jit(solution)/shard_map/ppermute | solution.py:490
  70.8 2.4 %collective-permute-done.15.got = bf16[16,3,72,128]{3,2,1,0:T(8,128)(2,1)S(1)} collective-permute-done((bf16[16,3,72,128]{3,2,1,0:T(8,128)(2,1)S(1)}, bf16[16,3,72,128]{3,2,1,0:T(8,128)(2,1)S(1)}, u32[]{:S(2)}, u32[]{:S(2)}) %collective-permute-start.15) | collective-permute-done | bytes 884768 | tf_op jit(solution)/shard_map/ppermute | solution.py:501
  73.4 0.8 collective-permute-start.16
  74.2 4.0 %collective-permute-start.19 = (bf16[4,3,72,128]{3,2,1,0:T(8,128)(2,1)S(1)}, bf16[4,3,72,128]{3,2,1,0:T(8,128)(2,1)S(1)}, u32[]{:S(2)}, u32[]{:S(2)}) collective-permute-start(bf16[4,3,72,128]{3,2,1,0:T(8,128)(2,1)S(1)} %get-tuple-element.112), channel_id=1, source_target_pairs={{0,20},{4,16},{16,4},{20,0},{1,21},{5,17},{17,5},{21,1},{2,22},{6,... | collective-permute-start | bytes 663560 | tf_op jit(solution)/shard_map/ppermute | solution.py:555
  78.2 5.9 %collective-permute-done.17.refs_2_ = bf16[22,72,128]{2,1,0:T(8,128)(2,1)S(1)} collective-permute-done((bf16[22,72,128]{2,1,0:T(8,128)(2,1)S(1)}, bf16[22,72,128]{2,1,0:T(8,128)(2,1)S(1)}, u32[]{:S(2)}, u32[]{:S(2)}) %collective-permute-start.17) | collective-permute-done | bytes 405536 | tf_op jit(solution)/shard_map/ppermute | solution.py:490
  84.3 0.8 collective-permute-start.23
  85.1 4.0 %collective-permute-start.25 = (bf16[6,72,128]{2,1,0:T(8,128)(2,1)S(1)}, bf16[6,72,128]{2,1,0:T(8,128)(2,1)S(1)}, u32[]{:S(2)}, u32[]{:S(2)}) collective-permute-start(bf16[6,72,128]{2,1,0:T(8,128)(2,1)S(1)} %get-tuple-element.119), channel_id=1, source_target_pairs={{0,20},{4,16},{16,4},{20,0},{1,21},{5,17},{17,5},{21,1},{2,22},{6,... | collective-permute-start | bytes 331784 | tf_op jit(solution)/shard_map/ppermute | solution.py:555
  89.2 0.4 collective-permute-start.20
  89.6 1.3 %collective-permute-start.21 = (bf16[3,72,128]{2,1,0:T(8,128)(2,1)S(1)}, bf16[3,72,128]{2,1,0:T(8,128)(2,1)S(1)}, u32[]{:S(2)}, u32[]{:S(2)}) collective-permute-start(bf16[3,72,128]{2,1,0:T(8,128)(2,1)S(1)} %get-tuple-element.115), channel_id=1, source_target_pairs={{0,2},{1,3},{2,0},{3,1},{4,6},{5,7},{6,4},{7,5},{8,10},{9,11},{10,... | collective-permute-start | bytes 165896 | tf_op jit(solution)/shard_map/ppermute | solution.py:490
  90.8 0.5 collective-permute-start.22
  91.4 2.0 %collective-permute-done.25.refs_7_ = bf16[6,72,128]{2,1,0:T(8,128)(2,1)S(1)} collective-permute-done((bf16[6,72,128]{2,1,0:T(8,128)(2,1)S(1)}, bf16[6,72,128]{2,1,0:T(8,128)(2,1)S(1)}, u32[]{:S(2)}, u32[]{:S(2)}) %collective-permute-start.25) | collective-permute-done | bytes 110624 | tf_op jit(solution)/shard_map/ppermute | solution.py:555
  93.4 2.1 %collective-permute-done.21.refs_2_ = bf16[3,72,128]{2,1,0:T(8,128)(2,1)S(1)} collective-permute-done((bf16[3,72,128]{2,1,0:T(8,128)(2,1)S(1)}, bf16[3,72,128]{2,1,0:T(8,128)(2,1)S(1)}, u32[]{:S(2)}, u32[]{:S(2)}) %collective-permute-start.21) | collective-permute-done | bytes 55328 | tf_op jit(solution)/shard_map/ppermute | solution.py:490
  95.5 0.7 collective-permute-done.22.refs_3_
  96.2 0.7 shard_map.154
  97.0 9.0 %all-to-all-start = ((bf16[8,72,128]{2,1,0:T(8,128)(2,1)}), bf16[8,72,128]{2,1,0:T(8,128)(2,1)S(1)}, u32[]{:S(2)}, u32[]{:S(2)}) async-start(bf16[8,72,128]{2,1,0:T(8,128)(2,1)} %shard_map.154), calls=%async_computation | async-start | bytes 294912 | tf_op jit(solution)/shard_map/all_to_all | solution.py:671
  106.0 1.2 shard_map.146
  107.1 8.1 %all-to-all-done.parts = bf16[8,72,128]{2,1,0:T(8,128)(2,1)S(1)} async-done(((bf16[8,72,128]{2,1,0:T(8,128)(2,1)}), bf16[8,72,128]{2,1,0:T(8,128)(2,1)S(1)}, u32[]{:S(2)}, u32[]{:S(2)}) %all-to-all-start) | async-done | bytes 147488 | tf_op jit(solution)/shard_map/all_to_all | solution.py:671
  115.3 0.6 slice_bitcast_fusion
  (47 shorter events, 1.4 us)
Async XLA Ops:
  1.3 0.9 copy-start.6
  2.2 0.7 copy-start.10
  2.9 8.4 %copy-start.3 = (bf16[400,800]{1,0:T(8,128)(2,1)S(1)}, bf16[400,800]{1,0:T(8,128)(2,1)}, u32[]{:S(2)}) copy-start(bf16[400,800]{1,0:T(8,128)(2,1)} %w_up.3) | copy-start | bytes 1920004
  2.9 8.4 %copy-start.7 = (bf16[1,2,16,3200]{3,2,1,0:T(8,128)(2,1)S(1)}, bf16[1,2,16,3200]{3,2,1,0:T(8,128)(2,1)}, u32[]{:S(2)}) copy-start(bf16[1,2,16,3200]{3,2,1,0:T(8,128)(2,1)} %param.25) | copy-start | bytes 614404
  3.4 9.6 %collective-permute-start = (bf16[2,3,16,200]{3,2,1,0:T(8,128)(2,1)S(1)}, bf16[2,3,16,200]{3,2,1,0:T(8,128)(2,1)S(1)}, u32[]{:S(2)}, u32[]{:S(2)}) collective-permute-start(bf16[2,3,16,200]{3,2,1,0:T(8,128)(2,1)S(1)} %get-tuple-element.63.east), channel_id=1, source_target_pairs={{0,8},{8,16},{16,24},{24,32},{32,40},{40,48},{48,56},{56,64},{64,7... | collective-permute-start | bytes 115208 | tf_op jit(solution)/shard_map/ppermute | solution.py:490
  3.5 9.6 %collective-permute-start.1 = (bf16[2,3,16,200]{3,2,1,0:T(8,128)(2,1)S(1)}, bf16[2,3,16,200]{3,2,1,0:T(8,128)(2,1)S(1)}, u32[]{:S(2)}, u32[]{:S(2)}) collective-permute-start(bf16[2,3,16,200]{3,2,1,0:T(8,128)(2,1)S(1)} %get-tuple-element.62.west), channel_id=1, source_target_pairs={{0,248},{8,0},{16,8},{24,16},{32,24},{40,32},{48,40},{56,48},{64,5... | collective-permute-start | bytes 115208 | tf_op jit(solution)/shard_map/ppermute | solution.py:490
  11.3 1.7 %copy-start.11 = (s32[1,2,4]{2,1,0:T(2,128)S(1)}, s32[1,2,4]{2,1,0:T(2,128)}, u32[]{:S(2)}) copy-start(s32[1,2,4]{2,1,0:T(2,128)} %param.16) | copy-start | bytes 100
  13.1 7.2 %copy-start.2 = (bf16[800,400]{0,1:T(8,128)(2,1)S(1)}, bf16[800,400]{0,1:T(8,128)(2,1)}, u32[]{:S(2)}) copy-start(bf16[800,400]{0,1:T(8,128)(2,1)} %param.20) | copy-start | bytes 1920004
  13.1 7.2 %copy-start.4 = (bf16[200,800]{1,0:T(8,128)(2,1)S(1)}, bf16[200,800]{1,0:T(8,128)(2,1)}, u32[]{:S(2)}) copy-start(bf16[200,800]{1,0:T(8,128)(2,1)} %w_in.5) | copy-start | bytes 960004
  13.1 7.2 %copy-start.5 = (bf16[800,200]{0,1:T(8,128)(2,1)S(1)}, bf16[800,200]{0,1:T(8,128)(2,1)}, u32[]{:S(2)}) copy-start(bf16[800,200]{0,1:T(8,128)(2,1)} %param.19) | copy-start | bytes 960004
  13.1 7.2 %copy-start.9 = (bf16[7,7,200]{2,1,0:T(8,128)(2,1)S(1)}, bf16[7,7,200]{2,1,0:T(8,128)(2,1)}, u32[]{:S(2)}) copy-start(bf16[7,7,200]{2,1,0:T(8,128)(2,1)} %kern.3) | copy-start | bytes 58804
  13.8 4.1 %collective-permute-start.2 = (bf16[22,3,200]{2,1,0:T(4,128)(2,1)S(1)}, bf16[22,3,200]{2,1,0:T(4,128)(2,1)S(1)}, u32[]{:S(2)}, u32[]{:S(2)}) collective-permute-start(bf16[22,3,200]{2,1,0:T(4,128)(2,1)S(1)} %get-tuple-element.65), channel_id=1, source_target_pairs={{0,1},{1,2},{2,3},{3,4},{4,5},{5,6},{6,7},{7,0},{8,9},{9,10},{10,1... | collective-permute-start | bytes 79208 | tf_op jit(solution)/shard_map/ppermute | solution.py:490
  14.2 6.2 %collective-permute-start.3 = (bf16[22,3,200]{2,1,0:T(4,128)(2,1)S(1)}, bf16[22,3,200]{2,1,0:T(4,128)(2,1)S(1)}, u32[]{:S(2)}, u32[]{:S(2)}) collective-permute-start(bf16[22,3,200]{2,1,0:T(4,128)(2,1)S(1)} %get-tuple-element.66), channel_id=1, source_target_pairs={{0,7},{1,0},{2,1},{3,2},{4,3},{5,4},{6,5},{7,6},{8,15},{9,8},{10,9... | collective-permute-start | bytes 79208 | tf_op jit(solution)/shard_map/ppermute | solution.py:490
  25.0 7.3 %collective-permute-start.4 = (bf16[2,3,8,400]{3,2,1,0:T(8,128)(2,1)S(1)}, bf16[2,3,8,400]{3,2,1,0:T(8,128)(2,1)S(1)}, u32[]{:S(2)}, u32[]{:S(2)}) collective-permute-start(bf16[2,3,8,400]{3,2,1,0:T(8,128)(2,1)S(1)} %get-tuple-element.72.east), channel_id=1, source_target_pairs={{0,8},{8,16},{16,24},{24,32},{32,40},{40,48},{48,56},{56,64},{64,7... | collective-permute-start | bytes 115208 | tf_op jit(solution)/shard_map/ppermute | solution.py:490
  25.1 7.2 %collective-permute-start.5 = (bf16[2,3,8,400]{3,2,1,0:T(8,128)(2,1)S(1)}, bf16[2,3,8,400]{3,2,1,0:T(8,128)(2,1)S(1)}, u32[]{:S(2)}, u32[]{:S(2)}) collective-permute-start(bf16[2,3,8,400]{3,2,1,0:T(8,128)(2,1)S(1)} %get-tuple-element.71.west), channel_id=1, source_target_pairs={{0,248},{8,0},{16,8},{24,16},{32,24},{40,32},{48,40},{56,48},{64,5... | collective-permute-start | bytes 115208 | tf_op jit(solution)/shard_map/ppermute | solution.py:490
  32.3 7.2 %copy-start = (bf16[400,1600]{1,0:T(8,128)(2,1)S(1)}, bf16[400,1600]{1,0:T(8,128)(2,1)}, u32[]{:S(2)}) copy-start(bf16[400,1600]{1,0:T(8,128)(2,1)} %w_in.4) | copy-start | bytes 3840004
  32.3 7.2 %copy-start.1 = (bf16[1600,400]{0,1:T(8,128)(2,1)S(1)}, bf16[1600,400]{0,1:T(8,128)(2,1)}, u32[]{:S(2)}) copy-start(bf16[1600,400]{0,1:T(8,128)(2,1)} %param.23) | copy-start | bytes 3840004
  32.3 7.2 %copy-start.8 = (bf16[7,7,400]{2,1,0:T(8,128)(2,1)S(1)}, bf16[7,7,400]{2,1,0:T(8,128)(2,1)}, u32[]{:S(2)}) copy-start(bf16[7,7,400]{2,1,0:T(8,128)(2,1)} %kern.5) | copy-start | bytes 117604
  33.1 4.3 %collective-permute-start.6 = (bf16[14,3,400]{2,1,0:T(4,128)(2,1)S(1)}, bf16[14,3,400]{2,1,0:T(4,128)(2,1)S(1)}, u32[]{:S(2)}, u32[]{:S(2)}) collective-permute-start(bf16[14,3,400]{2,1,0:T(4,128)(2,1)S(1)} %get-tuple-element.74), channel_id=1, source_target_pairs={{0,1},{1,2},{2,3},{3,4},{4,5},{5,6},{6,7},{7,0},{8,9},{9,10},{10,1... | collective-permute-start | bytes 100808 | tf_op jit(solution)/shard_map/ppermute | solution.py:490
  33.1 6.4 %collective-permute-start.7 = (bf16[14,3,400]{2,1,0:T(4,128)(2,1)S(1)}, bf16[14,3,400]{2,1,0:T(4,128)(2,1)S(1)}, u32[]{:S(2)}, u32[]{:S(2)}) collective-permute-start(bf16[14,3,400]{2,1,0:T(4,128)(2,1)S(1)} %get-tuple-element.75), channel_id=1, source_target_pairs={{0,7},{1,0},{2,1},{3,2},{4,3},{5,4},{6,5},{7,6},{8,15},{9,8},{10,9... | collective-permute-start | bytes 100808 | tf_op jit(solution)/shard_map/ppermute | solution.py:490
  43.5 9.3 %collective-permute-start.8 = (bf16[2,3,8,400]{3,2,1,0:T(8,128)(2,1)S(1)}, bf16[2,3,8,400]{3,2,1,0:T(8,128)(2,1)S(1)}, u32[]{:S(2)}, u32[]{:S(2)}) collective-permute-start(bf16[2,3,8,400]{3,2,1,0:T(8,128)(2,1)S(1)} %get-tuple-element.80.east), channel_id=1, source_target_pairs={{0,8},{8,16},{16,24},{24,32},{32,40},{40,48},{48,56},{56,64},{64,7... | collective-permute-start | bytes 115208 | tf_op jit(solution)/shard_map/ppermute | solution.py:490
  43.8 9.0 %collective-permute-start.9 = (bf16[2,3,8,400]{3,2,1,0:T(8,128)(2,1)S(1)}, bf16[2,3,8,400]{3,2,1,0:T(8,128)(2,1)S(1)}, u32[]{:S(2)}, u32[]{:S(2)}) collective-permute-start(bf16[2,3,8,400]{3,2,1,0:T(8,128)(2,1)S(1)} %get-tuple-element.79.west), channel_id=1, source_target_pairs={{0,248},{8,0},{16,8},{24,16},{32,24},{40,32},{48,40},{56,48},{64,5... | collective-permute-start | bytes 115208 | tf_op jit(solution)/shard_map/ppermute | solution.py:490
  52.8 3.8 %collective-permute-start.12 = (bf16[16,6,72,128]{3,2,1,0:T(8,128)(2,1)S(1)}, bf16[16,6,72,128]{3,2,1,0:T(8,128)(2,1)S(1)}, u32[]{:S(2)}, u32[]{:S(2)}) collective-permute-start(bf16[16,6,72,128]{3,2,1,0:T(8,128)(2,1)S(1)} %get-tuple-element.99), channel_id=1, source_target_pairs={{0,8},{8,0},{1,9},{9,1},{2,10},{10,2},{3,11},{11,3},{4,12},{12,4},... | collective-permute-start | bytes 5308424 | tf_op jit(solution)/shard_map/ppermute | solution.py:501
  53.7 5.4 %collective-permute-start.10 = (bf16[14,3,400]{2,1,0:T(4,128)(2,1)S(1)}, bf16[14,3,400]{2,1,0:T(4,128)(2,1)S(1)}, u32[]{:S(2)}, u32[]{:S(2)}) collective-permute-start(bf16[14,3,400]{2,1,0:T(4,128)(2,1)S(1)} %get-tuple-element.90), channel_id=1, source_target_pairs={{0,1},{1,2},{2,3},{3,4},{4,5},{5,6},{6,7},{7,0},{8,9},{9,10},{10,1... | collective-permute-start | bytes 100808 | tf_op jit(solution)/shard_map/ppermute | solution.py:490
  53.8 6.5 %collective-permute-start.11 = (bf16[14,3,400]{2,1,0:T(4,128)(2,1)S(1)}, bf16[14,3,400]{2,1,0:T(4,128)(2,1)S(1)}, u32[]{:S(2)}, u32[]{:S(2)}) collective-permute-start(bf16[14,3,400]{2,1,0:T(4,128)(2,1)S(1)} %get-tuple-element.91), channel_id=1, source_target_pairs={{0,7},{1,0},{2,1},{3,2},{4,3},{5,4},{6,5},{7,6},{8,15},{9,8},{10,9... | collective-permute-start | bytes 100808 | tf_op jit(solution)/shard_map/ppermute | solution.py:490
  57.0 11.5 %collective-permute-start.13 = (bf16[22,72,128]{2,1,0:T(8,128)(2,1)S(1)}, bf16[22,72,128]{2,1,0:T(8,128)(2,1)S(1)}, u32[]{:S(2)}, u32[]{:S(2)}) collective-permute-start(bf16[22,72,128]{2,1,0:T(8,128)(2,1)S(1)} %get-tuple-element.100), channel_id=1, source_target_pairs={{0,1},{1,2},{2,3},{3,0},{4,5},{5,6},{6,7},{7,4},{8,9},{9,10},{10,1... | collective-permute-start | bytes 1216520 | tf_op jit(solution)/shard_map/ppermute | solution.py:490
  58.3 12.4 %collective-permute-start.14 = (bf16[22,72,128]{2,1,0:T(8,128)(2,1)S(1)}, bf16[22,72,128]{2,1,0:T(8,128)(2,1)S(1)}, u32[]{:S(2)}, u32[]{:S(2)}) collective-permute-start(bf16[22,72,128]{2,1,0:T(8,128)(2,1)S(1)} %get-tuple-element.101), channel_id=1, source_target_pairs={{0,3},{1,0},{2,1},{3,2},{4,7},{5,4},{6,5},{7,6},{8,11},{9,8},{10,9... | collective-permute-start | bytes 1216520 | tf_op jit(solution)/shard_map/ppermute | solution.py:490
  70.8 2.4 %collective-permute-start.15 = (bf16[16,3,72,128]{3,2,1,0:T(8,128)(2,1)S(1)}, bf16[16,3,72,128]{3,2,1,0:T(8,128)(2,1)S(1)}, u32[]{:S(2)}, u32[]{:S(2)}) collective-permute-start(bf16[16,3,72,128]{3,2,1,0:T(8,128)(2,1)S(1)} %get-tuple-element.102), channel_id=1, source_target_pairs={{0,8},{8,0},{1,9},{9,1},{2,10},{10,2},{3,11},{11,3},{4,12},{12,4},... | collective-permute-start | bytes 2654216 | tf_op jit(solution)/shard_map/ppermute | solution.py:501
  70.8 13.3 %collective-permute-start.17 = (bf16[22,72,128]{2,1,0:T(8,128)(2,1)S(1)}, bf16[22,72,128]{2,1,0:T(8,128)(2,1)S(1)}, u32[]{:S(2)}, u32[]{:S(2)}) collective-permute-start(bf16[22,72,128]{2,1,0:T(8,128)(2,1)S(1)} %get-tuple-element.107), channel_id=1, source_target_pairs={{0,2},{1,3},{2,0},{3,1},{4,6},{5,7},{6,4},{7,5},{8,10},{9,11},{10,... | collective-permute-start | bytes 1216520 | tf_op jit(solution)/shard_map/ppermute | solution.py:490
  73.4 11.7 %collective-permute-start.16 = (bf16[4,3,72,128]{3,2,1,0:T(8,128)(2,1)S(1)}, bf16[4,3,72,128]{3,2,1,0:T(8,128)(2,1)S(1)}, u32[]{:S(2)}, u32[]{:S(2)}) collective-permute-start(bf16[4,3,72,128]{3,2,1,0:T(8,128)(2,1)S(1)} %get-tuple-element.104), channel_id=1, source_target_pairs={{0,4},{4,0},{16,20},{20,16},{1,5},{5,1},{17,21},{21,17},{2,6},{6,2... | collective-permute-start | bytes 663560 | tf_op jit(solution)/shard_map/ppermute | solution.py:555
  74.2 14.9 %collective-permute-start.18 = (bf16[4,3,72,128]{3,2,1,0:T(8,128)(2,1)S(1)}, bf16[4,3,72,128]{3,2,1,0:T(8,128)(2,1)S(1)}, u32[]{:S(2)}, u32[]{:S(2)}) collective-permute-start(bf16[4,3,72,128]{3,2,1,0:T(8,128)(2,1)S(1)} %get-tuple-element.111), channel_id=1, source_target_pairs={{0,16},{4,20},{16,0},{20,4},{1,17},{5,21},{17,1},{21,5},{2,18},{6,... | collective-permute-start | bytes 663560 | tf_op jit(solution)/shard_map/ppermute | solution.py:555
  74.2 14.9 %collective-permute-start.19 = (bf16[4,3,72,128]{3,2,1,0:T(8,128)(2,1)S(1)}, bf16[4,3,72,128]{3,2,1,0:T(8,128)(2,1)S(1)}, u32[]{:S(2)}, u32[]{:S(2)}) collective-permute-start(bf16[4,3,72,128]{3,2,1,0:T(8,128)(2,1)S(1)} %get-tuple-element.112), channel_id=1, source_target_pairs={{0,20},{4,16},{16,4},{20,0},{1,21},{5,17},{17,5},{21,1},{2,22},{6,... | collective-permute-start | bytes 663560 | tf_op jit(solution)/shard_map/ppermute | solution.py:555
  84.3 6.5 %collective-permute-start.23 = (bf16[6,72,128]{2,1,0:T(8,128)(2,1)S(1)}, bf16[6,72,128]{2,1,0:T(8,128)(2,1)S(1)}, u32[]{:S(2)}, u32[]{:S(2)}) collective-permute-start(bf16[6,72,128]{2,1,0:T(8,128)(2,1)S(1)} %get-tuple-element.109), channel_id=1, source_target_pairs={{0,4},{4,0},{16,20},{20,16},{1,5},{5,1},{17,21},{21,17},{2,6},{6,2... | collective-permute-start | bytes 331784 | tf_op jit(solution)/shard_map/ppermute | solution.py:555
  85.1 6.3 %collective-permute-start.24 = (bf16[6,72,128]{2,1,0:T(8,128)(2,1)S(1)}, bf16[6,72,128]{2,1,0:T(8,128)(2,1)S(1)}, u32[]{:S(2)}, u32[]{:S(2)}) collective-permute-start(bf16[6,72,128]{2,1,0:T(8,128)(2,1)S(1)} %get-tuple-element.118), channel_id=1, source_target_pairs={{0,16},{4,20},{16,0},{20,4},{1,17},{5,21},{17,1},{21,5},{2,18},{6,... | collective-permute-start | bytes 331784 | tf_op jit(solution)/shard_map/ppermute | solution.py:555
  85.1 8.3 %collective-permute-start.25 = (bf16[6,72,128]{2,1,0:T(8,128)(2,1)S(1)}, bf16[6,72,128]{2,1,0:T(8,128)(2,1)S(1)}, u32[]{:S(2)}, u32[]{:S(2)}) collective-permute-start(bf16[6,72,128]{2,1,0:T(8,128)(2,1)S(1)} %get-tuple-element.119), channel_id=1, source_target_pairs={{0,20},{4,16},{16,4},{20,0},{1,21},{5,17},{17,5},{21,1},{2,22},{6,... | collective-permute-start | bytes 331784 | tf_op jit(solution)/shard_map/ppermute | solution.py:555
  89.2 4.2 %collective-permute-start.20 = (bf16[3,72,128]{2,1,0:T(8,128)(2,1)S(1)}, bf16[3,72,128]{2,1,0:T(8,128)(2,1)S(1)}, u32[]{:S(2)}, u32[]{:S(2)}) collective-permute-start(bf16[3,72,128]{2,1,0:T(8,128)(2,1)S(1)} %get-tuple-element.114), channel_id=1, source_target_pairs={{0,1},{1,2},{2,3},{3,0},{4,5},{5,6},{6,7},{7,4},{8,9},{9,10},{10,1... | collective-permute-start | bytes 165896 | tf_op jit(solution)/shard_map/ppermute | solution.py:490
  89.6 6.0 %collective-permute-start.21 = (bf16[3,72,128]{2,1,0:T(8,128)(2,1)S(1)}, bf16[3,72,128]{2,1,0:T(8,128)(2,1)S(1)}, u32[]{:S(2)}, u32[]{:S(2)}) collective-permute-start(bf16[3,72,128]{2,1,0:T(8,128)(2,1)S(1)} %get-tuple-element.115), channel_id=1, source_target_pairs={{0,2},{1,3},{2,0},{3,1},{4,6},{5,7},{6,4},{7,5},{8,10},{9,11},{10,... | collective-permute-start | bytes 165896 | tf_op jit(solution)/shard_map/ppermute | solution.py:490
  90.8 5.4 %collective-permute-start.22 = (bf16[3,72,128]{2,1,0:T(8,128)(2,1)S(1)}, bf16[3,72,128]{2,1,0:T(8,128)(2,1)S(1)}, u32[]{:S(2)}, u32[]{:S(2)}) collective-permute-start(bf16[3,72,128]{2,1,0:T(8,128)(2,1)S(1)} %get-tuple-element.116), channel_id=1, source_target_pairs={{0,3},{1,0},{2,1},{3,2},{4,7},{5,4},{6,5},{7,6},{8,11},{9,8},{10,9... | collective-permute-start | bytes 165896 | tf_op jit(solution)/shard_map/ppermute | solution.py:490
  97.0 18.3 %all-to-all-start = ((bf16[8,72,128]{2,1,0:T(8,128)(2,1)}), bf16[8,72,128]{2,1,0:T(8,128)(2,1)S(1)}, u32[]{:S(2)}, u32[]{:S(2)}) async-start(bf16[8,72,128]{2,1,0:T(8,128)(2,1)} %shard_map.154), calls=%async_computation | async-start | bytes 294912 | tf_op jit(solution)/shard_map/all_to_all | solution.py:671

commit v3 on v1

--- a/solution.py
+++ b/solution.py
@@ -648,7 +648,7 @@
         ],
         room=16, us=10, smem=1,
     )(entries, *sides, kern_two, change, mask_two, mask_cat, cot_cat, blocks, w_down, w_in_one, w_out_one, normed_one, scales_one, field_one_own)
-    send_one, parts_two[1], parts_two[3] = lax.optimization_barrier((send_one, parts_two[1], parts_two[3]))
+    send_one, parts_two[1] = lax.optimization_barrier((send_one, parts_two[1]))
     return prediction[None], finish(keep_one, send_one, parts_two)
 
 

time: 115 us -> 123 us (1.070)
  waiting for transfers between devices: 38.7 us -> 43.1 us
  starting transfers between devices: 46 us -> 49.3 us
    ppermute x18, waiting for transfers between devices: 25.3 us -> 32 us  [around(): lax.ppermute(array, axes, [(i, (i + step) % size) for i in range(size)])]
    ppermute x18, starting transfers between devices: 29.5 us -> 32.8 us  [around(): lax.ppermute(array, axes, [(i, (i + step) % size) for i in range(size)])]
    ppermute x2, waiting for transfers between devices: 3.25 us -> 0.83 us  [other_core(): return lax.ppermute(send, 'c', [(0, 1), (1, 0)])]
  transfers between devices with their start and end apart: 27 -> 27, of which waited for: 19 -> 17; matrix products, arithmetic and copies ran while one was open for 0% -> 0% of each run, Pallas kernels for 13% -> 13%
where the time goes in v3:
time: 123 us
  starting transfers between devices  49.3 us (40%)
  waiting for transfers between devices  43.1 us (35%)
  Pallas kernels  26.7 us (22%)
  local copies, waits for them, and re-layouts  2.26 us (2%)
  between operations  1.5 us (1%)
    ppermute x18, starting transfers between devices, around(): lax.ppermute(array, axes, [(i, (i + step) % size) for i in range(size)])  32.8 us
    ppermute x18, waiting for transfers between devices, around(): lax.ppermute(array, axes, [(i, (i + step) % size) for i in range(size)])  32 us
    pallas_call x16, Pallas kernels, run(): pl.pallas_call(body, out_shape=[jax.ShapeDtypeStruct(shape, kind) for sha...  26.7 us
    ppermute x6, starting transfers between devices, over_x(): lax.ppermute(parts[k], ('xh', 'xl'), [(i, i ^ k) for i in range(4)])  9.57 us
    all_to_all x1, waiting for transfers between devices, finish(): total = lax.all_to_all(total, 'z', 0, 0)  8.1 us
    all_to_all x1, starting transfers between devices, finish(): total = lax.all_to_all(total, 'z', 0, 0)  6.84 us
  transfers between devices with their start and end apart: 27, of which 17 were waited for; matrix products, arithmetic and copies ran while one was open for 0% of the time, Pallas kernels for 13%

profile of v3, /device:TPU:24, one launch (start us, length us, event | category | flops | bytes accessed | tf_op | source)
XLA Modules:
  0.0 122.8 jit_solution(6086822047116042836)
XLA Ops:
  1.3 0.9 copy-done.6
  2.2 0.7 copy-done.10
  2.9 0.5 shard_map.141
  3.5 7.8 %collective-permute-start.1 = (bf16[2,3,16,200]{3,2,1,0:T(8,128)(2,1)S(1)}, bf16[2,3,16,200]{3,2,1,0:T(8,128)(2,1)S(1)}, u32[]{:S(2)}, u32[]{:S(2)}) collective-permute-start(bf16[2,3,16,200]{3,2,1,0:T(8,128)(2,1)S(1)} %get-tuple-element.60.west), channel_id=1, source_target_pairs={{0,248},{8,0},{16,8},{24,16},{32,24},{40,32},{48,40},{56,48},{64,5... | collective-permute-start | bytes 115208 | tf_op jit(solution)/shard_map/ppermute | solution.py:488
  11.3 1.0 shard_map.140
  12.3 0.7 collective-permute-done.west_got
  13.1 0.7 shard_map.142
  13.8 0.3 collective-permute-start.2
  14.2 1.8 %collective-permute-start.3 = (bf16[22,3,200]{2,1,0:T(4,128)(2,1)S(1)}, bf16[22,3,200]{2,1,0:T(4,128)(2,1)S(1)}, u32[]{:S(2)}, u32[]{:S(2)}) collective-permute-start(bf16[22,3,200]{2,1,0:T(4,128)(2,1)S(1)} %get-tuple-element.64), channel_id=1, source_target_pairs={{0,7},{1,0},{2,1},{3,2},{4,3},{5,4},{6,5},{7,6},{8,15},{9,8},{10,9... | collective-permute-start | bytes 79208 | tf_op jit(solution)/shard_map/ppermute | solution.py:488
  15.9 2.0 %collective-permute-done.2.top_got = bf16[22,3,200]{2,1,0:T(4,128)(2,1)S(1)} collective-permute-done((bf16[22,3,200]{2,1,0:T(4,128)(2,1)S(1)}, bf16[22,3,200]{2,1,0:T(4,128)(2,1)S(1)}, u32[]{:S(2)}, u32[]{:S(2)}) %collective-permute-start.2) | collective-permute-done | bytes 26432 | tf_op jit(solution)/shard_map/ppermute | solution.py:488
  18.0 2.4 %collective-permute-done.3.bottom_got = bf16[22,3,200]{2,1,0:T(4,128)(2,1)S(1)} collective-permute-done((bf16[22,3,200]{2,1,0:T(4,128)(2,1)S(1)}, bf16[22,3,200]{2,1,0:T(4,128)(2,1)S(1)}, u32[]{:S(2)}, u32[]{:S(2)}) %collective-permute-start.3) | collective-permute-done | bytes 26432 | tf_op jit(solution)/shard_map/ppermute | solution.py:488
  20.3 4.5 %shard_map.143 = (f32[2,2,22,24,128]{4,3,2,1,0:T(8,128)S(1)}, f32[512,256]{1,0:T(8,128)S(1)}, f32[512,128]{1,0:T(8,128)S(1)}, bf16[128,800]{1,0:T(8,128)(2,1)S(1...) custom-call(s32[2,4]{1,0:T(2,128)S(1)} %bitcast.21, ...), custom_call_target="tpu_custom_call" | custom-call | flops 6000000000 | bytes 1000000 | tf_op jit(solution)/shard_map/pallas_call | solution.py:32
  25.0 5.3 %collective-permute-start.5 = (bf16[2,3,8,400]{3,2,1,0:T(8,128)(2,1)S(1)}, bf16[2,3,8,400]{3,2,1,0:T(8,128)(2,1)S(1)}, u32[]{:S(2)}, u32[]{:S(2)}) collective-permute-start(bf16[2,3,8,400]{3,2,1,0:T(8,128)(2,1)S(1)} %get-tuple-element.69.west), channel_id=1, source_target_pairs={{0,248},{8,0},{16,8},{24,16},{32,24},{40,32},{48,40},{56,48},{64,5... | collective-permute-start | bytes 115208 | tf_op jit(solution)/shard_map/ppermute | solution.py:488
  30.3 1.9 %collective-permute-done.4.west_got = bf16[2,3,8,400]{3,2,1,0:T(8,128)(2,1)S(1)} collective-permute-done((bf16[2,3,8,400]{3,2,1,0:T(8,128)(2,1)S(1)}, bf16[2,3,8,400]{3,2,1,0:T(8,128)(2,1)S(1)}, u32[]{:S(2)}, u32[]{:S(2)}) %collective-permute-start.4) | collective-permute-done | bytes 38432 | tf_op jit(solution)/shard_map/ppermute | solution.py:488
  32.2 0.7 shard_map.144
  33.1 2.0 %collective-permute-start.7 = (bf16[14,3,400]{2,1,0:T(4,128)(2,1)S(1)}, bf16[14,3,400]{2,1,0:T(4,128)(2,1)S(1)}, u32[]{:S(2)}, u32[]{:S(2)}) collective-permute-start(bf16[14,3,400]{2,1,0:T(4,128)(2,1)S(1)} %get-tuple-element.73), channel_id=1, source_target_pairs={{0,7},{1,0},{2,1},{3,2},{4,3},{5,4},{6,5},{7,6},{8,15},{9,8},{10,9... | collective-permute-start | bytes 100808 | tf_op jit(solution)/shard_map/ppermute | solution.py:488
  35.1 2.2 %collective-permute-done.6.top_got = bf16[14,3,400]{2,1,0:T(4,128)(2,1)S(1)} collective-permute-done((bf16[14,3,400]{2,1,0:T(4,128)(2,1)S(1)}, bf16[14,3,400]{2,1,0:T(4,128)(2,1)S(1)}, u32[]{:S(2)}, u32[]{:S(2)}) %collective-permute-start.6) | collective-permute-done | bytes 33632 | tf_op jit(solution)/shard_map/ppermute | solution.py:488
  37.2 2.2 %collective-permute-done.7.bottom_got = bf16[14,3,400]{2,1,0:T(4,128)(2,1)S(1)} collective-permute-done((bf16[14,3,400]{2,1,0:T(4,128)(2,1)S(1)}, bf16[14,3,400]{2,1,0:T(4,128)(2,1)S(1)}, u32[]{:S(2)}, u32[]{:S(2)}) %collective-permute-start.7) | collective-permute-done | bytes 33632 | tf_op jit(solution)/shard_map/ppermute | solution.py:488
  39.4 4.0 %shard_map.145 = (f32[2,4,14,16,128]{4,3,2,1,0:T(8,128)S(1)}, bf16[128,400]{1,0:T(8,128)(2,1)S(1)}, bf16[128,1600]{1,0:T(8,128)(2,1)S(1)}, bf16[128,1600]{1,0:T(...) custom-call(s32[2,4]{1,0:T(2,128)S(1)} %bitcast.23, ...), custom_call_target="tpu_custom_call" | custom-call | flops 6000000000 | bytes 1000000 | tf_op jit(solution)/shard_map/pallas_call | solution.py:32
  43.7 5.3 %collective-permute-start.9 = (bf16[2,3,8,400]{3,2,1,0:T(8,128)(2,1)S(1)}, bf16[2,3,8,400]{3,2,1,0:T(8,128)(2,1)S(1)}, u32[]{:S(2)}, u32[]{:S(2)}) collective-permute-start(bf16[2,3,8,400]{3,2,1,0:T(8,128)(2,1)S(1)} %get-tuple-element.77.west), channel_id=1, source_target_pairs={{0,248},{8,0},{16,8},{24,16},{32,24},{40,32},{48,40},{56,48},{64,5... | collective-permute-start | bytes 115208 | tf_op jit(solution)/shard_map/ppermute | solution.py:488
  49.0 3.6 %shard_map.147 = (bf16[16,6,72,128]{3,2,1,0:T(8,128)(2,1)S(1)}, bf16[16,6,72,128]{3,2,1,0:T(8,128)(2,1)S(1)}) custom-call(f32[2,4,14,16,128]{4,3,2,1,0:T(8,128)S(1)} %get-tuple-element.79.field, bf16[128,400]{1,0:T(8,128)(2,1)S(1)} %get-tuple-element.76.back.rows, bf16[128,400]{1,0:T(8,128)(2,1)S(1)} %get-tuple-element.80.normed_b, ...), custom_call_target="tpu_custom_call" | custom-call | flops 7000000000 | bytes 1000000 | tf_op jit(solution)/shard_map/pallas_call | solution.py:32
  52.8 0.7 shard_map.148
  53.6 2.0 %collective-permute-start.11 = (bf16[14,3,400]{2,1,0:T(4,128)(2,1)S(1)}, bf16[14,3,400]{2,1,0:T(4,128)(2,1)S(1)}, u32[]{:S(2)}, u32[]{:S(2)}) collective-permute-start(bf16[14,3,400]{2,1,0:T(4,128)(2,1)S(1)} %get-tuple-element.89), channel_id=1, source_target_pairs={{0,7},{1,0},{2,1},{3,2},{4,3},{5,4},{6,5},{7,6},{8,15},{9,8},{10,9... | collective-permute-start | bytes 100808 | tf_op jit(solution)/shard_map/ppermute | solution.py:488
  55.6 0.8 collective-permute-done.12.got
  56.5 0.4 shard_map.150
  56.9 1.6 %collective-permute-start.13 = (bf16[4,6,72,128]{3,2,1,0:T(8,128)(2,1)S(1)}, bf16[4,6,72,128]{3,2,1,0:T(8,128)(2,1)S(1)}, u32[]{:S(2)}, u32[]{:S(2)}) collective-permute-start(bf16[4,6,72,128]{3,2,1,0:T(8,128)(2,1)S(1)} %get-tuple-element.97), channel_id=1, source_target_pairs={{0,1},{1,2},{2,3},{3,0},{4,5},{5,6},{6,7},{7,4},{8,9},{9,10},{10,1... | collective-permute-start | bytes 1327112 | tf_op jit(solution)/shard_map/ppermute | solution.py:488
  58.4 1.7 %collective-permute-done.11.bottom_got = bf16[14,3,400]{2,1,0:T(4,128)(2,1)S(1)} collective-permute-done((bf16[14,3,400]{2,1,0:T(4,128)(2,1)S(1)}, bf16[14,3,400]{2,1,0:T(4,128)(2,1)S(1)}, u32[]{:S(2)}, u32[]{:S(2)}) %collective-permute-start.11) | collective-permute-done | bytes 33632 | tf_op jit(solution)/shard_map/ppermute | solution.py:488
  60.1 8.0 %shard_map.149 = (bf16[16,3,72,128]{3,2,1,0:T(8,128)(2,1)S(1)}, bf16[16,3,72,128]{3,2,1,0:T(8,128)(2,1)S(1)}) custom-call(s32[2,4]{1,0:T(2,128)S(1)} %bitcast.25, f32[2,4,14,16,128]{4,3,2,1,0:T(8,128)S(1)} %get-tuple-element.87.delta, bf16[14,3,400]{2,1,0:T(4,128)(2,1)S(1)} %collective-permute-done.10.top_got, ...), custom_call_target="tpu_custom_call" | custom-call | flops 10000000000 | bytes 1000000 | tf_op jit(solution)/shard_map/pallas_call | solution.py:32
  68.1 1.2 %collective-permute-done.13.refs_1_ = bf16[4,6,72,128]{3,2,1,0:T(8,128)(2,1)S(1)} collective-permute-done((bf16[4,6,72,128]{3,2,1,0:T(8,128)(2,1)S(1)}, bf16[4,6,72,128]{3,2,1,0:T(8,128)(2,1)S(1)}, u32[]{:S(2)}, u32[]{:S(2)}) %collective-permute-start.13) | collective-permute-done | bytes 442400 | tf_op jit(solution)/shard_map/ppermute | solution.py:488
  69.4 1.1 collective-permute-start.16
  70.4 2.3 %collective-permute-start.17 = (bf16[4,6,72,128]{3,2,1,0:T(8,128)(2,1)S(1)}, bf16[4,6,72,128]{3,2,1,0:T(8,128)(2,1)S(1)}, u32[]{:S(2)}, u32[]{:S(2)}) collective-permute-start(bf16[4,6,72,128]{3,2,1,0:T(8,128)(2,1)S(1)} %get-tuple-element.104), channel_id=1, source_target_pairs={{0,3},{1,0},{2,1},{3,2},{4,7},{5,4},{6,5},{7,6},{8,11},{9,8},{10,9... | collective-permute-start | bytes 1327112 | tf_op jit(solution)/shard_map/ppermute | solution.py:488
  73.0 0.8 collective-permute-start.15
  73.8 4.0 %collective-permute-start.19 = (bf16[4,3,72,128]{3,2,1,0:T(8,128)(2,1)S(1)}, bf16[4,3,72,128]{3,2,1,0:T(8,128)(2,1)S(1)}, u32[]{:S(2)}, u32[]{:S(2)}) collective-permute-start(bf16[4,3,72,128]{3,2,1,0:T(8,128)(2,1)S(1)} %get-tuple-element.108), channel_id=1, source_target_pairs={{0,20},{4,16},{16,4},{20,0},{1,21},{5,17},{17,5},{21,1},{2,22},{6,... | collective-permute-start | bytes 663560 | tf_op jit(solution)/shard_map/ppermute | solution.py:548
  77.8 6.1 %collective-permute-done.16.refs_2_ = bf16[4,6,72,128]{3,2,1,0:T(8,128)(2,1)S(1)} collective-permute-done((bf16[4,6,72,128]{3,2,1,0:T(8,128)(2,1)S(1)}, bf16[4,6,72,128]{3,2,1,0:T(8,128)(2,1)S(1)}, u32[]{:S(2)}, u32[]{:S(2)}) %collective-permute-start.16) | collective-permute-done | bytes 442400 | tf_op jit(solution)/shard_map/ppermute | solution.py:488
  83.9 9.1 %collective-permute-done.17.refs_3_ = bf16[4,6,72,128]{3,2,1,0:T(8,128)(2,1)S(1)} collective-permute-done((bf16[4,6,72,128]{3,2,1,0:T(8,128)(2,1)S(1)}, bf16[4,6,72,128]{3,2,1,0:T(8,128)(2,1)S(1)}, u32[]{:S(2)}, u32[]{:S(2)}) %collective-permute-start.17) | collective-permute-done | bytes 442400 | tf_op jit(solution)/shard_map/ppermute | solution.py:488
  93.2 1.3 %collective-permute-start.23 = (bf16[6,72,128]{2,1,0:T(8,128)(2,1)S(1)}, bf16[6,72,128]{2,1,0:T(8,128)(2,1)S(1)}, u32[]{:S(2)}, u32[]{:S(2)}) collective-permute-start(bf16[6,72,128]{2,1,0:T(8,128)(2,1)S(1)} %get-tuple-element.105), channel_id=1, source_target_pairs={{0,4},{4,0},{16,20},{20,16},{1,5},{5,1},{17,21},{21,17},{2,6},{6,2... | collective-permute-start | bytes 331784 | tf_op jit(solution)/shard_map/ppermute | solution.py:548
  94.4 3.5 %collective-permute-start.25 = (bf16[6,72,128]{2,1,0:T(8,128)(2,1)S(1)}, bf16[6,72,128]{2,1,0:T(8,128)(2,1)S(1)}, u32[]{:S(2)}, u32[]{:S(2)}) collective-permute-start(bf16[6,72,128]{2,1,0:T(8,128)(2,1)S(1)} %get-tuple-element.115), channel_id=1, source_target_pairs={{0,20},{4,16},{16,4},{20,0},{1,21},{5,17},{17,5},{21,1},{2,22},{6,... | collective-permute-start | bytes 331784 | tf_op jit(solution)/shard_map/ppermute | solution.py:548
  98.1 0.7 collective-permute-start.20
  98.8 1.1 collective-permute-start.21
  99.8 0.8 collective-permute-start.22
  100.7 2.1 %collective-permute-done.25.refs_7_ = bf16[6,72,128]{2,1,0:T(8,128)(2,1)S(1)} collective-permute-done((bf16[6,72,128]{2,1,0:T(8,128)(2,1)S(1)}, bf16[6,72,128]{2,1,0:T(8,128)(2,1)S(1)}, u32[]{:S(2)}, u32[]{:S(2)}) %collective-permute-start.25) | collective-permute-done | bytes 110624 | tf_op jit(solution)/shard_map/ppermute | solution.py:548
  102.8 1.9 %collective-permute-done.21.refs_2_ = bf16[3,72,128]{2,1,0:T(8,128)(2,1)S(1)} collective-permute-done((bf16[3,72,128]{2,1,0:T(8,128)(2,1)S(1)}, bf16[3,72,128]{2,1,0:T(8,128)(2,1)S(1)}, u32[]{:S(2)}, u32[]{:S(2)}) %collective-permute-start.21) | collective-permute-done | bytes 55328 | tf_op jit(solution)/shard_map/ppermute | solution.py:488
  104.7 0.6 collective-permute-done.22.refs_3_
  105.3 0.7 shard_map.154
  106.1 6.8 %all-to-all-start = ((bf16[8,72,128]{2,1,0:T(8,128)(2,1)}), bf16[8,72,128]{2,1,0:T(8,128)(2,1)S(1)}, u32[]{:S(2)}, u32[]{:S(2)}) async-start(bf16[8,72,128]{2,1,0:T(8,128)(2,1)} %shard_map.154), calls=%async_computation | async-start | bytes 294912 | tf_op jit(solution)/shard_map/all_to_all | solution.py:664
  112.9 1.2 shard_map.146
  114.1 8.1 %all-to-all-done.parts = bf16[8,72,128]{2,1,0:T(8,128)(2,1)S(1)} async-done(((bf16[8,72,128]{2,1,0:T(8,128)(2,1)}), bf16[8,72,128]{2,1,0:T(8,128)(2,1)S(1)}, u32[]{:S(2)}, u32[]{:S(2)}) %all-to-all-start) | async-done | bytes 147488 | tf_op jit(solution)/shard_map/all_to_all | solution.py:664
  122.2 0.6 slice_bitcast_fusion
  (47 shorter events, 1.5 us)
Async XLA Ops:
  1.3 0.9 copy-start.6
  2.2 0.7 copy-start.10
  2.9 8.4 %copy-start.3 = (bf16[400,800]{1,0:T(8,128)(2,1)S(1)}, bf16[400,800]{1,0:T(8,128)(2,1)}, u32[]{:S(2)}) copy-start(bf16[400,800]{1,0:T(8,128)(2,1)} %w_up.3) | copy-start | bytes 1920004
  2.9 8.4 %copy-start.7 = (bf16[1,2,16,3200]{3,2,1,0:T(8,128)(2,1)S(1)}, bf16[1,2,16,3200]{3,2,1,0:T(8,128)(2,1)}, u32[]{:S(2)}) copy-start(bf16[1,2,16,3200]{3,2,1,0:T(8,128)(2,1)} %param.25) | copy-start | bytes 614404
  3.4 9.6 %collective-permute-start = (bf16[2,3,16,200]{3,2,1,0:T(8,128)(2,1)S(1)}, bf16[2,3,16,200]{3,2,1,0:T(8,128)(2,1)S(1)}, u32[]{:S(2)}, u32[]{:S(2)}) collective-permute-start(bf16[2,3,16,200]{3,2,1,0:T(8,128)(2,1)S(1)} %get-tuple-element.61.east), channel_id=1, source_target_pairs={{0,8},{8,16},{16,24},{24,32},{32,40},{40,48},{48,56},{56,64},{64,7... | collective-permute-start | bytes 115208 | tf_op jit(solution)/shard_map/ppermute | solution.py:488
  3.5 9.6 %collective-permute-start.1 = (bf16[2,3,16,200]{3,2,1,0:T(8,128)(2,1)S(1)}, bf16[2,3,16,200]{3,2,1,0:T(8,128)(2,1)S(1)}, u32[]{:S(2)}, u32[]{:S(2)}) collective-permute-start(bf16[2,3,16,200]{3,2,1,0:T(8,128)(2,1)S(1)} %get-tuple-element.60.west), channel_id=1, source_target_pairs={{0,248},{8,0},{16,8},{24,16},{32,24},{40,32},{48,40},{56,48},{64,5... | collective-permute-start | bytes 115208 | tf_op jit(solution)/shard_map/ppermute | solution.py:488
  11.3 1.7 %copy-start.11 = (s32[1,2,4]{2,1,0:T(2,128)S(1)}, s32[1,2,4]{2,1,0:T(2,128)}, u32[]{:S(2)}) copy-start(s32[1,2,4]{2,1,0:T(2,128)} %param.16) | copy-start | bytes 100
  13.1 7.2 %copy-start.2 = (bf16[800,400]{0,1:T(8,128)(2,1)S(1)}, bf16[800,400]{0,1:T(8,128)(2,1)}, u32[]{:S(2)}) copy-start(bf16[800,400]{0,1:T(8,128)(2,1)} %param.20) | copy-start | bytes 1920004
  13.1 7.2 %copy-start.4 = (bf16[200,800]{1,0:T(8,128)(2,1)S(1)}, bf16[200,800]{1,0:T(8,128)(2,1)}, u32[]{:S(2)}) copy-start(bf16[200,800]{1,0:T(8,128)(2,1)} %w_in.5) | copy-start | bytes 960004
  13.1 7.2 %copy-start.5 = (bf16[800,200]{0,1:T(8,128)(2,1)S(1)}, bf16[800,200]{0,1:T(8,128)(2,1)}, u32[]{:S(2)}) copy-start(bf16[800,200]{0,1:T(8,128)(2,1)} %param.19) | copy-start | bytes 960004
  13.1 7.2 %copy-start.9 = (bf16[7,7,200]{2,1,0:T(8,128)(2,1)S(1)}, bf16[7,7,200]{2,1,0:T(8,128)(2,1)}, u32[]{:S(2)}) copy-start(bf16[7,7,200]{2,1,0:T(8,128)(2,1)} %kern.3) | copy-start | bytes 58804
  13.8 4.1 %collective-permute-start.2 = (bf16[22,3,200]{2,1,0:T(4,128)(2,1)S(1)}, bf16[22,3,200]{2,1,0:T(4,128)(2,1)S(1)}, u32[]{:S(2)}, u32[]{:S(2)}) collective-permute-start(bf16[22,3,200]{2,1,0:T(4,128)(2,1)S(1)} %get-tuple-element.63), channel_id=1, source_target_pairs={{0,1},{1,2},{2,3},{3,4},{4,5},{5,6},{6,7},{7,0},{8,9},{9,10},{10,1... | collective-permute-start | bytes 79208 | tf_op jit(solution)/shard_map/ppermute | solution.py:488
  14.2 6.2 %collective-permute-start.3 = (bf16[22,3,200]{2,1,0:T(4,128)(2,1)S(1)}, bf16[22,3,200]{2,1,0:T(4,128)(2,1)S(1)}, u32[]{:S(2)}, u32[]{:S(2)}) collective-permute-start(bf16[22,3,200]{2,1,0:T(4,128)(2,1)S(1)} %get-tuple-element.64), channel_id=1, source_target_pairs={{0,7},{1,0},{2,1},{3,2},{4,3},{5,4},{6,5},{7,6},{8,15},{9,8},{10,9... | collective-permute-start | bytes 79208 | tf_op jit(solution)/shard_map/ppermute | solution.py:488
  24.9 7.3 %collective-permute-start.4 = (bf16[2,3,8,400]{3,2,1,0:T(8,128)(2,1)S(1)}, bf16[2,3,8,400]{3,2,1,0:T(8,128)(2,1)S(1)}, u32[]{:S(2)}, u32[]{:S(2)}) collective-permute-start(bf16[2,3,8,400]{3,2,1,0:T(8,128)(2,1)S(1)} %get-tuple-element.70.east), channel_id=1, source_target_pairs={{0,8},{8,16},{16,24},{24,32},{32,40},{40,48},{48,56},{56,64},{64,7... | collective-permute-start | bytes 115208 | tf_op jit(solution)/shard_map/ppermute | solution.py:488
  25.0 7.2 %collective-permute-start.5 = (bf16[2,3,8,400]{3,2,1,0:T(8,128)(2,1)S(1)}, bf16[2,3,8,400]{3,2,1,0:T(8,128)(2,1)S(1)}, u32[]{:S(2)}, u32[]{:S(2)}) collective-permute-start(bf16[2,3,8,400]{3,2,1,0:T(8,128)(2,1)S(1)} %get-tuple-element.69.west), channel_id=1, source_target_pairs={{0,248},{8,0},{16,8},{24,16},{32,24},{40,32},{48,40},{56,48},{64,5... | collective-permute-start | bytes 115208 | tf_op jit(solution)/shard_map/ppermute | solution.py:488
  32.2 7.2 %copy-start = (bf16[400,1600]{1,0:T(8,128)(2,1)S(1)}, bf16[400,1600]{1,0:T(8,128)(2,1)}, u32[]{:S(2)}) copy-start(bf16[400,1600]{1,0:T(8,128)(2,1)} %w_in.4) | copy-start | bytes 3840004
  32.2 7.2 %copy-start.1 = (bf16[1600,400]{0,1:T(8,128)(2,1)S(1)}, bf16[1600,400]{0,1:T(8,128)(2,1)}, u32[]{:S(2)}) copy-start(bf16[1600,400]{0,1:T(8,128)(2,1)} %param.23) | copy-start | bytes 3840004
  32.2 7.2 %copy-start.8 = (bf16[7,7,400]{2,1,0:T(8,128)(2,1)S(1)}, bf16[7,7,400]{2,1,0:T(8,128)(2,1)}, u32[]{:S(2)}) copy-start(bf16[7,7,400]{2,1,0:T(8,128)(2,1)} %kern.5) | copy-start | bytes 117604
  33.0 4.3 %collective-permute-start.6 = (bf16[14,3,400]{2,1,0:T(4,128)(2,1)S(1)}, bf16[14,3,400]{2,1,0:T(4,128)(2,1)S(1)}, u32[]{:S(2)}, u32[]{:S(2)}) collective-permute-start(bf16[14,3,400]{2,1,0:T(4,128)(2,1)S(1)} %get-tuple-element.72), channel_id=1, source_target_pairs={{0,1},{1,2},{2,3},{3,4},{4,5},{5,6},{6,7},{7,0},{8,9},{9,10},{10,1... | collective-permute-start | bytes 100808 | tf_op jit(solution)/shard_map/ppermute | solution.py:488
  33.1 6.4 %collective-permute-start.7 = (bf16[14,3,400]{2,1,0:T(4,128)(2,1)S(1)}, bf16[14,3,400]{2,1,0:T(4,128)(2,1)S(1)}, u32[]{:S(2)}, u32[]{:S(2)}) collective-permute-start(bf16[14,3,400]{2,1,0:T(4,128)(2,1)S(1)} %get-tuple-element.73), channel_id=1, source_target_pairs={{0,7},{1,0},{2,1},{3,2},{4,3},{5,4},{6,5},{7,6},{8,15},{9,8},{10,9... | collective-permute-start | bytes 100808 | tf_op jit(solution)/shard_map/ppermute | solution.py:488
  43.4 9.2 %collective-permute-start.8 = (bf16[2,3,8,400]{3,2,1,0:T(8,128)(2,1)S(1)}, bf16[2,3,8,400]{3,2,1,0:T(8,128)(2,1)S(1)}, u32[]{:S(2)}, u32[]{:S(2)}) collective-permute-start(bf16[2,3,8,400]{3,2,1,0:T(8,128)(2,1)S(1)} %get-tuple-element.78.east), channel_id=1, source_target_pairs={{0,8},{8,16},{16,24},{24,32},{32,40},{40,48},{48,56},{56,64},{64,7... | collective-permute-start | bytes 115208 | tf_op jit(solution)/shard_map/ppermute | solution.py:488
  43.7 9.0 %collective-permute-start.9 = (bf16[2,3,8,400]{3,2,1,0:T(8,128)(2,1)S(1)}, bf16[2,3,8,400]{3,2,1,0:T(8,128)(2,1)S(1)}, u32[]{:S(2)}, u32[]{:S(2)}) collective-permute-start(bf16[2,3,8,400]{3,2,1,0:T(8,128)(2,1)S(1)} %get-tuple-element.77.west), channel_id=1, source_target_pairs={{0,248},{8,0},{16,8},{24,16},{32,24},{40,32},{48,40},{56,48},{64,5... | collective-permute-start | bytes 115208 | tf_op jit(solution)/shard_map/ppermute | solution.py:488
  52.7 3.8 %collective-permute-start.12 = (bf16[16,6,72,128]{3,2,1,0:T(8,128)(2,1)S(1)}, bf16[16,6,72,128]{3,2,1,0:T(8,128)(2,1)S(1)}, u32[]{:S(2)}, u32[]{:S(2)}) collective-permute-start(bf16[16,6,72,128]{3,2,1,0:T(8,128)(2,1)S(1)} %get-tuple-element.96), channel_id=1, source_target_pairs={{0,8},{8,0},{1,9},{9,1},{2,10},{10,2},{3,11},{11,3},{4,12},{12,4},... | collective-permute-start | bytes 5308424 | tf_op jit(solution)/shard_map/ppermute | solution.py:499
  53.5 4.9 %collective-permute-start.10 = (bf16[14,3,400]{2,1,0:T(4,128)(2,1)S(1)}, bf16[14,3,400]{2,1,0:T(4,128)(2,1)S(1)}, u32[]{:S(2)}, u32[]{:S(2)}) collective-permute-start(bf16[14,3,400]{2,1,0:T(4,128)(2,1)S(1)} %get-tuple-element.88), channel_id=1, source_target_pairs={{0,1},{1,2},{2,3},{3,4},{4,5},{5,6},{6,7},{7,0},{8,9},{9,10},{10,1... | collective-permute-start | bytes 100808 | tf_op jit(solution)/shard_map/ppermute | solution.py:488
  53.6 6.5 %collective-permute-start.11 = (bf16[14,3,400]{2,1,0:T(4,128)(2,1)S(1)}, bf16[14,3,400]{2,1,0:T(4,128)(2,1)S(1)}, u32[]{:S(2)}, u32[]{:S(2)}) collective-permute-start(bf16[14,3,400]{2,1,0:T(4,128)(2,1)S(1)} %get-tuple-element.89), channel_id=1, source_target_pairs={{0,7},{1,0},{2,1},{3,2},{4,3},{5,4},{6,5},{7,6},{8,15},{9,8},{10,9... | collective-permute-start | bytes 100808 | tf_op jit(solution)/shard_map/ppermute | solution.py:488
  56.9 12.5 %collective-permute-start.13 = (bf16[4,6,72,128]{3,2,1,0:T(8,128)(2,1)S(1)}, bf16[4,6,72,128]{3,2,1,0:T(8,128)(2,1)S(1)}, u32[]{:S(2)}, u32[]{:S(2)}) collective-permute-start(bf16[4,6,72,128]{3,2,1,0:T(8,128)(2,1)S(1)} %get-tuple-element.97), channel_id=1, source_target_pairs={{0,1},{1,2},{2,3},{3,0},{4,5},{5,6},{6,7},{7,4},{8,9},{9,10},{10,1... | collective-permute-start | bytes 1327112 | tf_op jit(solution)/shard_map/ppermute | solution.py:488
  69.4 3.4 %collective-permute-start.14 = (bf16[16,3,72,128]{3,2,1,0:T(8,128)(2,1)S(1)}, bf16[16,3,72,128]{3,2,1,0:T(8,128)(2,1)S(1)}, u32[]{:S(2)}, u32[]{:S(2)}) collective-permute-start(bf16[16,3,72,128]{3,2,1,0:T(8,128)(2,1)S(1)} %get-tuple-element.98), channel_id=1, source_target_pairs={{0,8},{8,0},{1,9},{9,1},{2,10},{10,2},{3,11},{11,3},{4,12},{12,4},... | collective-permute-start | bytes 2654216 | tf_op jit(solution)/shard_map/ppermute | solution.py:499
  69.4 14.5 %collective-permute-start.16 = (bf16[4,6,72,128]{3,2,1,0:T(8,128)(2,1)S(1)}, bf16[4,6,72,128]{3,2,1,0:T(8,128)(2,1)S(1)}, u32[]{:S(2)}, u32[]{:S(2)}) collective-permute-start(bf16[4,6,72,128]{3,2,1,0:T(8,128)(2,1)S(1)} %get-tuple-element.103), channel_id=1, source_target_pairs={{0,2},{1,3},{2,0},{3,1},{4,6},{5,7},{6,4},{7,5},{8,10},{9,11},{10,... | collective-permute-start | bytes 1327112 | tf_op jit(solution)/shard_map/ppermute | solution.py:488
  70.4 22.5 %collective-permute-start.17 = (bf16[4,6,72,128]{3,2,1,0:T(8,128)(2,1)S(1)}, bf16[4,6,72,128]{3,2,1,0:T(8,128)(2,1)S(1)}, u32[]{:S(2)}, u32[]{:S(2)}) collective-permute-start(bf16[4,6,72,128]{3,2,1,0:T(8,128)(2,1)S(1)} %get-tuple-element.104), channel_id=1, source_target_pairs={{0,3},{1,0},{2,1},{3,2},{4,7},{5,4},{6,5},{7,6},{8,11},{9,8},{10,9... | collective-permute-start | bytes 1327112 | tf_op jit(solution)/shard_map/ppermute | solution.py:488
  73.0 21.4 %collective-permute-start.15 = (bf16[4,3,72,128]{3,2,1,0:T(8,128)(2,1)S(1)}, bf16[4,3,72,128]{3,2,1,0:T(8,128)(2,1)S(1)}, u32[]{:S(2)}, u32[]{:S(2)}) collective-permute-start(bf16[4,3,72,128]{3,2,1,0:T(8,128)(2,1)S(1)} %get-tuple-element.100), channel_id=1, source_target_pairs={{0,4},{4,0},{16,20},{20,16},{1,5},{5,1},{17,21},{21,17},{2,6},{6,2... | collective-permute-start | bytes 663560 | tf_op jit(solution)/shard_map/ppermute | solution.py:548
  73.8 24.2 %collective-permute-start.18 = (bf16[4,3,72,128]{3,2,1,0:T(8,128)(2,1)S(1)}, bf16[4,3,72,128]{3,2,1,0:T(8,128)(2,1)S(1)}, u32[]{:S(2)}, u32[]{:S(2)}) collective-permute-start(bf16[4,3,72,128]{3,2,1,0:T(8,128)(2,1)S(1)} %get-tuple-element.107), channel_id=1, source_target_pairs={{0,16},{4,20},{16,0},{20,4},{1,17},{5,21},{17,1},{21,5},{2,18},{6,... | collective-permute-start | bytes 663560 | tf_op jit(solution)/shard_map/ppermute | solution.py:548
  73.8 24.2 %collective-permute-start.19 = (bf16[4,3,72,128]{3,2,1,0:T(8,128)(2,1)S(1)}, bf16[4,3,72,128]{3,2,1,0:T(8,128)(2,1)S(1)}, u32[]{:S(2)}, u32[]{:S(2)}) collective-permute-start(bf16[4,3,72,128]{3,2,1,0:T(8,128)(2,1)S(1)} %get-tuple-element.108), channel_id=1, source_target_pairs={{0,20},{4,16},{16,4},{20,0},{1,21},{5,17},{17,5},{21,1},{2,22},{6,... | collective-permute-start | bytes 663560 | tf_op jit(solution)/shard_map/ppermute | solution.py:548
  93.2 6.7 %collective-permute-start.23 = (bf16[6,72,128]{2,1,0:T(8,128)(2,1)S(1)}, bf16[6,72,128]{2,1,0:T(8,128)(2,1)S(1)}, u32[]{:S(2)}, u32[]{:S(2)}) collective-permute-start(bf16[6,72,128]{2,1,0:T(8,128)(2,1)S(1)} %get-tuple-element.105), channel_id=1, source_target_pairs={{0,4},{4,0},{16,20},{20,16},{1,5},{5,1},{17,21},{21,17},{2,6},{6,2... | collective-permute-start | bytes 331784 | tf_op jit(solution)/shard_map/ppermute | solution.py:548
  94.4 6.3 %collective-permute-start.24 = (bf16[6,72,128]{2,1,0:T(8,128)(2,1)S(1)}, bf16[6,72,128]{2,1,0:T(8,128)(2,1)S(1)}, u32[]{:S(2)}, u32[]{:S(2)}) collective-permute-start(bf16[6,72,128]{2,1,0:T(8,128)(2,1)S(1)} %get-tuple-element.114), channel_id=1, source_target_pairs={{0,16},{4,20},{16,0},{20,4},{1,17},{5,21},{17,1},{21,5},{2,18},{6,... | collective-permute-start | bytes 331784 | tf_op jit(solution)/shard_map/ppermute | solution.py:548
  94.4 8.4 %collective-permute-start.25 = (bf16[6,72,128]{2,1,0:T(8,128)(2,1)S(1)}, bf16[6,72,128]{2,1,0:T(8,128)(2,1)S(1)}, u32[]{:S(2)}, u32[]{:S(2)}) collective-permute-start(bf16[6,72,128]{2,1,0:T(8,128)(2,1)S(1)} %get-tuple-element.115), channel_id=1, source_target_pairs={{0,20},{4,16},{16,4},{20,0},{1,21},{5,17},{17,5},{21,1},{2,22},{6,... | collective-permute-start | bytes 331784 | tf_op jit(solution)/shard_map/ppermute | solution.py:548
  98.1 4.7 %collective-permute-start.20 = (bf16[3,72,128]{2,1,0:T(8,128)(2,1)S(1)}, bf16[3,72,128]{2,1,0:T(8,128)(2,1)S(1)}, u32[]{:S(2)}, u32[]{:S(2)}) collective-permute-start(bf16[3,72,128]{2,1,0:T(8,128)(2,1)S(1)} %get-tuple-element.110), channel_id=1, source_target_pairs={{0,1},{1,2},{2,3},{3,0},{4,5},{5,6},{6,7},{7,4},{8,9},{9,10},{10,1... | collective-permute-start | bytes 165896 | tf_op jit(solution)/shard_map/ppermute | solution.py:488
  98.8 6.0 %collective-permute-start.21 = (bf16[3,72,128]{2,1,0:T(8,128)(2,1)S(1)}, bf16[3,72,128]{2,1,0:T(8,128)(2,1)S(1)}, u32[]{:S(2)}, u32[]{:S(2)}) collective-permute-start(bf16[3,72,128]{2,1,0:T(8,128)(2,1)S(1)} %get-tuple-element.111), channel_id=1, source_target_pairs={{0,2},{1,3},{2,0},{3,1},{4,6},{5,7},{6,4},{7,5},{8,10},{9,11},{10,... | collective-permute-start | bytes 165896 | tf_op jit(solution)/shard_map/ppermute | solution.py:488
  99.8 5.5 %collective-permute-start.22 = (bf16[3,72,128]{2,1,0:T(8,128)(2,1)S(1)}, bf16[3,72,128]{2,1,0:T(8,128)(2,1)S(1)}, u32[]{:S(2)}, u32[]{:S(2)}) collective-permute-start(bf16[3,72,128]{2,1,0:T(8,128)(2,1)S(1)} %get-tuple-element.112), channel_id=1, source_target_pairs={{0,3},{1,0},{2,1},{3,2},{4,7},{5,4},{6,5},{7,6},{8,11},{9,8},{10,9... | collective-permute-start | bytes 165896 | tf_op jit(solution)/shard_map/ppermute | solution.py:488
  106.1 16.1 %all-to-all-start = ((bf16[8,72,128]{2,1,0:T(8,128)(2,1)}), bf16[8,72,128]{2,1,0:T(8,128)(2,1)S(1)}, u32[]{:S(2)}, u32[]{:S(2)}) async-start(bf16[8,72,128]{2,1,0:T(8,128)(2,1)} %shard_map.154), calls=%async_computation | async-start | bytes 294912 | tf_op jit(solution)/shard_map/all_to_all | solution.py:664
